TPU v7x, 256 devices: a whole 4x4x8 slice. The times are simulated.
256 devices in a mesh: rep: 16 (over y_lo, z), fsdp: 16 (over y_hi, x, core).
Axes of the slice: x: 4, y: 4 (y_hi: 2, y_lo: 2; y = y_hi * 2 + y_lo), z: 8, core: 2. Of those that a mesh axis runs over, the one named last changes fastest.
Arguments:
- outer_weights: bfloat16 [8192, 1024], P('fsdp'), may hold values from -4 to 4
- inner_weights: bfloat16 [16, 8192, 1024], P('rep', 'fsdp'), may hold values from -10 to 10
- momentum: float32 [8192, 1024], P('fsdp'), may hold values from -1.2 to 1.2
- tokens: bfloat16 [16, 8192, 8192], P('rep', 'fsdp'), may hold values from -6 to 6
Outputs:
- outer_next: bfloat16 [8192, 1024], P('fsdp')
- momentum_next: float32 [8192, 1024], P('fsdp')
- keys: bfloat16 [16, 8192, 1024], P('rep', 'fsdp')
All inputs are finite; a program needn't handle non-finite values. Where the computation divides by a largest or mean magnitude, that divisor is 1e-20 or more.
Results may differ from a plain program's by a relative error of at most 0.015.
Values may be sent and summed in bfloat16 or wider, within the bound.
No kernel may reach another device: no remote copies, remote signals or barrier semaphores. Data moves between devices by JAX's collectives and lax.ppermute only.
A program may use at most 128 MiB of HBM per device.

v0:
```python
import jax
import jax.numpy as jnp
from jax import lax
from jax.sharding import PartitionSpec as P


def dequantized(outer_weights, inner_one):
    delta = outer_weights.astype(jnp.float32) - inner_one.astype(jnp.float32)
    rows = delta.shape[0]
    blocks = delta.reshape(rows, delta.shape[1] // 128, 128)
    scale = jnp.max(jnp.abs(blocks), axis=2, keepdims=True) + 1e-06
    quant = (blocks / scale).astype(jnp.bfloat16)
    quant = lax.optimization_barrier(quant)
    return (quant.astype(jnp.float32) * scale).reshape(rows, delta.shape[1])


def outer_update(outer_rows, momentum_rows, average):
    momentum_next = 0.9 * momentum_rows + average
    outer_next = (outer_rows.astype(jnp.float32) - 0.7 * (average + 0.9 * momentum_next)).astype(
        jnp.bfloat16
    )
    return (outer_next, momentum_next)


def shards(outer_weights, inner_weights, momentum, tokens):
    inner_one = inner_weights[0]
    replicas = lax.axis_size("rep")
    term = dequantized(outer_weights, inner_one)
    total = lax.psum(term, "rep")
    outer_next, momentum_next = outer_update(outer_weights, momentum, total / replicas)
    mixed = (0.5 * inner_one.astype(jnp.float32) + 0.5 * outer_next.astype(jnp.float32)).astype(
        jnp.bfloat16
    )
    token_rows = tokens[0]
    width = token_rows.shape[1]
    summed = jnp.dot(
        token_rows,
        lax.all_gather(mixed, "fsdp", axis=0, tiled=True),
        preferred_element_type=jnp.float32,
    )
    keys = (summed * width ** (-0.5)).astype(jnp.bfloat16)
    return (outer_next, momentum_next, keys[None])


def solution(mesh):
    placed = (P("fsdp", None), P("rep", "fsdp", None), P("fsdp", None), P("rep", "fsdp", None))
    return jax.shard_map(
        shards,
        mesh=mesh,
        in_specs=placed,
        out_specs=(P("fsdp", None), P("fsdp", None), P("rep", "fsdp", None)),
        check_vma=False,
    )
```

profile of v0, /device:TPU:1, one launch (start us, length us, event | category | flops | bytes accessed | tf_op | source)
XLA Modules:
  0.0 301.0 jit_solution(13125674515295840068)
XLA Ops:
  7.2 0.0 all-reduce.2.cloned.1.call-start
  7.2 1.9 fusion.3
  9.1 0.5 copy.8
  9.6 0.6 abs_reduce_fusion
  10.3 0.9 divide_convert_fusion
  11.2 0.6 convert_multiply_fusion
  11.8 1.8 copy.11
  13.5 0.0 copy-start
  13.5 0.0 copy-start.1
  13.6 0.0 all-reduce.2.cloned.1.call-update
  13.6 0.0 all-gather.2.cloned.1.call-start
  13.6 136.3 %all-reduce.2.cloned.1.call-done = f32[512,1024]{1,0:T(8,128)} async-done(((f32[512,1024]{1,0:T(8,128)}), f32[512,1024]{1,0:T(8,128)}) %all-reduce.2.cloned.1.call-update) | async-done | bytes 2097168 | tf_op jit(solution)/shard_map/psum | solution.py:29
  149.9 0.0 copy-done
  149.9 0.0 copy-done.1
  149.9 5.1 %fusion.5 = (bf16[512,1024]{1,0:T(8,128)(2,1)}, bf16[512,1024]{1,0:T(8,128)(2,1)}, f32[512,1024]{1,0:T(8,128)}) fusion(bf16[1,512,1024]{2,1,0:T(8,128)(2,1)S(1)} %copy-done, f32[512,1024]{1,0:T(8,128)} %all-reduce.2.cloned.1.call-done, bf16[512,1024]{1,0:T(8,128)(2,1)S(1)} %copy-done.1, f32[512,1024]{1,0:T(8,128)} %param.6), kind=kLoop, calls=%fused_computation.8 | loop fusion | flops 7340032 | bytes 10485760 | tf_op jit(solution)/shard_map/convert_element_type | solution.py:31
  155.0 0.0 all-gather.2.cloned.1.call-update
  155.0 122.9 %all-gather.2.cloned.1.call-done = bf16[8192,1024]{1,0:T(8,128)(2,1)} async-done(((bf16[512,1024]{1,0:T(8,128)(2,1)}), bf16[8192,1024]{1,0:T(8,128)(2,1)}) %all-gather.2.cloned.1.call-update) | async-done | bytes 16777232 | tf_op jit(solution)/shard_map/all_gather | solution.py:38
  277.9 14.9 %fusion.8 = bf16[1,512,1024]{1,2,0:T(8,128)(2,1)S(1)} fusion(bf16[8192,1024]{1,0:T(8,128)(2,1)} %all-gather.2.cloned.1.call-done, bf16[1,512,8192]{2,1,0:T(8,128)(2,1)} %param.7), kind=kOutput, calls=%fused_computation.15 | convolution fusion | flops 8590983168 | bytes 26214400 | tf_op jit(solution)/shard_map/dot_general | solution.py:36
  292.8 1.3 copy.7
  (1 shorter events, 0.0 us)
Async XLA Ops:
  7.2 142.7 %all-reduce.2.cloned.1.call-start = ((), (), s32[]{:S(2)}) async-start(), calls=%async_computation | async-start | bytes 4194304 | tf_op jit(solution)/shard_map/psum | solution.py:29
  13.5 136.4 %copy-start = (bf16[1,512,1024]{2,1,0:T(8,128)(2,1)S(1)}, bf16[1,512,1024]{2,1,0:T(8,128)(2,1)}, u32[]{:S(2)}) copy-start(bf16[1,512,1024]{2,1,0:T(8,128)(2,1)} %param.5) | copy-start | bytes 3145732
  13.5 136.4 %copy-start.1 = (bf16[512,1024]{1,0:T(8,128)(2,1)S(1)}, bf16[512,1024]{1,0:T(8,128)(2,1)}, u32[]{:S(2)}) copy-start(bf16[512,1024]{1,0:T(8,128)(2,1)} %param.4) | copy-start | bytes 3145732
  13.6 264.3 %all-gather.2.cloned.1.call-start = ((), (), s32[]{:S(2)}) async-start(), calls=%async_computation.1 | async-start | bytes 17825792 | tf_op jit(solution)/shard_map/all_gather | solution.py:38
Sparse Core Ops, SparseCore 0:
  13.7 136.1 all-reduce.1
  155.2 122.7 all-gather.1
where the time goes:
time: 301 us
  waiting for transfers between devices  259 us (86%)
  matrix products  14.9 us (5%)
  between operations  14.1 us (5%)
  other arithmetic  9.14 us (3%)
  local copies, waits for them, and re-layouts  3.57 us (1%)
    psum x1, waiting for transfers between devices, shards(): total = lax.psum(term, 'rep')  136 us
    all_gather x1, waiting for transfers between devices, shards(): lax.all_gather(mixed, 'fsdp', axis=0, tiled=True)  123 us
    dot_general x1, matrix products, shards(): jnp.dot(token_rows, lax.all_gather(mixed, 'fsdp', axis=0, tiled=True), pr...  14.9 us
  transfers between devices with their start and end apart: 2, of which 2 were waited for; matrix products, arithmetic and copies ran while one was open for 0% of the time, Pallas kernels for 0%

commit v1 on v0

v1 whole, which is shorter than its diff:
```python
import jax
import jax.numpy as jnp
from jax import lax
from jax.experimental import pallas as pl
from jax.experimental.pallas import tpu as pltpu
from jax.sharding import PartitionSpec as P

YH, X, CORE = 2, 4, 2
CHIPS = YH * X
REP = 16
MAIN, EARLY_WIDE = 768, 256
NEAR = ((0, 0), (0, -1), (0, 1), (1, 0))
SIDES = ((1, -1), (1, 1))
LAST = ((0, 2), (1, 2))
ORDER = tuple((dy, dx) for dx in (0, -1, 1, 2) for dy in range(YH))
MIB = 1 << 20
F32, BF16 = jnp.float32, jnp.bfloat16
YL, Z = 2, 8
SAME_YL = [[yl * Z + z for z in range(Z)] for yl in range(YL)]


def fsdp_move(array, dy=0, dx=0, dc=0):
    perm = []
    for y in range(YH):
        for x in range(X):
            for c in range(CORE):
                to = (((y + dy) % YH) * X + (x + dx) % X) * CORE + (c + dc) % CORE
                perm.append(((y * X + x) * CORE + c, to))
    return lax.ppermute(array, "fsdp", perm)


def swap_yl(array):
    return lax.ppermute(array, "rep", [(r, (r + Z) % REP) for r in range(REP)])


def to_all_replicas(array):
    return lax.all_to_all(jnp.broadcast_to(array[None], (REP, *array.shape)), "rep", 0, 0)


def to_all_z(array):
    return lax.all_to_all(
        jnp.broadcast_to(array[None], (Z, *array.shape)), "rep", 0, 0, axis_index_groups=SAME_YL
    )


def after(array, *others):
    def kernel(*refs):
        pass

    space = pl.BlockSpec(memory_space=pl.ANY)
    return pl.pallas_call(
        kernel,
        in_specs=[space] * (1 + len(others)),
        out_specs=space,
        out_shape=jax.ShapeDtypeStruct(array.shape, array.dtype),
        input_output_aliases={0: 0},
        name="after",
    )(array, *others)


def update(outer, moment, average):
    momentum_next = 0.9 * moment + average
    return (outer.astype(F32) - 0.7 * (average + 0.9 * momentum_next)).astype(BF16), momentum_next


def average_slice(recv, outer_rows, momentum_rows):
    replicas, rows, columns = recv.shape

    def kernel(recv_ref, outer_ref, momentum_ref, copies_ref, early_ref, mean_ref):
        for first in range(0, columns, 128):
            cols = slice(first, first + 128)
            outer = outer_ref[:, cols].astype(F32)
            total = jnp.zeros((rows, 128), F32)
            for r in range(replicas):
                delta = outer - recv_ref[r, :, cols].astype(F32)
                scale = jnp.max(jnp.abs(delta), axis=1, keepdims=True) + 1e-6
                quant = (delta / scale).astype(BF16)
                total = total + quant.astype(F32) * scale
            mean = total / replicas
            if first < MAIN:
                for r in range(replicas):
                    copies_ref[r, :, cols] = mean.astype(BF16)
            else:
                cols = slice(first - MAIN, first - MAIN + 128)
                mean_ref[:, cols] = mean.astype(BF16)
                early_ref[:, cols] = update(outer, momentum_ref[:, cols], mean)[0]

    return pl.pallas_call(
        kernel,
        out_shape=[
            jax.ShapeDtypeStruct((replicas, rows, MAIN), BF16),
            jax.ShapeDtypeStruct((rows, columns - MAIN), BF16),
            jax.ShapeDtypeStruct((rows, columns - MAIN), BF16),
        ],
        cost_estimate=pl.CostEstimate(
            flops=10 * replicas * rows * columns, bytes_accessed=4 * replicas * rows * columns, transcendentals=0
        ),
        name="average_slice",
    )(recv, outer_rows, momentum_rows)


def mix(one, other):
    return (0.5 * one.astype(F32) + 0.5 * other.astype(F32)).astype(BF16)


def mix_early(inners, late, yl):
    count, (rows, wide) = len(inners), inners[0].shape
    half = rows // YL

    def kernel(yl_ref, *refs):
        mixed_ref, outer_ref, average_ref = refs[-3:]
        lates = refs[count:-3]
        for h in range(YL):
            at = slice(h * half, h * half + half)
            outers = [r[...].reshape(half, wide) for r in lates[h * (count + 1) : (h + 1) * (count + 1)]]
            for k in range(count):
                mixed_ref[k, at] = mix(refs[k][at], outers[k])
            outer_ref[at] = outers[0]
            average_ref[at] = outers[count]

    def late_spec(h, k):
        return pl.BlockSpec((Z, None, None, rows // REP, wide), lambda i, yl: (0, (yl[0] + h) % YL, k, 0, 0))

    def whole(*shape):
        return pl.BlockSpec(shape, lambda i, yl: (0,) * len(shape))

    lates = [late_spec(h, k) for h in range(YL) for k in range(count + 1)]
    return pl.pallas_call(
        kernel,
        grid_spec=pltpu.PrefetchScalarGridSpec(
            num_scalar_prefetch=1,
            grid=(1,),
            in_specs=[whole(rows, wide)] * count + lates,
            out_specs=[whole(count, rows, wide), whole(rows, wide), whole(rows, wide)],
        ),
        out_shape=[
            jax.ShapeDtypeStruct((count, rows, wide), BF16),
            jax.ShapeDtypeStruct((rows, wide), BF16),
            jax.ShapeDtypeStruct((rows, wide), BF16),
        ],
        compiler_params=pltpu.CompilerParams(vmem_limit_bytes=48 * MIB),
        cost_estimate=pl.CostEstimate(
            flops=3 * count * rows * wide, bytes_accessed=6 * count * rows * wide, transcendentals=0
        ),
        name="mix_early",
    )(yl[None], *inners, *([late] * len(lates)))


def blocks_dot(lefts, blocks, pieces, start=None):
    rows, tile = lefts[0].shape[0], 256
    steps = rows // tile
    count, sides = len(pieces), len(lefts)
    arrays = []
    for piece in pieces:
        if not any(piece[0] is a for a in arrays):
            arrays.append(piece[0])
    found = [next(i for i, a in enumerate(arrays) if a is piece[0]) for piece in pieces]
    deep, width = arrays[0].shape[-2:]
    added = list(start) if start else []

    def kernel(at_ref, *refs):
        rights = refs[sides * count : sides * count + len(arrays)]
        starts = refs[sides * count + len(arrays) : -sides]
        step = pl.program_id(0)
        for side in range(sides):

            @pl.when(step // steps == side)
            def _(side=side):
                total = starts[side][...] if starts else jnp.zeros((tile, width), F32)
                for k, piece in enumerate(pieces):
                    right = rights[found[k]]
                    right = right[piece[1]] if len(piece) > 1 else right[...]
                    total = total + jnp.dot(refs[side * count + k][...], right, preferred_element_type=F32)
                refs[side - sides][...] = total

    def row(side, i):
        return jnp.clip(i - side * steps, 0, steps - 1)

    def left_spec(side, k):
        return pl.BlockSpec((tile, deep), lambda i, at: (row(side, i), at[k]))

    def row_spec(side):
        return pl.BlockSpec((tile, width), lambda i, at: (row(side, i), 0))

    def whole(array):
        return pl.BlockSpec(array.shape, lambda i, at: (0,) * array.ndim)

    return list(
        pl.pallas_call(
            kernel,
            grid_spec=pltpu.PrefetchScalarGridSpec(
                num_scalar_prefetch=1,
                grid=(sides * steps,),
                in_specs=[left_spec(side, k) for side in range(sides) for k in range(count)]
                + [whole(a) for a in arrays]
                + [row_spec(side) for side in range(len(added))],
                out_specs=[row_spec(side) for side in range(sides)],
            ),
            out_shape=[jax.ShapeDtypeStruct((rows, width), F32)] * sides,
            compiler_params=pltpu.CompilerParams(vmem_limit_bytes=48 * MIB),
            cost_estimate=pl.CostEstimate(
                flops=2 * sides * rows * deep * count * width,
                bytes_accessed=2 * deep * count * (sides * rows + width) + 4 * sides * rows * width,
                transcendentals=0,
            ),
            name="blocks_dot",
        )(blocks, *[left for left in lefts for _ in range(count)], *arrays, *added)
    )


def shards(outer_weights, inner_weights, momentum, tokens):
    inner = inner_weights[0]
    token_rows = tokens[0]
    rows, columns = inner.shape
    part = rows // REP
    rep = lax.axis_index("rep")
    core = lax.axis_index("fsdp") % CORE
    chip = lax.axis_index("fsdp") // CORE
    y, x = chip // X, chip % X
    width = token_rows.shape[1]

    def chips_of(moves):
        return jnp.stack([((y + dy) % YH) * X + (x + dx) % X for dy, dx in moves]).astype(jnp.int32)

    early = slice(MAIN, MAIN + EARLY_WIDE)
    yl = (rep // Z).astype(jnp.int32)

    recv = lax.all_to_all(inner.reshape(REP, part, columns), "rep", 0, 0)
    their_tokens = fsdp_move(token_rows, dc=1)
    mine = inner[:, early]
    there, left, right, across = (fsdp_move(mine, *to) for to in ((1, 0), (0, 1), (0, -1), (0, 2)))
    outer_part = lax.dynamic_slice(outer_weights, (rep * part, 0), (part, columns))
    outer_part = after(outer_part, their_tokens, there, left, right, across)
    momentum_part = lax.dynamic_slice(momentum, (rep * part, MAIN), (part, EARLY_WIDE))
    copies, outer_slice, mean = average_slice(recv, outer_part, momentum_part)
    average = lax.all_to_all(copies, "rep", 0, 0).reshape(rows, MAIN)

    there_left, there_right, there_across = (fsdp_move(there, 0, dx) for dx in (1, -1, 2))
    inners = [mine, there, left, there_left, right, there_right, across, there_across]
    pair = jnp.stack([outer_slice, fsdp_move(outer_slice, dy=1)])
    slices = jnp.concatenate(
        [pair, fsdp_move(pair, dx=1), fsdp_move(pair, dx=-1), fsdp_move(pair, dx=2), mean[None]]
    )
    slices = jnp.stack([slices, swap_yl(slices)])
    average = after(average, there_left, there_right, there_across)
    mixed = mix(
        inner[:, :MAIN], update(outer_weights[:, :MAIN], momentum[:, :MAIN], average.astype(F32))[0]
    )
    late = to_all_z(after(slices, mixed))

    both = [their_tokens, token_rows]

    def dot(chips, pieces, start=None, lefts=both):
        return blocks_dot(lefts, CORE * chips_of(chips) + core, pieces, start)

    left, right, there = fsdp_move(mixed, dx=1), fsdp_move(mixed, dx=-1), fsdp_move(mixed, dy=1)
    there_left, there_right, across = fsdp_move(there, dx=1), fsdp_move(there, dx=-1), fsdp_move(left, dx=1)
    sums = dot(NEAR, [(mixed,), (left,), (right,), (there,)])
    there_right = after(there_right, sums[0])
    there_across = fsdp_move(there_right, dx=-1)
    sums = dot(SIDES, [(there_left,), (there_right,)], sums)

    mixed_early, outer_early, average_early = mix_early(inners, after(late, sums[0]), yl)
    sums_early = dot(ORDER, [(mixed_early, k) for k in range(CHIPS)])
    theirs_early = fsdp_move(sums_early[0], dc=1)
    outer_main, momentum_main = update(
        outer_weights[:, :MAIN], momentum[:, :MAIN], after(average, there_right).astype(F32)
    )
    momentum_early = 0.9 * momentum[:, early] + average_early.astype(F32)
    outer_next = jnp.concatenate([outer_main, outer_early], axis=1)
    momentum_next = jnp.concatenate([momentum_main, momentum_early], axis=1)

    last = [(across,), (there_across,)]
    theirs = fsdp_move(dot(LAST, last, sums[:1], both[:1])[0], dc=1)
    ours = dot(LAST, last, sums[1:], both[1:])[0]
    keys = jnp.concatenate([ours + theirs, sums_early[1] + theirs_early], axis=1) * width ** (-0.5)
    return outer_next, momentum_next, keys.astype(BF16)[None]


def solution(mesh):
    placed = (P("fsdp", None), P("rep", "fsdp", None), P("fsdp", None), P("rep", "fsdp", None))
    return jax.shard_map(
        shards,
        mesh=mesh,
        in_specs=placed,
        out_specs=(P("fsdp", None), P("fsdp", None), P("rep", "fsdp", None)),
        check_vma=False,
    )
```

time: 301 us -> 171 us (0.57)
  waiting for transfers between devices: 259 us -> 49.7 us
  starting transfers between devices: 0.08 us -> 57.1 us
  Pallas kernels: 0 us -> 32.8 us
  matrix products: 14.9 us -> 0 us
  between operations: 14.1 us -> 0.95 us
  local copies, waits for them, and re-layouts: 3.57 us -> 14 us
  other arithmetic: 9.14 us -> 16 us
    psum x1 -> x0, waiting for transfers between devices: 136 us -> none  [shards(): total = lax.psum(term, 'rep')]
    all_gather x1 -> x0, waiting for transfers between devices: 123 us -> none  [shards(): lax.all_gather(mixed, 'fsdp', axis=0, tiled=True)]
    ppermute x0 -> x22, waiting for transfers between devices: none -> 42.6 us  [the longest x21 42.6 us: fsdp_move(): return lax.ppermute(array, 'fsdp', perm)]
    ppermute x0 -> x22, starting transfers between devices: none -> 37 us  [the longest x21 35.8 us: fsdp_move(): return lax.ppermute(array, 'fsdp', perm)]
    pallas_call x0 -> x13, Pallas kernels: none -> 32.8 us  [the longest x5 27.5 us: blocks_dot(): pl.pallas_call(kernel, grid_spec=pltpu.PrefetchScalarGridSpec(num_scalar_...]
    all_to_all x0 -> x3, starting transfers between devices: none -> 20.1 us  [the longest x1 7.62 us: shards(): recv = lax.all_to_all(inner.reshape(REP, part, columns), 'rep', 0, 0)]
    dot_general x1 -> x0, matrix products: 14.9 us -> none  [shards(): jnp.dot(token_rows, lax.all_gather(mixed, 'fsdp', axis=0, tiled=True), pr...]
    all_to_all x0 -> x3, waiting for transfers between devices: none -> 7.04 us  [the longest x1 7.03 us: shards(): recv = lax.all_to_all(inner.reshape(REP, part, columns), 'rep', 0, 0)]
  transfers between devices with their start and end apart: 2 -> 25, of which waited for: 2 -> 12; matrix products, arithmetic and copies ran while one was open for 0% -> 12% of each run, Pallas kernels for 0% -> 12%
where the time goes in v1:
time: 171 us; the launch traced here: 170 us
  starting transfers between devices  57.1 us (33%)
  waiting for transfers between devices  49.7 us (29%)
  Pallas kernels  32.8 us (19%)
  other arithmetic  16 us (9%)
  local copies, waits for them, and re-layouts  14 us (8%)
    ppermute x21, waiting for transfers between devices, fsdp_move(): return lax.ppermute(array, 'fsdp', perm)  42.6 us
    ppermute x21, starting transfers between devices, fsdp_move(): return lax.ppermute(array, 'fsdp', perm)  35.8 us
    pallas_call x5, Pallas kernels, blocks_dot(): pl.pallas_call(kernel, grid_spec=pltpu.PrefetchScalarGridSpec(num_scalar_...  27.5 us
    unnamed x63, local copies, waits for them, and re-layouts  8.41 us
    all_to_all x1, starting transfers between devices, shards(): recv = lax.all_to_all(inner.reshape(REP, part, columns), 'rep', 0, 0)  7.62 us
    all_to_all x1, waiting for transfers between devices, shards(): recv = lax.all_to_all(inner.reshape(REP, part, columns), 'rep', 0, 0)  7.03 us
    all_to_all x1, starting transfers between devices, shards(): average = lax.all_to_all(copies, 'rep', 0, 0).reshape(rows, MAIN)  6.44 us
    all_to_all x1, starting transfers between devices, to_all_z(): lax.all_to_all(jnp.broadcast_to(array[None], (Z, *array.shape)), 'rep', 0...  6.07 us
  transfers between devices with their start and end apart: 25, of which 12 were waited for; matrix products, arithmetic and copies ran while one was open for 12% of the time, Pallas kernels for 12%

profile of v1, /device:TPU:1, one launch (start us, length us, event | category | flops | bytes accessed | tf_op | source)
XLA Modules:
  0.0 170.5 jit_solution(10812108843967440021)
XLA Ops:
  0.6 3.3 %collective-permute-start = (bf16[512,8192]{1,0:T(8,128)(2,1)}, bf16[512,8192]{1,0:T(8,128)(2,1)}, u32[]{:S(2)}, u32[]{:S(2)}) collective-permute-start(bf16[512,8192]{1,0:T(8,128)(2,1)} %bitcast.25), channel_id=1, source_target_pairs={{0,1},{1,0},{2,3},{3,2},{4,5},{5,4},{6,7},{7,6},{8,9},{9,8},{10,11... | collective-permute-start | bytes 25165832 | tf_op jit(solution)/shard_map/ppermute | solution.py:29
  4.0 7.6 %all-to-all-start = ((bf16[16,32,1024]{2,1,0:T(8,128)(2,1)}), bf16[16,32,1024]{2,1,0:T(8,128)(2,1)}, u32[]{:S(2)}, u32[]{:S(2)}) async-start(bf16[16,32,1024]{2,1,0:T(8,128)(2,1)} %bitcast.43), calls=%async_computation | async-start | bytes 2097152 | tf_op jit(solution)/shard_map/all_to_all | solution.py:228
  11.6 2.8 %collective-permute-start.4 = (bf16[512,256]{1,0:T(8,128)(2,1)S(1)}, bf16[512,256]{1,0:T(8,128)(2,1)S(1)}, u32[]{:S(2)}, u32[]{:S(2)}) collective-permute-start(bf16[512,256]{1,0:T(8,128)(2,1)S(1)} %slice.22.refs_0_), channel_id=1, source_target_pairs={{0,4},{1,5},{2,6},{3,7},{4,0},{5,1},{6,2},{7,3},{8,12},{9,13},{10,... | collective-permute-start | bytes 786440 | tf_op jit(solution)/shard_map/ppermute | solution.py:29
  14.5 0.9 collective-permute-start.3
  15.3 0.6 collective-permute-start.2
  15.9 2.6 %collective-permute-start.1 = (bf16[512,256]{1,0:T(8,128)(2,1)S(1)}, bf16[512,256]{1,0:T(8,128)(2,1)S(1)}, u32[]{:S(2)}, u32[]{:S(2)}) collective-permute-start(bf16[512,256]{1,0:T(8,128)(2,1)S(1)} %slice.22.refs_0_), channel_id=1, source_target_pairs={{0,8},{1,9},{2,10},{3,11},{4,12},{5,13},{6,14},{7,15},{8,0},{9,1},... | collective-permute-start | bytes 786440 | tf_op jit(solution)/shard_map/ppermute | solution.py:29
  18.6 0.7 copy-done.20
  19.3 1.4 constant_dynamic-slice_fusion.momentum_ref
  20.6 1.5 constant_dynamic-slice_fusion.1.refs_0_
  22.1 4.4 %collective-permute-done.3.refs_4_ = bf16[512,256]{1,0:T(8,128)(2,1)S(1)} collective-permute-done((bf16[512,256]{1,0:T(8,128)(2,1)S(1)}, bf16[512,256]{1,0:T(8,128)(2,1)S(1)}, u32[]{:S(2)}, u32[]{:S(2)}) %collective-permute-start.3) | collective-permute-done | bytes 262176 | tf_op jit(solution)/shard_map/ppermute | solution.py:29
  26.5 0.7 collective-permute-done.2.refs_3_.refs_2_
  27.2 2.1 %collective-permute-done.1.refs_2_.refs_1_ = bf16[512,256]{1,0:T(8,128)(2,1)S(1)} collective-permute-done((bf16[512,256]{1,0:T(8,128)(2,1)S(1)}, bf16[512,256]{1,0:T(8,128)(2,1)S(1)}, u32[]{:S(2)}, u32[]{:S(2)}) %collective-permute-start.1) | collective-permute-done | bytes 262176 | tf_op jit(solution)/shard_map/ppermute | solution.py:29
  29.3 0.7 copy-done.12
  30.0 7.0 %all-to-all-done.recv_ref = bf16[16,32,1024]{2,1,0:T(8,128)(2,1)} async-done(((bf16[16,32,1024]{2,1,0:T(8,128)(2,1)}), bf16[16,32,1024]{2,1,0:T(8,128)(2,1)}, u32[]{:S(2)}, u32[]{:S(2)}) %all-to-all-start) | async-done | bytes 1048608 | tf_op jit(solution)/shard_map/all_to_all | solution.py:228
  37.0 2.8 %average_slice.1 = (bf16[16,32,768]{2,1,0:T(8,128)(2,1)}, bf16[32,256]{1,0:T(8,128)(2,1)}, bf16[32,256]{1,0:T(8,128)(2,1)}) custom-call(bf16[16,32,1024]{2,1,0:T(8,128)(2,1)} %all-to-all-done.recv_ref, bf16[32,1024]{1,0:T(8,128)(2,1)} %after.6.outer_ref, f32[32,256]{1,0:T(8,128)} %constant_dynamic-slice_fusion.momentum_ref), custom_call_target="tpu_custom_call" | custom-call | flops 5242880 | bytes 2097152 | tf_op jit(solution)/shard_map/average_slice/pallas_call | solution.py:88
  39.8 6.4 %all-to-all-start.1 = ((bf16[16,32,768]{2,1,0:T(8,128)(2,1)}), bf16[16,32,768]{2,1,0:T(8,128)(2,1)S(1)}, u32[]{:S(2)}, u32[]{:S(2)}) async-start(bf16[16,32,768]{2,1,0:T(8,128)(2,1)} %get-tuple-element.15), calls=%async_computation.1 | async-start | bytes 1572864 | tf_op jit(solution)/shard_map/all_to_all | solution.py:236
  46.3 2.8 %collective-permute-start.7 = (bf16[512,256]{1,0:T(8,128)(2,1)S(1)}, bf16[512,256]{1,0:T(8,128)(2,1)S(1)}, u32[]{:S(2)}, u32[]{:S(2)}) collective-permute-start(bf16[512,256]{1,0:T(8,128)(2,1)S(1)} %copy-done.13), channel_id=1, source_target_pairs={{0,4},{1,5},{2,6},{3,7},{4,0},{5,1},{6,2},{7,3},{8,12},{9,13},{10,... | collective-permute-start | bytes 786440 | tf_op jit(solution)/shard_map/ppermute | solution.py:29
  49.1 0.9 collective-permute-start.6
  50.0 0.6 collective-permute-start.5
  50.6 2.6 %collective-permute-start.12 = (bf16[32,256]{1,0:T(8,128)(2,1)S(1)}, bf16[32,256]{1,0:T(8,128)(2,1)S(1)}, u32[]{:S(2)}, u32[]{:S(2)}) collective-permute-start(bf16[32,256]{1,0:T(8,128)(2,1)S(1)} %copy-done.27), channel_id=1, source_target_pairs={{0,8},{1,9},{2,10},{3,11},{4,12},{5,13},{6,14},{7,15},{8,0},{9,1},... | collective-permute-start | bytes 49160 | tf_op jit(solution)/shard_map/ppermute | solution.py:29
  53.2 1.8 %collective-permute-done.12 = bf16[32,256]{1,0:T(8,128)(2,1)S(1)} collective-permute-done((bf16[32,256]{1,0:T(8,128)(2,1)S(1)}, bf16[32,256]{1,0:T(8,128)(2,1)S(1)}, u32[]{:S(2)}, u32[]{:S(2)}) %collective-permute-start.12) | collective-permute-done | bytes 16416 | tf_op jit(solution)/shard_map/ppermute | solution.py:29
  55.0 0.6 collective-permute-start.15
  55.6 2.0 %collective-permute-start.13 = (bf16[2,32,256]{2,1,0:T(8,128)(2,1)S(1)}, bf16[2,32,256]{2,1,0:T(8,128)(2,1)S(1)}, u32[]{:S(2)}, u32[]{:S(2)}) collective-permute-start(bf16[2,32,256]{2,1,0:T(8,128)(2,1)S(1)} %pad_maximum_fusion.3), channel_id=1, source_target_pairs={{0,2},{1,3},{2,4},{3,5},{4,6},{5,7},{6,0},{7,1},{8,10},{9,11},{10,... | collective-permute-start | bytes 98312 | tf_op jit(solution)/shard_map/ppermute | solution.py:29
  57.6 4.8 %collective-permute-done.13 = bf16[2,32,256]{2,1,0:T(8,128)(2,1)S(1)} collective-permute-done((bf16[2,32,256]{2,1,0:T(8,128)(2,1)S(1)}, bf16[2,32,256]{2,1,0:T(8,128)(2,1)S(1)}, u32[]{:S(2)}, u32[]{:S(2)}) %collective-permute-start.13) | collective-permute-done | bytes 32800 | tf_op jit(solution)/shard_map/ppermute | solution.py:29
  62.4 3.1 %collective-permute-done.14 = bf16[2,32,256]{2,1,0:T(8,128)(2,1)S(1)} collective-permute-done((bf16[2,32,256]{2,1,0:T(8,128)(2,1)S(1)}, bf16[2,32,256]{2,1,0:T(8,128)(2,1)S(1)}, u32[]{:S(2)}, u32[]{:S(2)}) %collective-permute-start.14) | collective-permute-done | bytes 32800 | tf_op jit(solution)/shard_map/ppermute | solution.py:29
  65.5 1.2 collective-permute-start.16
  66.7 0.7 copy-done.14
  67.4 0.1 copy-done.16
  67.6 0.2 copy-done.22
  67.8 3.3 %multiply_convert_fusion.refs_8_.refs_1_ = bf16[512,768]{1,0:T(8,128)(2,1)} fusion(f32[512,1024]{1,0:T(8,128)} %param.6, bf16[512,768]{1,0:T(8,128)(2,1)} %after.7.refs_0_, bf16[512,1024]{1,0:T(8,128)(2,1)S(1)} %bitcast.45, bf16[512,1024]{1,0:T(8,128)(2,1)} %param.4), kind=kLoop, calls=%fused_computation.15 | loop fusion | flops 5505024 | bytes 4718592 | tf_op jit(solution)/shard_map/convert_element_type | solution.py:103
  71.1 2.6 %collective-permute-start.8 = (bf16[512,768]{1,0:T(8,128)(2,1)}, bf16[512,768]{1,0:T(8,128)(2,1)S(1)}, u32[]{:S(2)}, u32[]{:S(2)}) collective-permute-start(bf16[512,768]{1,0:T(8,128)(2,1)} %multiply_convert_fusion.refs_8_.refs_1_), channel_id=1, source_target_pairs={{0,8},{1,9},{2,10},{3,11},{4,12},{5,13},{6,14},{7,15},{8,0},{9,1},... | collective-permute-start | bytes 2359304 | tf_op jit(solution)/shard_map/ppermute | solution.py:29
  73.8 0.7 pad_maximum_fusion.2.refs_0_
  74.5 2.6 %broadcast_in_dim.15 = bf16[8,2,9,32,256]{4,3,2,1,0:T(8,128)(2,1)} broadcast(bf16[2,9,32,256]{3,2,1,0:T(8,128)(2,1)} %after.10), dimensions={1,2,3,4} | broadcast | bytes 2654208 | tf_op jit(solution)/shard_map/broadcast_in_dim | solution.py:42
  77.1 6.1 %all-to-all-start.2 = ((bf16[8,2,9,32,256]{4,3,2,1,0:T(8,128)(2,1)}), bf16[8,2,9,32,256]{4,3,2,1,0:T(8,128)(2,1)}, u32[]{:S(2)}, u32[]{:S(2)}) async-start(bf16[8,2,9,32,256]{4,3,2,1,0:T(8,128)(2,1)} %broadcast_in_dim.15), calls=%async_computation.2 | async-start | bytes 4718592 | tf_op jit(solution)/shard_map/all_to_all | solution.py:41
  83.2 2.0 %collective-permute-start.10 = (bf16[512,768]{1,0:T(8,128)(2,1)}, bf16[512,768]{1,0:T(8,128)(2,1)}, u32[]{:S(2)}, u32[]{:S(2)}) collective-permute-start(bf16[512,768]{1,0:T(8,128)(2,1)} %multiply_convert_fusion.refs_8_.refs_1_), channel_id=1, source_target_pairs={{0,2},{1,3},{2,4},{3,5},{4,6},{5,7},{6,0},{7,1},{8,10},{9,11},{10,... | collective-permute-start | bytes 2359304 | tf_op jit(solution)/shard_map/ppermute | solution.py:29
  85.2 0.7 collective-permute-start.11
  85.9 2.6 %collective-permute-done.8.refs_11_ = bf16[512,768]{1,0:T(8,128)(2,1)S(1)} collective-permute-done((bf16[512,768]{1,0:T(8,128)(2,1)}, bf16[512,768]{1,0:T(8,128)(2,1)S(1)}, u32[]{:S(2)}, u32[]{:S(2)}) %collective-permute-start.8) | collective-permute-done | bytes 786464 | tf_op jit(solution)/shard_map/ppermute | solution.py:29
  88.4 2.4 %collective-permute-start.9 = (bf16[512,768]{1,0:T(8,128)(2,1)S(1)}, bf16[512,768]{1,0:T(8,128)(2,1)S(1)}, u32[]{:S(2)}, u32[]{:S(2)}) collective-permute-start(bf16[512,768]{1,0:T(8,128)(2,1)S(1)} %collective-permute-done.8.refs_11_), channel_id=1, source_target_pairs={{0,6},{1,7},{2,0},{3,1},{4,2},{5,3},{6,4},{7,5},{8,14},{9,15},{10,... | collective-permute-start | bytes 2359304 | tf_op jit(solution)/shard_map/ppermute | solution.py:29
  90.9 1.1 collective-permute-start.17
  92.0 8.3 %collective-permute-done.10.refs_9_ = bf16[512,768]{1,0:T(8,128)(2,1)} collective-permute-done((bf16[512,768]{1,0:T(8,128)(2,1)}, bf16[512,768]{1,0:T(8,128)(2,1)}, u32[]{:S(2)}, u32[]{:S(2)}) %collective-permute-start.10) | collective-permute-done | bytes 786464 | tf_op jit(solution)/shard_map/ppermute | solution.py:29
  100.3 1.4 collective-permute-start.18
  101.7 8.1 %blocks_dot.5 = (f32[512,768]{1,0:T(8,128)S(1)}, f32[512,768]{1,0:T(8,128)}) custom-call(s32[4]{0:T(128)S(1)} %fusion.6.at_ref, bf16[512,8192]{1,0:T(8,128)(2,1)} %collective-permute-done.refs_1_.refs_0_.refs_2_.refs_3_.refs_4_.refs_5_.refs_6_.refs_7_, bf16[512,8192]{1,0:T(8,128)(2,1)} %collective-permute-done.refs_1_.refs_0_.refs_2_.refs_3_.refs_4_.refs_5_.refs_6_.refs_7_, ...), custom_call_target="tpu_custom_call" | custom-call | flops 3221225472 | bytes 10485760 | tf_op jit(solution)/shard_map/blocks_dot/pallas_call | solution.py:189
  109.8 1.2 copy-done.2
  111.0 7.4 %collective-permute-done.9.refs_0_ = bf16[512,768]{1,0:T(8,128)(2,1)S(1)} collective-permute-done((bf16[512,768]{1,0:T(8,128)(2,1)S(1)}, bf16[512,768]{1,0:T(8,128)(2,1)S(1)}, u32[]{:S(2)}, u32[]{:S(2)}) %collective-permute-start.9) | collective-permute-done | bytes 786464 | tf_op jit(solution)/shard_map/ppermute | solution.py:29
  118.3 0.9 copy-done
  119.2 1.2 collective-permute-start.19
  120.6 1.1 copy-done.1
  121.7 5.8 %blocks_dot.6 = (f32[512,768]{1,0:T(8,128)S(1)}, f32[512,768]{1,0:T(8,128)S(1)}) custom-call(s32[2]{0:T(128)S(1)} %fusion.7.at_ref, bf16[512,8192]{1,0:T(8,128)(2,1)} %collective-permute-done.refs_1_.refs_0_.refs_2_.refs_3_.refs_4_.refs_5_.refs_6_.refs_7_, ...), custom_call_target="tpu_custom_call" | custom-call | flops 1610612736 | bytes 6815744 | tf_op jit(solution)/shard_map/blocks_dot/pallas_call | solution.py:189
  127.6 6.4 %collective-permute-done.18.refs_2_ = bf16[512,768]{1,0:T(8,128)(2,1)S(1)} collective-permute-done((bf16[512,768]{1,0:T(8,128)(2,1)}, bf16[512,768]{1,0:T(8,128)(2,1)S(1)}, u32[]{:S(2)}, u32[]{:S(2)}) %collective-permute-start.18) | collective-permute-done | bytes 786464 | tf_op jit(solution)/shard_map/ppermute | solution.py:29
  134.0 1.2 collective-permute-done.19.refs_3_
  135.2 3.7 %blocks_dot.8 = f32[512,768]{1,0:T(8,128)} custom-call(s32[2]{0:T(128)S(1)} %fusion.8.at_ref, bf16[512,8192]{1,0:T(8,128)(2,1)} %collective-permute-done.refs_1_.refs_0_.refs_2_.refs_3_.refs_4_.refs_5_.refs_6_.refs_7_, bf16[512,8192]{1,0:T(8,128)(2,1)} %collective-permute-done.refs_1_.refs_0_.refs_2_.refs_3_.refs_4_.refs_5_.refs_6_.refs_7_, ...), custom_call_target="tpu_custom_call" | custom-call | flops 805306368 | bytes 4194304 | tf_op jit(solution)/shard_map/blocks_dot/pallas_call | solution.py:189
  138.9 4.5 %collective-permute-start.20 = (f32[512,768]{1,0:T(8,128)}, f32[512,768]{1,0:T(8,128)}, u32[]{:S(2)}, u32[]{:S(2)}) collective-permute-start(f32[512,768]{1,0:T(8,128)} %blocks_dot.8), channel_id=1, source_target_pairs={{0,1},{1,0},{2,3},{3,2},{4,5},{5,4},{6,7},{7,6},{8,9},{9,8},{10,11... | collective-permute-start | bytes 4718600 | tf_op jit(solution)/shard_map/ppermute | solution.py:29
  143.5 3.8 %convert_add_fusion.1 = (f32[512,768]{1,0:T(8,128)}, bf16[512,768]{1,0:T(8,128)(2,1)}) fusion(bf16[512,768]{1,0:T(8,128)(2,1)} %after.9, f32[512,1024]{1,0:T(8,128)} %param.6, bf16[512,1024]{1,0:T(8,128)(2,1)} %param.4), kind=kLoop, calls=%fused_computation.4 | loop fusion | flops 3538944 | bytes 5505024 | tf_op jit(solution)/shard_map/add | solution.py:62
  147.3 2.8 %blocks_dot.7 = f32[512,768]{1,0:T(8,128)S(1)} custom-call(s32[2]{0:T(128)S(1)} %fusion.8.at_ref, bf16[512,8192]{1,0:T(8,128)(2,1)} %bitcast.32, bf16[512,8192]{1,0:T(8,128)(2,1)} %bitcast.33, bf16[512,768]{1,0:T(8,128)(2,1)S(1)} %collective-permute-done.18.refs_2_, bf16[512,768]{1,0:T(8,128)(2,1)S(1)} %collective-permute-done.19.refs_3_, ...), custom_call_target="tpu_custom_call" | custom-call | flops 805306368 | bytes 4194304 | tf_op jit(solution)/shard_map/blocks_dot/pallas_call | solution.py:189
  150.1 2.8 %add_bitcast_fusion = f32[1,512,768]{2,1,0:T(8,128)} fusion(f32[512,768]{1,0:T(8,128)S(1)} %blocks_dot.7, f32[512,768]{1,0:T(8,128)} %collective-permute-done.20), kind=kLoop, calls=%fused_computation.14 | loop fusion | flops 393216 | bytes 4718592 | tf_op jit(solution)/shard_map/concatenate | solution.py:276
  153.0 0.9 copy-done.7
  154.3 2.5 %mix_early.1 = (bf16[8,512,256]{2,1,0:T(8,128)(2,1)S(1)}, bf16[512,256]{1,0:T(8,128)(2,1)S(1)}, bf16[512,256]{1,0:T(8,128)(2,1)S(1)}) custom-call(s32[1]{0:T(128)} %bitcast.8.yl_ref, bf16[512,256]{1,0:T(8,128)(2,1)S(1)} %copy-done.21, bf16[512,256]{1,0:T(8,128)(2,1)S(1)} %copy-done.13, bf16[512,256]{1,0:T(8,128)(2,1)S(1)} %copy-done.11, ...), custom_call_target="tpu_custom_call" | custom-call | flops 3145728 | bytes 6291456 | tf_op jit(solution)/shard_map/mix_early/pallas_call | solution.py:128
  156.8 7.1 %blocks_dot.9 = (f32[512,256]{1,0:T(8,128)S(1)}, f32[512,256]{1,0:T(8,128)S(1)}) custom-call(s32[8]{0:T(128)S(1)} %multiply_add_fusion.at_ref, bf16[512,8192]{1,0:T(8,128)(2,1)} %collective-permute-done.refs_1_.refs_0_.refs_2_.refs_3_.refs_4_.refs_5_.refs_6_.refs_7_, ...), custom_call_target="tpu_custom_call" | custom-call | flops 2147483648 | bytes 11534336 | tf_op jit(solution)/shard_map/blocks_dot/pallas_call | solution.py:189
  163.9 0.1 collective-permute-start.21
  164.0 1.1 pad_maximum_fusion.1
  165.1 1.1 convert_add_fusion.4
  166.3 1.6 pad_maximum_fusion
  168.0 1.3 copy-done.23
  169.3 1.2 fusion
  (82 shorter events, 1.1 us)
Async XLA Ops:
  0.6 11.0 %copy-start.25 = (bf16[1,512,1024]{2,1,0:T(8,128)(2,1)S(1)}, bf16[1,512,1024]{2,1,0:T(8,128)(2,1)}, u32[]{:S(2)}) copy-start(bf16[1,512,1024]{2,1,0:T(8,128)(2,1)} %param.5) | copy-start | bytes 3145732
  0.6 28.6 %collective-permute-start = (bf16[512,8192]{1,0:T(8,128)(2,1)}, bf16[512,8192]{1,0:T(8,128)(2,1)}, u32[]{:S(2)}, u32[]{:S(2)}) collective-permute-start(bf16[512,8192]{1,0:T(8,128)(2,1)} %bitcast.25), channel_id=1, source_target_pairs={{0,1},{1,0},{2,3},{3,2},{4,5},{5,4},{6,7},{7,6},{8,9},{9,8},{10,11... | collective-permute-start | bytes 25165832 | tf_op jit(solution)/shard_map/ppermute | solution.py:29
  4.0 33.0 %all-to-all-start = ((bf16[16,32,1024]{2,1,0:T(8,128)(2,1)}), bf16[16,32,1024]{2,1,0:T(8,128)(2,1)}, u32[]{:S(2)}, u32[]{:S(2)}) async-start(bf16[16,32,1024]{2,1,0:T(8,128)(2,1)} %bitcast.43), calls=%async_computation | async-start | bytes 2097152 | tf_op jit(solution)/shard_map/all_to_all | solution.py:228
  11.6 10.5 %collective-permute-start.4 = (bf16[512,256]{1,0:T(8,128)(2,1)S(1)}, bf16[512,256]{1,0:T(8,128)(2,1)S(1)}, u32[]{:S(2)}, u32[]{:S(2)}) collective-permute-start(bf16[512,256]{1,0:T(8,128)(2,1)S(1)} %slice.22.refs_0_), channel_id=1, source_target_pairs={{0,4},{1,5},{2,6},{3,7},{4,0},{5,1},{6,2},{7,3},{8,12},{9,13},{10,... | collective-permute-start | bytes 786440 | tf_op jit(solution)/shard_map/ppermute | solution.py:29
  14.5 12.0 %collective-permute-start.3 = (bf16[512,256]{1,0:T(8,128)(2,1)S(1)}, bf16[512,256]{1,0:T(8,128)(2,1)S(1)}, u32[]{:S(2)}, u32[]{:S(2)}) collective-permute-start(bf16[512,256]{1,0:T(8,128)(2,1)S(1)} %slice.22.refs_0_), channel_id=1, source_target_pairs={{0,6},{1,7},{2,0},{3,1},{4,2},{5,3},{6,4},{7,5},{8,14},{9,15},{10,... | collective-permute-start | bytes 786440 | tf_op jit(solution)/shard_map/ppermute | solution.py:29
  15.3 11.8 %collective-permute-start.2 = (bf16[512,256]{1,0:T(8,128)(2,1)S(1)}, bf16[512,256]{1,0:T(8,128)(2,1)S(1)}, u32[]{:S(2)}, u32[]{:S(2)}) collective-permute-start(bf16[512,256]{1,0:T(8,128)(2,1)S(1)} %slice.22.refs_0_), channel_id=1, source_target_pairs={{0,2},{1,3},{2,4},{3,5},{4,6},{5,7},{6,0},{7,1},{8,10},{9,11},{10,... | collective-permute-start | bytes 786440 | tf_op jit(solution)/shard_map/ppermute | solution.py:29
  15.9 13.3 %collective-permute-start.1 = (bf16[512,256]{1,0:T(8,128)(2,1)S(1)}, bf16[512,256]{1,0:T(8,128)(2,1)S(1)}, u32[]{:S(2)}, u32[]{:S(2)}) collective-permute-start(bf16[512,256]{1,0:T(8,128)(2,1)S(1)} %slice.22.refs_0_), channel_id=1, source_target_pairs={{0,8},{1,9},{2,10},{3,11},{4,12},{5,13},{6,14},{7,15},{8,0},{9,1},... | collective-permute-start | bytes 786440 | tf_op jit(solution)/shard_map/ppermute | solution.py:29
  18.6 0.7 copy-start.20
  22.1 7.1 %copy-start.6 = (bf16[512,256]{1,0:T(8,128)(2,1)}, bf16[512,256]{1,0:T(8,128)(2,1)S(1)}, u32[]{:S(2)}) copy-start(bf16[512,256]{1,0:T(8,128)(2,1)S(1)} %collective-permute-done.4.refs_5_.refs_6_) | copy-start | bytes 786436
  26.5 2.7 %copy-start.8 = (bf16[512,256]{1,0:T(8,128)(2,1)}, bf16[512,256]{1,0:T(8,128)(2,1)S(1)}, u32[]{:S(2)}) copy-start(bf16[512,256]{1,0:T(8,128)(2,1)S(1)} %collective-permute-done.3.refs_4_) | copy-start | bytes 786436
  27.2 2.1 %copy-start.10 = (bf16[512,256]{1,0:T(8,128)(2,1)}, bf16[512,256]{1,0:T(8,128)(2,1)S(1)}, u32[]{:S(2)}) copy-start(bf16[512,256]{1,0:T(8,128)(2,1)S(1)} %collective-permute-done.2.refs_3_.refs_2_) | copy-start | bytes 786436
  29.3 0.7 copy-start.12
  30.0 16.3 %copy-start.13 = (bf16[512,256]{1,0:T(8,128)(2,1)S(1)}, bf16[512,256]{1,0:T(8,128)(2,1)}, u32[]{:S(2)}) copy-start(bf16[512,256]{1,0:T(8,128)(2,1)} %copy-done.12) | copy-start | bytes 786436
  39.8 10.8 %copy-start.27 = (bf16[32,256]{1,0:T(8,128)(2,1)S(1)}, bf16[32,256]{1,0:T(8,128)(2,1)}, u32[]{:S(2)}) copy-start(bf16[32,256]{1,0:T(8,128)(2,1)} %get-tuple-element.17) | copy-start | bytes 49156
  39.8 25.7 %copy-start.28 = (bf16[32,256]{1,0:T(8,128)(2,1)S(1)}, bf16[32,256]{1,0:T(8,128)(2,1)}, u32[]{:S(2)}) copy-start(bf16[32,256]{1,0:T(8,128)(2,1)} %get-tuple-element.18) | copy-start | bytes 49156
  39.8 26.9 %all-to-all-start.1 = ((bf16[16,32,768]{2,1,0:T(8,128)(2,1)}), bf16[16,32,768]{2,1,0:T(8,128)(2,1)S(1)}, u32[]{:S(2)}, u32[]{:S(2)}) async-start(bf16[16,32,768]{2,1,0:T(8,128)(2,1)} %get-tuple-element.15), calls=%async_computation.1 | async-start | bytes 1572864 | tf_op jit(solution)/shard_map/all_to_all | solution.py:236
  46.3 20.4 %collective-permute-start.7 = (bf16[512,256]{1,0:T(8,128)(2,1)S(1)}, bf16[512,256]{1,0:T(8,128)(2,1)S(1)}, u32[]{:S(2)}, u32[]{:S(2)}) collective-permute-start(bf16[512,256]{1,0:T(8,128)(2,1)S(1)} %copy-done.13), channel_id=1, source_target_pairs={{0,4},{1,5},{2,6},{3,7},{4,0},{5,1},{6,2},{7,3},{8,12},{9,13},{10,... | collective-permute-start | bytes 786440 | tf_op jit(solution)/shard_map/ppermute | solution.py:29
  49.1 17.6 %collective-permute-start.6 = (bf16[512,256]{1,0:T(8,128)(2,1)S(1)}, bf16[512,256]{1,0:T(8,128)(2,1)S(1)}, u32[]{:S(2)}, u32[]{:S(2)}) collective-permute-start(bf16[512,256]{1,0:T(8,128)(2,1)S(1)} %copy-done.13), channel_id=1, source_target_pairs={{0,6},{1,7},{2,0},{3,1},{4,2},{5,3},{6,4},{7,5},{8,14},{9,15},{10,... | collective-permute-start | bytes 786440 | tf_op jit(solution)/shard_map/ppermute | solution.py:29
  50.0 16.7 %collective-permute-start.5 = (bf16[512,256]{1,0:T(8,128)(2,1)S(1)}, bf16[512,256]{1,0:T(8,128)(2,1)S(1)}, u32[]{:S(2)}, u32[]{:S(2)}) collective-permute-start(bf16[512,256]{1,0:T(8,128)(2,1)S(1)} %copy-done.13), channel_id=1, source_target_pairs={{0,2},{1,3},{2,4},{3,5},{4,6},{5,7},{6,0},{7,1},{8,10},{9,11},{10,... | collective-permute-start | bytes 786440 | tf_op jit(solution)/shard_map/ppermute | solution.py:29
  50.6 4.4 %collective-permute-start.12 = (bf16[32,256]{1,0:T(8,128)(2,1)S(1)}, bf16[32,256]{1,0:T(8,128)(2,1)S(1)}, u32[]{:S(2)}, u32[]{:S(2)}) collective-permute-start(bf16[32,256]{1,0:T(8,128)(2,1)S(1)} %copy-done.27), channel_id=1, source_target_pairs={{0,8},{1,9},{2,10},{3,11},{4,12},{5,13},{6,14},{7,15},{8,0},{9,1},... | collective-permute-start | bytes 49160 | tf_op jit(solution)/shard_map/ppermute | solution.py:29
  55.0 10.5 %collective-permute-start.15 = (bf16[2,32,256]{2,1,0:T(8,128)(2,1)S(1)}, bf16[2,32,256]{2,1,0:T(8,128)(2,1)S(1)}, u32[]{:S(2)}, u32[]{:S(2)}) collective-permute-start(bf16[2,32,256]{2,1,0:T(8,128)(2,1)S(1)} %pad_maximum_fusion.3), channel_id=1, source_target_pairs={{0,4},{1,5},{2,6},{3,7},{4,0},{5,1},{6,2},{7,3},{8,12},{9,13},{10,... | collective-permute-start | bytes 98312 | tf_op jit(solution)/shard_map/ppermute | solution.py:29
  55.6 6.8 %collective-permute-start.13 = (bf16[2,32,256]{2,1,0:T(8,128)(2,1)S(1)}, bf16[2,32,256]{2,1,0:T(8,128)(2,1)S(1)}, u32[]{:S(2)}, u32[]{:S(2)}) collective-permute-start(bf16[2,32,256]{2,1,0:T(8,128)(2,1)S(1)} %pad_maximum_fusion.3), channel_id=1, source_target_pairs={{0,2},{1,3},{2,4},{3,5},{4,6},{5,7},{6,0},{7,1},{8,10},{9,11},{10,... | collective-permute-start | bytes 98312 | tf_op jit(solution)/shard_map/ppermute | solution.py:29
  62.4 3.1 %collective-permute-start.14 = (bf16[2,32,256]{2,1,0:T(8,128)(2,1)S(1)}, bf16[2,32,256]{2,1,0:T(8,128)(2,1)S(1)}, u32[]{:S(2)}, u32[]{:S(2)}) collective-permute-start(bf16[2,32,256]{2,1,0:T(8,128)(2,1)S(1)} %pad_maximum_fusion.3), channel_id=1, source_target_pairs={{0,6},{1,7},{2,0},{3,1},{4,2},{5,3},{6,4},{7,5},{8,14},{9,15},{10,... | collective-permute-start | bytes 98312 | tf_op jit(solution)/shard_map/ppermute | solution.py:29
  65.5 8.2 %collective-permute-start.16 = (bf16[9,32,256]{2,1,0:T(8,128)(2,1)S(1)}, bf16[9,32,256]{2,1,0:T(8,128)(2,1)S(1)}, u32[]{:S(2)}, u32[]{:S(2)}) collective-permute-start(bf16[9,32,256]{2,1,0:T(8,128)(2,1)S(1)} %bitcast_dynamic-update-slice_fusion), channel_id=1, source_target_pairs={{0,128},{16,144},{32,160},{48,176},{64,192},{80,208},{96,224},{112... | collective-permute-start | bytes 442376 | tf_op jit(solution)/shard_map/ppermute | solution.py:33
  66.7 0.7 copy-start.14
  66.7 0.9 copy-start.16
  66.7 0.9 copy-start.18
  66.7 1.1 copy-start.22
  71.1 17.3 %collective-permute-start.8 = (bf16[512,768]{1,0:T(8,128)(2,1)}, bf16[512,768]{1,0:T(8,128)(2,1)S(1)}, u32[]{:S(2)}, u32[]{:S(2)}) collective-permute-start(bf16[512,768]{1,0:T(8,128)(2,1)} %multiply_convert_fusion.refs_8_.refs_1_), channel_id=1, source_target_pairs={{0,8},{1,9},{2,10},{3,11},{4,12},{5,13},{6,14},{7,15},{8,0},{9,1},... | collective-permute-start | bytes 2359304 | tf_op jit(solution)/shard_map/ppermute | solution.py:29
  77.1 75.8 %all-to-all-start.2 = ((bf16[8,2,9,32,256]{4,3,2,1,0:T(8,128)(2,1)}), bf16[8,2,9,32,256]{4,3,2,1,0:T(8,128)(2,1)}, u32[]{:S(2)}, u32[]{:S(2)}) async-start(bf16[8,2,9,32,256]{4,3,2,1,0:T(8,128)(2,1)} %broadcast_in_dim.15), calls=%async_computation.2 | async-start | bytes 4718592 | tf_op jit(solution)/shard_map/all_to_all | solution.py:41
  83.2 17.1 %collective-permute-start.10 = (bf16[512,768]{1,0:T(8,128)(2,1)}, bf16[512,768]{1,0:T(8,128)(2,1)}, u32[]{:S(2)}, u32[]{:S(2)}) collective-permute-start(bf16[512,768]{1,0:T(8,128)(2,1)} %multiply_convert_fusion.refs_8_.refs_1_), channel_id=1, source_target_pairs={{0,2},{1,3},{2,4},{3,5},{4,6},{5,7},{6,0},{7,1},{8,10},{9,11},{10,... | collective-permute-start | bytes 2359304 | tf_op jit(solution)/shard_map/ppermute | solution.py:29
  85.2 16.5 %collective-permute-start.11 = (bf16[512,768]{1,0:T(8,128)(2,1)}, bf16[512,768]{1,0:T(8,128)(2,1)S(1)}, u32[]{:S(2)}, u32[]{:S(2)}) collective-permute-start(bf16[512,768]{1,0:T(8,128)(2,1)} %multiply_convert_fusion.refs_8_.refs_1_), channel_id=1, source_target_pairs={{0,6},{1,7},{2,0},{3,1},{4,2},{5,3},{6,4},{7,5},{8,14},{9,15},{10,... | collective-permute-start | bytes 2359304 | tf_op jit(solution)/shard_map/ppermute | solution.py:29
  88.4 29.9 %collective-permute-start.9 = (bf16[512,768]{1,0:T(8,128)(2,1)S(1)}, bf16[512,768]{1,0:T(8,128)(2,1)S(1)}, u32[]{:S(2)}, u32[]{:S(2)}) collective-permute-start(bf16[512,768]{1,0:T(8,128)(2,1)S(1)} %collective-permute-done.8.refs_11_), channel_id=1, source_target_pairs={{0,6},{1,7},{2,0},{3,1},{4,2},{5,3},{6,4},{7,5},{8,14},{9,15},{10,... | collective-permute-start | bytes 2359304 | tf_op jit(solution)/shard_map/ppermute | solution.py:29
  90.9 29.7 %collective-permute-start.17 = (bf16[512,768]{1,0:T(8,128)(2,1)S(1)}, bf16[512,768]{1,0:T(8,128)(2,1)}, u32[]{:S(2)}, u32[]{:S(2)}) collective-permute-start(bf16[512,768]{1,0:T(8,128)(2,1)S(1)} %collective-permute-done.8.refs_11_), channel_id=1, source_target_pairs={{0,2},{1,3},{2,4},{3,5},{4,6},{5,7},{6,0},{7,1},{8,10},{9,11},{10,... | collective-permute-start | bytes 2359304 | tf_op jit(solution)/shard_map/ppermute | solution.py:29
  100.3 33.7 %collective-permute-start.18 = (bf16[512,768]{1,0:T(8,128)(2,1)}, bf16[512,768]{1,0:T(8,128)(2,1)S(1)}, u32[]{:S(2)}, u32[]{:S(2)}) collective-permute-start(bf16[512,768]{1,0:T(8,128)(2,1)} %collective-permute-done.10.refs_9_), channel_id=1, source_target_pairs={{0,2},{1,3},{2,4},{3,5},{4,6},{5,7},{6,0},{7,1},{8,10},{9,11},{10,... | collective-permute-start | bytes 2359304 | tf_op jit(solution)/shard_map/ppermute | solution.py:29
  109.8 1.2 copy-start.2
  118.3 0.9 copy-start
  119.2 16.0 %collective-permute-start.19 = (bf16[512,768]{1,0:T(8,128)(2,1)}, bf16[512,768]{1,0:T(8,128)(2,1)S(1)}, u32[]{:S(2)}, u32[]{:S(2)}) collective-permute-start(bf16[512,768]{1,0:T(8,128)(2,1)} %after.8.refs_1_.refs_5_), channel_id=1, source_target_pairs={{0,6},{1,7},{2,0},{3,1},{4,2},{5,3},{6,4},{7,5},{8,14},{9,15},{10,... | collective-permute-start | bytes 2359304 | tf_op jit(solution)/shard_map/ppermute | solution.py:29
  120.6 1.1 copy-start.1
  127.6 11.3 %copy-start.3 = (f32[512,768]{1,0:T(8,128)}, f32[512,768]{1,0:T(8,128)S(1)}, u32[]{:S(2)}) copy-start(f32[512,768]{1,0:T(8,128)S(1)} %get-tuple-element.20.refs_1_.refs_4_) | copy-start | bytes 4718596
  127.6 11.3 %copy-start.4 = (f32[512,768]{1,0:T(8,128)}, f32[512,768]{1,0:T(8,128)S(1)}, u32[]{:S(2)}) copy-start(f32[512,768]{1,0:T(8,128)S(1)} %get-tuple-element.23.refs_4_) | copy-start | bytes 4718596
  138.9 11.2 %collective-permute-start.20 = (f32[512,768]{1,0:T(8,128)}, f32[512,768]{1,0:T(8,128)}, u32[]{:S(2)}, u32[]{:S(2)}) collective-permute-start(f32[512,768]{1,0:T(8,128)} %blocks_dot.8), channel_id=1, source_target_pairs={{0,1},{1,0},{2,3},{3,2},{4,5},{5,4},{6,7},{7,6},{8,9},{9,8},{10,11... | collective-permute-start | bytes 4718600 | tf_op jit(solution)/shard_map/ppermute | solution.py:29
  143.5 3.8 %copy-start.5 = (f32[512,768]{1,0:T(8,128)S(1)}, f32[512,768]{1,0:T(8,128)}, u32[]{:S(2)}) copy-start(f32[512,768]{1,0:T(8,128)} %copy-done.4) | copy-start | bytes 4718596
  152.9 0.9 copy-start.7
  152.9 1.0 copy-start.9
  152.9 1.1 copy-start.11
  152.9 1.2 copy-start.15
  152.9 1.3 copy-start.17
  152.9 1.3 copy-start.19
  152.9 1.4 copy-start.21
  156.8 7.2 %copy-start.26 = (bf16[512,768]{1,0:T(8,128)(2,1)S(1)}, bf16[512,768]{1,0:T(8,128)(2,1)}, u32[]{:S(2)}) copy-start(bf16[512,768]{1,0:T(8,128)(2,1)} %get-tuple-element.28) | copy-start | bytes 2359300
  163.9 4.0 %collective-permute-start.21 = (f32[512,256]{1,0:T(8,128)S(1)}, f32[512,256]{1,0:T(8,128)S(1)}, u32[]{:S(2)}, u32[]{:S(2)}) collective-permute-start(f32[512,256]{1,0:T(8,128)S(1)} %get-tuple-element.26), channel_id=1, source_target_pairs={{0,1},{1,0},{2,3},{3,2},{4,5},{5,4},{6,7},{7,6},{8,9},{9,8},{10,11... | collective-permute-start | bytes 1572872 | tf_op jit(solution)/shard_map/ppermute | solution.py:29
  164.0 2.2 %copy-start.24 = (f32[512,768]{1,0:T(8,128)S(1)}, f32[512,768]{1,0:T(8,128)}, u32[]{:S(2)}) copy-start(f32[512,768]{1,0:T(8,128)} %get-tuple-element.27) | copy-start | bytes 4718596
  167.9 1.4 copy-start.23

commit v2 on v1

--- a/solution.py
+++ b/solution.py
@@ -35,12 +35,6 @@
 
 def to_all_replicas(array):
     return lax.all_to_all(jnp.broadcast_to(array[None], (REP, *array.shape)), "rep", 0, 0)
-
-
-def to_all_z(array):
-    return lax.all_to_all(
-        jnp.broadcast_to(array[None], (Z, *array.shape)), "rep", 0, 0, axis_index_groups=SAME_YL
-    )
 
 
 def after(array, *others):
@@ -138,7 +132,7 @@
             jax.ShapeDtypeStruct((rows, wide), BF16),
             jax.ShapeDtypeStruct((rows, wide), BF16),
         ],
-        compiler_params=pltpu.CompilerParams(vmem_limit_bytes=48 * MIB),
+        compiler_params=pltpu.CompilerParams(vmem_limit_bytes=60 * MIB),
         cost_estimate=pl.CostEstimate(
             flops=3 * count * rows * wide, bytes_accessed=6 * count * rows * wide, transcendentals=0
         ),
@@ -146,7 +140,7 @@
     )(yl[None], *inners, *([late] * len(lates)))
 
 
-def blocks_dot(lefts, blocks, pieces, start=None):
+def blocks_dot(lefts, blocks, pieces, start=None, out=F32):
     rows, tile = lefts[0].shape[0], 256
     steps = rows // tile
     count, sides = len(pieces), len(lefts)
@@ -171,7 +165,7 @@
                     right = rights[found[k]]
                     right = right[piece[1]] if len(piece) > 1 else right[...]
                     total = total + jnp.dot(refs[side * count + k][...], right, preferred_element_type=F32)
-                refs[side - sides][...] = total
+                refs[side - sides][...] = total.astype(out)
 
     def row(side, i):
         return jnp.clip(i - side * steps, 0, steps - 1)
@@ -196,7 +190,7 @@
                 + [row_spec(side) for side in range(len(added))],
                 out_specs=[row_spec(side) for side in range(sides)],
             ),
-            out_shape=[jax.ShapeDtypeStruct((rows, width), F32)] * sides,
+            out_shape=[jax.ShapeDtypeStruct((rows, width), out)] * sides,
             compiler_params=pltpu.CompilerParams(vmem_limit_bytes=48 * MIB),
             cost_estimate=pl.CostEstimate(
                 flops=2 * sides * rows * deep * count * width,
@@ -230,28 +224,27 @@
     mine = inner[:, early]
     there, left, right, across = (fsdp_move(mine, *to) for to in ((1, 0), (0, 1), (0, -1), (0, 2)))
     outer_part = lax.dynamic_slice(outer_weights, (rep * part, 0), (part, columns))
-    outer_part = after(outer_part, their_tokens, there, left, right, across)
+    there_left, there_right, there_across = (fsdp_move(there, 0, dx) for dx in (1, -1, 2))
+    outer_part = after(outer_part, there, left, right, across, there_left, there_right, there_across)
     momentum_part = lax.dynamic_slice(momentum, (rep * part, MAIN), (part, EARLY_WIDE))
     copies, outer_slice, mean = average_slice(recv, outer_part, momentum_part)
     average = lax.all_to_all(copies, "rep", 0, 0).reshape(rows, MAIN)
 
-    there_left, there_right, there_across = (fsdp_move(there, 0, dx) for dx in (1, -1, 2))
     inners = [mine, there, left, there_left, right, there_right, across, there_across]
     pair = jnp.stack([outer_slice, fsdp_move(outer_slice, dy=1)])
     slices = jnp.concatenate(
         [pair, fsdp_move(pair, dx=1), fsdp_move(pair, dx=-1), fsdp_move(pair, dx=2), mean[None]]
     )
     slices = jnp.stack([slices, swap_yl(slices)])
-    average = after(average, there_left, there_right, there_across)
-    mixed = mix(
-        inner[:, :MAIN], update(outer_weights[:, :MAIN], momentum[:, :MAIN], average.astype(F32))[0]
-    )
-    late = to_all_z(after(slices, mixed))
+    slices = jnp.broadcast_to(slices[None], (Z, *slices.shape))
+    outer_main, momentum_main = update(outer_weights[:, :MAIN], momentum[:, :MAIN], average.astype(F32))
+    mixed = mix(inner[:, :MAIN], outer_main)
+    late = lax.all_to_all(slices, "rep", 0, 0, axis_index_groups=SAME_YL)
 
     both = [their_tokens, token_rows]
 
-    def dot(chips, pieces, start=None, lefts=both):
-        return blocks_dot(lefts, CORE * chips_of(chips) + core, pieces, start)
+    def dot(chips, pieces, start=None, lefts=both, out=F32):
+        return blocks_dot(lefts, CORE * chips_of(chips) + core, pieces, start, out)
 
     left, right, there = fsdp_move(mixed, dx=1), fsdp_move(mixed, dx=-1), fsdp_move(mixed, dy=1)
     there_left, there_right, across = fsdp_move(there, dx=1), fsdp_move(there, dx=-1), fsdp_move(left, dx=1)
@@ -261,20 +254,19 @@
     sums = dot(SIDES, [(there_left,), (there_right,)], sums)
 
     mixed_early, outer_early, average_early = mix_early(inners, after(late, sums[0]), yl)
-    sums_early = dot(ORDER, [(mixed_early, k) for k in range(CHIPS)])
-    theirs_early = fsdp_move(sums_early[0], dc=1)
-    outer_main, momentum_main = update(
-        outer_weights[:, :MAIN], momentum[:, :MAIN], after(average, there_right).astype(F32)
-    )
+    pieces = [(mixed_early, k) for k in range(CHIPS)]
+    theirs_early = fsdp_move(dot(ORDER, pieces, lefts=both[:1], out=BF16)[0], dc=1)
+    ours_early = dot(ORDER, pieces, lefts=both[1:])[0]
     momentum_early = 0.9 * momentum[:, early] + average_early.astype(F32)
     outer_next = jnp.concatenate([outer_main, outer_early], axis=1)
     momentum_next = jnp.concatenate([momentum_main, momentum_early], axis=1)
 
     last = [(across,), (there_across,)]
-    theirs = fsdp_move(dot(LAST, last, sums[:1], both[:1])[0], dc=1)
+    theirs = fsdp_move(dot(LAST, last, sums[:1], both[:1], BF16)[0], dc=1)
     ours = dot(LAST, last, sums[1:], both[1:])[0]
-    keys = jnp.concatenate([ours + theirs, sums_early[1] + theirs_early], axis=1) * width ** (-0.5)
-    return outer_next, momentum_next, keys.astype(BF16)[None]
+    scale = width ** (-0.5)
+    keys = [((o + t.astype(F32)) * scale).astype(BF16) for o, t in ((ours, theirs), (ours_early, theirs_early))]
+    return outer_next, momentum_next, jnp.concatenate(keys, axis=1)[None]
 
 
 def solution(mesh):

time: 171 us -> 162 us (0.947)
  other arithmetic: 16 us -> 9.26 us
  starting transfers between devices: 57.1 us -> 54.1 us
    all_to_all x1, waiting for transfers between devices: 7.03 us -> 0.01 us  [shards(): recv = lax.all_to_all(inner.reshape(REP, part, columns), 'rep', 0, 0)]
    ppermute x1, waiting for transfers between devices: 0.01 us -> 4.19 us  [swap_yl(): return lax.ppermute(array, 'rep', [(r, (r + Z) % REP) for r in range(REP)])]
    ppermute x21, starting transfers between devices: 35.8 us -> 31.7 us  [fsdp_move(): return lax.ppermute(array, 'fsdp', perm)]
    add x5 -> x4, other arithmetic: 4.03 us -> 0.24 us  [dot(): return blocks_dot(lefts, CORE * chips_of(chips) + core, pieces, start, out)]
    all_to_all x1, waiting for transfers between devices: 0.01 us -> 3.29 us  [shards(): late = lax.all_to_all(slices, 'rep', 0, 0, axis_index_groups=SAME_YL)]
    concatenate x2 -> x0, other arithmetic: 2.84 us -> none  [shards(): jnp.concatenate([ours + theirs, sums_early[1] + theirs_early], axis=1)]
    pallas_call x1, Pallas kernels: 2.45 us -> 4.35 us  [mix_early(): pl.pallas_call(kernel, grid_spec=pltpu.PrefetchScalarGridSpec(num_scalar_...]
    unnamed x63 -> x45, local copies, waits for them, and re-layouts: 8.41 us -> 6.9 us
  transfers between devices with their start and end apart: 25 -> 25, of which waited for: 12 -> 11; matrix products, arithmetic and copies ran while one was open for 12% -> 8% of each run, Pallas kernels for 12% -> 21%
where the time goes in v2:
time: 162 us; the launch traced here: 161 us
  starting transfers between devices  54.1 us (33%)
  waiting for transfers between devices  50.5 us (31%)
  Pallas kernels  34.2 us (21%)
  local copies, waits for them, and re-layouts  12.4 us (8%)
  other arithmetic  9.26 us (6%)
    ppermute x21, waiting for transfers between devices, fsdp_move(): return lax.ppermute(array, 'fsdp', perm)  42.1 us
    ppermute x21, starting transfers between devices, fsdp_move(): return lax.ppermute(array, 'fsdp', perm)  31.7 us
    pallas_call x6, Pallas kernels, blocks_dot(): pl.pallas_call(kernel, grid_spec=pltpu.PrefetchScalarGridSpec(num_scalar_...  27 us
    all_to_all x1, starting transfers between devices, shards(): recv = lax.all_to_all(inner.reshape(REP, part, columns), 'rep', 0, 0)  7.57 us
    all_to_all x1, starting transfers between devices, shards(): average = lax.all_to_all(copies, 'rep', 0, 0).reshape(rows, MAIN)  7.28 us
    unnamed x45, local copies, waits for them, and re-layouts  6.9 us
    all_to_all x1, starting transfers between devices, shards(): late = lax.all_to_all(slices, 'rep', 0, 0, axis_index_groups=SAME_YL)  5.99 us
    pallas_call x1, Pallas kernels, mix_early(): pl.pallas_call(kernel, grid_spec=pltpu.PrefetchScalarGridSpec(num_scalar_...  4.35 us
  transfers between devices with their start and end apart: 25, of which 11 were waited for; matrix products, arithmetic and copies ran while one was open for 8% of the time, Pallas kernels for 21%

profile of v2, /device:TPU:1, one launch (start us, length us, event | category | flops | bytes accessed | tf_op | source)
XLA Modules:
  0.0 161.4 jit_solution(13655003425260583636)
XLA Ops:
  0.6 3.3 %collective-permute-start.12 = (bf16[512,8192]{1,0:T(8,128)(2,1)}, bf16[512,8192]{1,0:T(8,128)(2,1)}, u32[]{:S(2)}, u32[]{:S(2)}) collective-permute-start(bf16[512,8192]{1,0:T(8,128)(2,1)} %bitcast.29), channel_id=1, source_target_pairs={{0,1},{1,0},{2,3},{3,2},{4,5},{5,4},{6,7},{7,6},{8,9},{9,8},{10,11... | collective-permute-start | bytes 25165832 | tf_op jit(solution)/shard_map/ppermute | solution.py:29
  4.0 7.6 %all-to-all-start = ((bf16[16,32,1024]{2,1,0:T(8,128)(2,1)}), bf16[16,32,1024]{2,1,0:T(8,128)(2,1)S(1)}, u32[]{:S(2)}, u32[]{:S(2)}) async-start(bf16[16,32,1024]{2,1,0:T(8,128)(2,1)} %bitcast.46), calls=%async_computation | async-start | bytes 2097152 | tf_op jit(solution)/shard_map/all_to_all | solution.py:222
  11.6 0.7 slice.20.refs_0_
  12.3 2.6 %collective-permute-start = (bf16[512,256]{1,0:T(8,128)(2,1)}, bf16[512,256]{1,0:T(8,128)(2,1)S(1)}, u32[]{:S(2)}, u32[]{:S(2)}) collective-permute-start(bf16[512,256]{1,0:T(8,128)(2,1)} %slice.20.refs_0_), channel_id=1, source_target_pairs={{0,8},{1,9},{2,10},{3,11},{4,12},{5,13},{6,14},{7,15},{8,0},{9,1},... | collective-permute-start | bytes 786440 | tf_op jit(solution)/shard_map/ppermute | solution.py:29
  14.9 1.2 collective-permute-start.1
  16.1 1.5 collective-permute-start.2
  17.6 1.5 collective-permute-start.3
  19.1 6.4 %collective-permute-done.refs_1_ = bf16[512,256]{1,0:T(8,128)(2,1)S(1)} collective-permute-done((bf16[512,256]{1,0:T(8,128)(2,1)}, bf16[512,256]{1,0:T(8,128)(2,1)S(1)}, u32[]{:S(2)}, u32[]{:S(2)}) %collective-permute-start) | collective-permute-done | bytes 262176 | tf_op jit(solution)/shard_map/ppermute | solution.py:29
  25.5 1.2 collective-permute-start.4
  26.7 1.5 collective-permute-start.5
  28.2 1.5 collective-permute-start.6
  29.7 1.4 constant_dynamic-slice_fusion.momentum_ref
  31.1 1.5 constant_dynamic-slice_fusion.1.refs_0_
  32.6 4.4 %collective-permute-done.4.refs_5_.refs_3_ = bf16[512,256]{1,0:T(8,128)(2,1)S(1)} collective-permute-done((bf16[512,256]{1,0:T(8,128)(2,1)S(1)}, bf16[512,256]{1,0:T(8,128)(2,1)S(1)}, u32[]{:S(2)}, u32[]{:S(2)}) %collective-permute-start.4) | collective-permute-done | bytes 262176 | tf_op jit(solution)/shard_map/ppermute | solution.py:29
  37.0 4.6 %collective-permute-done.6.refs_7_ = bf16[512,256]{1,0:T(8,128)(2,1)} collective-permute-done((bf16[512,256]{1,0:T(8,128)(2,1)S(1)}, bf16[512,256]{1,0:T(8,128)(2,1)}, u32[]{:S(2)}, u32[]{:S(2)}) %collective-permute-start.6) | collective-permute-done | bytes 262176 | tf_op jit(solution)/shard_map/ppermute | solution.py:29
  41.7 0.0 copy-start.9
  41.7 1.0 copy-done.9
  42.7 2.8 %average_slice.1 = (bf16[16,32,768]{2,1,0:T(8,128)(2,1)}, bf16[32,256]{1,0:T(8,128)(2,1)}, bf16[32,256]{1,0:T(8,128)(2,1)}) custom-call(bf16[16,32,1024]{2,1,0:T(8,128)(2,1)} %copy-done.9, bf16[32,1024]{1,0:T(8,128)(2,1)} %after.3.outer_ref, f32[32,256]{1,0:T(8,128)} %constant_dynamic-slice_fusion.momentum_ref), custom_call_target="tpu_custom_call" | custom-call | flops 5242880 | bytes 2097152 | tf_op jit(solution)/shard_map/average_slice/pallas_call | solution.py:82
  45.5 7.3 %all-to-all-start.1 = ((bf16[16,32,768]{2,1,0:T(8,128)(2,1)}), bf16[16,32,768]{2,1,0:T(8,128)(2,1)S(1)}, u32[]{:S(2)}, u32[]{:S(2)}) async-start(bf16[16,32,768]{2,1,0:T(8,128)(2,1)} %get-tuple-element.13), calls=%async_computation.1 | async-start | bytes 1572864 | tf_op jit(solution)/shard_map/all_to_all | solution.py:231
  52.8 1.3 collective-permute-start.7
  54.1 2.9 %collective-permute-done.7 = bf16[32,256]{1,0:T(8,128)(2,1)S(1)} collective-permute-done((bf16[32,256]{1,0:T(8,128)(2,1)S(1)}, bf16[32,256]{1,0:T(8,128)(2,1)S(1)}, u32[]{:S(2)}, u32[]{:S(2)}) %collective-permute-start.7) | collective-permute-done | bytes 16416 | tf_op jit(solution)/shard_map/ppermute | solution.py:29
  57.0 0.5 collective-permute-start.8
  57.5 2.1 %collective-permute-start.9 = (bf16[2,32,256]{2,1,0:T(8,128)(2,1)S(1)}, bf16[2,32,256]{2,1,0:T(8,128)(2,1)S(1)}, u32[]{:S(2)}, u32[]{:S(2)}) collective-permute-start(bf16[2,32,256]{2,1,0:T(8,128)(2,1)S(1)} %pad_maximum_fusion.3), channel_id=1, source_target_pairs={{0,6},{1,7},{2,0},{3,1},{4,2},{5,3},{6,4},{7,5},{8,14},{9,15},{10,... | collective-permute-start | bytes 98312 | tf_op jit(solution)/shard_map/ppermute | solution.py:29
  59.7 1.6 collective-permute-done.8
  61.3 3.0 %collective-permute-done.10 = bf16[2,32,256]{2,1,0:T(8,128)(2,1)S(1)} collective-permute-done((bf16[2,32,256]{2,1,0:T(8,128)(2,1)S(1)}, bf16[2,32,256]{2,1,0:T(8,128)(2,1)S(1)}, u32[]{:S(2)}, u32[]{:S(2)}) %collective-permute-start.10) | collective-permute-done | bytes 32800 | tf_op jit(solution)/shard_map/ppermute | solution.py:29
  64.2 1.6 collective-permute-start.11
  65.8 4.2 %collective-permute-done.11 = bf16[9,32,256]{2,1,0:T(8,128)(2,1)S(1)} collective-permute-done((bf16[9,32,256]{2,1,0:T(8,128)(2,1)S(1)}, bf16[9,32,256]{2,1,0:T(8,128)(2,1)S(1)}, u32[]{:S(2)}, u32[]{:S(2)}) %collective-permute-start.11) | collective-permute-done | bytes 147488 | tf_op jit(solution)/shard_map/ppermute | solution.py:33
  70.1 0.9 all-to-all-done.1
  71.0 1.8 %broadcast_in_dim.17 = bf16[8,2,9,32,256]{4,3,2,1,0:T(8,128)(2,1)} broadcast(bf16[2,9,32,256]{3,2,1,0:T(8,128)(2,1)S(1)} %pad_maximum_fusion.2), dimensions={1,2,3,4} | broadcast | bytes 2654208 | tf_op jit(solution)/shard_map/broadcast_in_dim | solution.py:239
  72.8 6.0 %all-to-all-start.2 = ((bf16[8,2,9,32,256]{4,3,2,1,0:T(8,128)(2,1)}), bf16[8,2,9,32,256]{4,3,2,1,0:T(8,128)(2,1)}, u32[]{:S(2)}, u32[]{:S(2)}) async-start(bf16[8,2,9,32,256]{4,3,2,1,0:T(8,128)(2,1)} %broadcast_in_dim.17), calls=%async_computation.2 | async-start | bytes 4718592 | tf_op jit(solution)/shard_map/all_to_all | solution.py:242
  78.8 3.6 %multiply_convert_fusion.1 = (bf16[512,768]{1,0:T(8,128)(2,1)S(1)}, bf16[512,768]{1,0:T(8,128)(2,1)}, f32[512,768]{1,0:T(8,128)}) fusion(bf16[512,1024]{1,0:T(8,128)(2,1)S(1)} %bitcast.48, f32[512,1024]{1,0:T(8,128)} %param.6, bf16[16,32,768]{2,1,0:T(8,128)(2,1)S(1)} %all-to-all-done.1, bf16[512,1024]{1,0:T(8,128)(2,1)} %param.4), kind=kLoop, calls=%fused_computation.7 | loop fusion | flops 5505024 | bytes 7077888 | tf_op jit(solution)/shard_map/convert_element_type | solution.py:97
  82.4 1.3 collective-permute-start.13
  83.7 2.7 %collective-permute-start.17 = (bf16[512,768]{1,0:T(8,128)(2,1)S(1)}, bf16[512,768]{1,0:T(8,128)(2,1)}, u32[]{:S(2)}, u32[]{:S(2)}) collective-permute-start(bf16[512,768]{1,0:T(8,128)(2,1)S(1)} %get-tuple-element.23.refs_8_), channel_id=1, source_target_pairs={{0,6},{1,7},{2,0},{3,1},{4,2},{5,3},{6,4},{7,5},{8,14},{9,15},{10,... | collective-permute-start | bytes 2359304 | tf_op jit(solution)/shard_map/ppermute | solution.py:29
  86.4 12.7 %collective-permute-done.13.refs_11_ = bf16[512,768]{1,0:T(8,128)(2,1)S(1)} collective-permute-done((bf16[512,768]{1,0:T(8,128)(2,1)S(1)}, bf16[512,768]{1,0:T(8,128)(2,1)S(1)}, u32[]{:S(2)}, u32[]{:S(2)}) %collective-permute-start.13) | collective-permute-done | bytes 786464 | tf_op jit(solution)/shard_map/ppermute | solution.py:29
  99.1 0.1 fusion.4.at_ref
  99.2 1.5 collective-permute-start.14
  100.6 0.1 collective-permute-start.18
  100.7 8.1 %blocks_dot.6 = (f32[512,768]{1,0:T(8,128)S(1)}, f32[512,768]{1,0:T(8,128)}) custom-call(s32[4]{0:T(128)S(1)} %fusion.4.at_ref, bf16[512,8192]{1,0:T(8,128)(2,1)} %collective-permute-done.12.refs_0_.refs_1_.refs_2_.refs_3_.refs_4_.refs_5_.refs_6_.refs_7_, ...), custom_call_target="tpu_custom_call" | custom-call | flops 3221225472 | bytes 10485760 | tf_op jit(solution)/shard_map/blocks_dot/pallas_call | solution.py:183
  108.8 1.1 copy-done.2
  110.0 6.5 %collective-permute-done.15.refs_0_ = bf16[512,768]{1,0:T(8,128)(2,1)S(1)} collective-permute-done((bf16[512,768]{1,0:T(8,128)(2,1)S(1)}, bf16[512,768]{1,0:T(8,128)(2,1)S(1)}, u32[]{:S(2)}, u32[]{:S(2)}) %collective-permute-start.15) | collective-permute-done | bytes 786464 | tf_op jit(solution)/shard_map/ppermute | solution.py:29
  116.5 0.9 copy-done.5
  117.4 3.5 %collective-permute-start.19 = (bf16[512,768]{1,0:T(8,128)(2,1)}, bf16[512,768]{1,0:T(8,128)(2,1)S(1)}, u32[]{:S(2)}, u32[]{:S(2)}) collective-permute-start(bf16[512,768]{1,0:T(8,128)(2,1)} %after.4.refs_5_), channel_id=1, source_target_pairs={{0,6},{1,7},{2,0},{3,1},{4,2},{5,3},{6,4},{7,5},{8,14},{9,15},{10,... | collective-permute-start | bytes 2359304 | tf_op jit(solution)/shard_map/ppermute | solution.py:29
  120.9 0.1 stack.91
  121.0 0.1 fusion.5.at_ref
  121.1 0.1 fusion.3.at_ref
  121.2 1.1 copy-done.6
  122.3 5.8 %blocks_dot.7 = (f32[512,768]{1,0:T(8,128)S(1)}, f32[512,768]{1,0:T(8,128)S(1)}) custom-call(s32[2]{0:T(128)S(1)} %fusion.3.at_ref, bf16[512,8192]{1,0:T(8,128)(2,1)} %collective-permute-done.12.refs_0_.refs_1_.refs_2_.refs_3_.refs_4_.refs_5_.refs_6_.refs_7_, ...), custom_call_target="tpu_custom_call" | custom-call | flops 1610612736 | bytes 6815744 | tf_op jit(solution)/shard_map/blocks_dot/pallas_call | solution.py:183
  128.1 1.1 copy-done.3
  129.3 3.3 %all-to-all-done.2.refs_0_ = bf16[8,2,9,32,256]{4,3,2,1,0:T(8,128)(2,1)} async-done(((bf16[8,2,9,32,256]{4,3,2,1,0:T(8,128)(2,1)}), bf16[8,2,9,32,256]{4,3,2,1,0:T(8,128)(2,1)}, u32[]{:S(2)}, u32[]{:S(2)}) %all-to-all-start.2) | async-done | bytes 2359328 | tf_op jit(solution)/shard_map/all_to_all | solution.py:242
  132.6 4.3 %mix_early.1 = (bf16[8,512,256]{2,1,0:T(8,128)(2,1)}, bf16[512,256]{1,0:T(8,128)(2,1)}, bf16[512,256]{1,0:T(8,128)(2,1)}) custom-call(s32[1]{0:T(128)} %bitcast.4.yl_ref, bf16[512,256]{1,0:T(8,128)(2,1)} %slice.20.refs_0_, bf16[512,256]{1,0:T(8,128)(2,1)} %copy-done.11, bf16[512,256]{1,0:T(8,128)(2,1)} %copy-done.12, bf16[512,256]{1,0:T(8,128)(2,1)} %copy-done.15, ...), custom_call_target="tpu_custom_call" | custom-call | flops 3145728 | bytes 6291456 | tf_op jit(solution)/shard_map/mix_early/pallas_call | solution.py:122
  136.9 0.0 copy-start
  136.9 1.6 copy-done
  138.5 3.7 %blocks_dot.11 = bf16[512,256]{1,0:T(8,128)(2,1)S(1)} custom-call(s32[8]{0:T(128)S(1)} %multiply_add_fusion.at_ref, bf16[512,8192]{1,0:T(8,128)(2,1)} %collective-permute-done.12.refs_0_.refs_1_.refs_2_.refs_3_.refs_4_.refs_5_.refs_6_.refs_7_, bf16[512,8192]{1,0:T(8,128)(2,1)} %collective-permute-done.12.refs_0_.refs_1_.refs_2_.refs_3_.refs_4_.refs_5_.refs_6_.refs_7_, ...), custom_call_target="tpu_custom_call" | custom-call | flops 1073741824 | bytes 6815744 | tf_op jit(solution)/shard_map/blocks_dot/pallas_call | solution.py:183
  142.3 4.2 %collective-permute-start.21 = (bf16[512,256]{1,0:T(8,128)(2,1)S(1)}, bf16[512,256]{1,0:T(8,128)(2,1)S(1)}, u32[]{:S(2)}, u32[]{:S(2)}) collective-permute-start(bf16[512,256]{1,0:T(8,128)(2,1)S(1)} %blocks_dot.11), channel_id=1, source_target_pairs={{0,1},{1,0},{2,3},{3,2},{4,5},{5,4},{6,7},{7,6},{8,9},{9,8},{10,11... | collective-permute-start | bytes 786440 | tf_op jit(solution)/shard_map/ppermute | solution.py:29
  146.4 2.8 %blocks_dot.9 = bf16[512,768]{1,0:T(8,128)(2,1)S(1)} custom-call(s32[2]{0:T(128)S(1)} %fusion.5.at_ref, bf16[512,8192]{1,0:T(8,128)(2,1)} %collective-permute-done.12.refs_0_.refs_1_.refs_2_.refs_3_.refs_4_.refs_5_.refs_6_.refs_7_, bf16[512,8192]{1,0:T(8,128)(2,1)} %collective-permute-done.12.refs_0_.refs_1_.refs_2_.refs_3_.refs_4_.refs_5_.refs_6_.refs_7_, ...), custom_call_target="tpu_custom_call" | custom-call | flops 805306368 | bytes 4194304 | tf_op jit(solution)/shard_map/blocks_dot/pallas_call | solution.py:183
  149.3 0.1 collective-permute-start.20
  149.4 1.3 convert_add_fusion.2
  150.7 1.1 pad_maximum_fusion.1
  151.8 3.7 %blocks_dot.10 = f32[512,256]{1,0:T(8,128)S(1)} custom-call(s32[8]{0:T(128)S(1)} %multiply_add_fusion.at_ref, bf16[512,8192]{1,0:T(8,128)(2,1)} %bitcast.36, bf16[512,8192]{1,0:T(8,128)(2,1)} %bitcast.37, bf16[512,8192]{1,0:T(8,128)(2,1)} %bitcast.38, bf16[512,8192]{1,0:T(8,128)(2,1)} %bitcast.39, bf16[512,8192]{1,0:T(8,128)(2,1)} %bitcast.40, ...), custom_call_target="tpu_custom_call" | custom-call | flops 1073741824 | bytes 6815744 | tf_op jit(solution)/shard_map/blocks_dot/pallas_call | solution.py:183
  155.5 1.6 pad_maximum_fusion
  157.1 0.1 multiply_convert_fusion.2
  157.2 2.8 %blocks_dot.8 = f32[512,768]{1,0:T(8,128)S(1)} custom-call(s32[2]{0:T(128)S(1)} %fusion.5.at_ref, bf16[512,8192]{1,0:T(8,128)(2,1)} %bitcast.44, bf16[512,8192]{1,0:T(8,128)(2,1)} %bitcast.45, bf16[512,768]{1,0:T(8,128)(2,1)S(1)} %collective-permute-done.18.refs_2_, bf16[512,768]{1,0:T(8,128)(2,1)S(1)} %collective-permute-done.19.refs_3_, ...), custom_call_target="tpu_custom_call" | custom-call | flops 805306368 | bytes 4194304 | tf_op jit(solution)/shard_map/blocks_dot/pallas_call | solution.py:183
  160.0 0.2 multiply_convert_fusion
  160.2 1.1 maximum_bitcast_fusion
  (61 shorter events, 0.2 us)
Async XLA Ops:
  0.6 10.9 %copy-start.8 = (bf16[1,512,1024]{2,1,0:T(8,128)(2,1)S(1)}, bf16[1,512,1024]{2,1,0:T(8,128)(2,1)}, u32[]{:S(2)}) copy-start(bf16[1,512,1024]{2,1,0:T(8,128)(2,1)} %param.5) | copy-start | bytes 3145732
  0.6 100.1 %collective-permute-start.12 = (bf16[512,8192]{1,0:T(8,128)(2,1)}, bf16[512,8192]{1,0:T(8,128)(2,1)}, u32[]{:S(2)}, u32[]{:S(2)}) collective-permute-start(bf16[512,8192]{1,0:T(8,128)(2,1)} %bitcast.29), channel_id=1, source_target_pairs={{0,1},{1,0},{2,3},{3,2},{4,5},{5,4},{6,7},{7,6},{8,9},{9,8},{10,11... | collective-permute-start | bytes 25165832 | tf_op jit(solution)/shard_map/ppermute | solution.py:29
  4.0 37.7 %all-to-all-start = ((bf16[16,32,1024]{2,1,0:T(8,128)(2,1)}), bf16[16,32,1024]{2,1,0:T(8,128)(2,1)S(1)}, u32[]{:S(2)}, u32[]{:S(2)}) async-start(bf16[16,32,1024]{2,1,0:T(8,128)(2,1)} %bitcast.46), calls=%async_computation | async-start | bytes 2097152 | tf_op jit(solution)/shard_map/all_to_all | solution.py:222
  12.3 13.2 %collective-permute-start = (bf16[512,256]{1,0:T(8,128)(2,1)}, bf16[512,256]{1,0:T(8,128)(2,1)S(1)}, u32[]{:S(2)}, u32[]{:S(2)}) collective-permute-start(bf16[512,256]{1,0:T(8,128)(2,1)} %slice.20.refs_0_), channel_id=1, source_target_pairs={{0,8},{1,9},{2,10},{3,11},{4,12},{5,13},{6,14},{7,15},{8,0},{9,1},... | collective-permute-start | bytes 786440 | tf_op jit(solution)/shard_map/ppermute | solution.py:29
  14.9 11.8 %collective-permute-start.1 = (bf16[512,256]{1,0:T(8,128)(2,1)}, bf16[512,256]{1,0:T(8,128)(2,1)S(1)}, u32[]{:S(2)}, u32[]{:S(2)}) collective-permute-start(bf16[512,256]{1,0:T(8,128)(2,1)} %slice.20.refs_0_), channel_id=1, source_target_pairs={{0,2},{1,3},{2,4},{3,5},{4,6},{5,7},{6,0},{7,1},{8,10},{9,11},{10,... | collective-permute-start | bytes 786440 | tf_op jit(solution)/shard_map/ppermute | solution.py:29
  16.1 12.1 %collective-permute-start.2 = (bf16[512,256]{1,0:T(8,128)(2,1)}, bf16[512,256]{1,0:T(8,128)(2,1)S(1)}, u32[]{:S(2)}, u32[]{:S(2)}) collective-permute-start(bf16[512,256]{1,0:T(8,128)(2,1)} %slice.20.refs_0_), channel_id=1, source_target_pairs={{0,6},{1,7},{2,0},{3,1},{4,2},{5,3},{6,4},{7,5},{8,14},{9,15},{10,... | collective-permute-start | bytes 786440 | tf_op jit(solution)/shard_map/ppermute | solution.py:29
  17.6 15.0 %collective-permute-start.3 = (bf16[512,256]{1,0:T(8,128)(2,1)}, bf16[512,256]{1,0:T(8,128)(2,1)S(1)}, u32[]{:S(2)}, u32[]{:S(2)}) collective-permute-start(bf16[512,256]{1,0:T(8,128)(2,1)} %slice.20.refs_0_), channel_id=1, source_target_pairs={{0,4},{1,5},{2,6},{3,7},{4,0},{5,1},{6,2},{7,3},{8,12},{9,13},{10,... | collective-permute-start | bytes 786440 | tf_op jit(solution)/shard_map/ppermute | solution.py:29
  25.5 16.1 %copy-start.11 = (bf16[512,256]{1,0:T(8,128)(2,1)}, bf16[512,256]{1,0:T(8,128)(2,1)S(1)}, u32[]{:S(2)}) copy-start(bf16[512,256]{1,0:T(8,128)(2,1)S(1)} %collective-permute-done.refs_1_) | copy-start | bytes 786436
  25.5 11.5 %collective-permute-start.4 = (bf16[512,256]{1,0:T(8,128)(2,1)S(1)}, bf16[512,256]{1,0:T(8,128)(2,1)S(1)}, u32[]{:S(2)}, u32[]{:S(2)}) collective-permute-start(bf16[512,256]{1,0:T(8,128)(2,1)S(1)} %collective-permute-done.refs_1_), channel_id=1, source_target_pairs={{0,2},{1,3},{2,4},{3,5},{4,6},{5,7},{6,0},{7,1},{8,10},{9,11},{10,... | collective-permute-start | bytes 786440 | tf_op jit(solution)/shard_map/ppermute | solution.py:29
  26.7 14.9 %copy-start.12 = (bf16[512,256]{1,0:T(8,128)(2,1)}, bf16[512,256]{1,0:T(8,128)(2,1)S(1)}, u32[]{:S(2)}) copy-start(bf16[512,256]{1,0:T(8,128)(2,1)S(1)} %collective-permute-done.1.refs_2_) | copy-start | bytes 786436
  26.7 10.3 %collective-permute-start.5 = (bf16[512,256]{1,0:T(8,128)(2,1)S(1)}, bf16[512,256]{1,0:T(8,128)(2,1)}, u32[]{:S(2)}, u32[]{:S(2)}) collective-permute-start(bf16[512,256]{1,0:T(8,128)(2,1)S(1)} %collective-permute-done.refs_1_), channel_id=1, source_target_pairs={{0,6},{1,7},{2,0},{3,1},{4,2},{5,3},{6,4},{7,5},{8,14},{9,15},{10,... | collective-permute-start | bytes 786440 | tf_op jit(solution)/shard_map/ppermute | solution.py:29
  28.2 13.4 %copy-start.13 = (bf16[512,256]{1,0:T(8,128)(2,1)}, bf16[512,256]{1,0:T(8,128)(2,1)S(1)}, u32[]{:S(2)}) copy-start(bf16[512,256]{1,0:T(8,128)(2,1)S(1)} %collective-permute-done.2.refs_3_.refs_4_) | copy-start | bytes 786436
  28.2 13.4 %collective-permute-start.6 = (bf16[512,256]{1,0:T(8,128)(2,1)S(1)}, bf16[512,256]{1,0:T(8,128)(2,1)}, u32[]{:S(2)}, u32[]{:S(2)}) collective-permute-start(bf16[512,256]{1,0:T(8,128)(2,1)S(1)} %collective-permute-done.refs_1_), channel_id=1, source_target_pairs={{0,4},{1,5},{2,6},{3,7},{4,0},{5,1},{6,2},{7,3},{8,12},{9,13},{10,... | collective-permute-start | bytes 786440 | tf_op jit(solution)/shard_map/ppermute | solution.py:29
  32.6 9.1 %copy-start.14 = (bf16[512,256]{1,0:T(8,128)(2,1)}, bf16[512,256]{1,0:T(8,128)(2,1)S(1)}, u32[]{:S(2)}) copy-start(bf16[512,256]{1,0:T(8,128)(2,1)S(1)} %collective-permute-done.3.refs_4_.refs_6_) | copy-start | bytes 786436
  37.0 4.6 %copy-start.15 = (bf16[512,256]{1,0:T(8,128)(2,1)}, bf16[512,256]{1,0:T(8,128)(2,1)S(1)}, u32[]{:S(2)}) copy-start(bf16[512,256]{1,0:T(8,128)(2,1)S(1)} %collective-permute-done.4.refs_5_.refs_3_) | copy-start | bytes 786436
  41.7 1.0 copy-start.9
  45.5 7.3 %copy-start.18 = (bf16[32,256]{1,0:T(8,128)(2,1)S(1)}, bf16[32,256]{1,0:T(8,128)(2,1)}, u32[]{:S(2)}) copy-start(bf16[32,256]{1,0:T(8,128)(2,1)} %get-tuple-element.14) | copy-start | bytes 49156
  45.5 18.7 %copy-start.19 = (bf16[32,256]{1,0:T(8,128)(2,1)S(1)}, bf16[32,256]{1,0:T(8,128)(2,1)}, u32[]{:S(2)}) copy-start(bf16[32,256]{1,0:T(8,128)(2,1)} %get-tuple-element.15) | copy-start | bytes 49156
  45.5 25.5 %all-to-all-start.1 = ((bf16[16,32,768]{2,1,0:T(8,128)(2,1)}), bf16[16,32,768]{2,1,0:T(8,128)(2,1)S(1)}, u32[]{:S(2)}, u32[]{:S(2)}) async-start(bf16[16,32,768]{2,1,0:T(8,128)(2,1)} %get-tuple-element.13), calls=%async_computation.1 | async-start | bytes 1572864 | tf_op jit(solution)/shard_map/all_to_all | solution.py:231
  52.8 4.2 %collective-permute-start.7 = (bf16[32,256]{1,0:T(8,128)(2,1)S(1)}, bf16[32,256]{1,0:T(8,128)(2,1)S(1)}, u32[]{:S(2)}, u32[]{:S(2)}) collective-permute-start(bf16[32,256]{1,0:T(8,128)(2,1)S(1)} %copy-done.18), channel_id=1, source_target_pairs={{0,8},{1,9},{2,10},{3,11},{4,12},{5,13},{6,14},{7,15},{8,0},{9,1},... | collective-permute-start | bytes 49160 | tf_op jit(solution)/shard_map/ppermute | solution.py:29
  57.0 4.3 %collective-permute-start.8 = (bf16[2,32,256]{2,1,0:T(8,128)(2,1)S(1)}, bf16[2,32,256]{2,1,0:T(8,128)(2,1)S(1)}, u32[]{:S(2)}, u32[]{:S(2)}) collective-permute-start(bf16[2,32,256]{2,1,0:T(8,128)(2,1)S(1)} %pad_maximum_fusion.3), channel_id=1, source_target_pairs={{0,2},{1,3},{2,4},{3,5},{4,6},{5,7},{6,0},{7,1},{8,10},{9,11},{10,... | collective-permute-start | bytes 98312 | tf_op jit(solution)/shard_map/ppermute | solution.py:29
  57.5 3.7 %collective-permute-start.9 = (bf16[2,32,256]{2,1,0:T(8,128)(2,1)S(1)}, bf16[2,32,256]{2,1,0:T(8,128)(2,1)S(1)}, u32[]{:S(2)}, u32[]{:S(2)}) collective-permute-start(bf16[2,32,256]{2,1,0:T(8,128)(2,1)S(1)} %pad_maximum_fusion.3), channel_id=1, source_target_pairs={{0,6},{1,7},{2,0},{3,1},{4,2},{5,3},{6,4},{7,5},{8,14},{9,15},{10,... | collective-permute-start | bytes 98312 | tf_op jit(solution)/shard_map/ppermute | solution.py:29
  59.7 4.6 %collective-permute-start.10 = (bf16[2,32,256]{2,1,0:T(8,128)(2,1)S(1)}, bf16[2,32,256]{2,1,0:T(8,128)(2,1)S(1)}, u32[]{:S(2)}, u32[]{:S(2)}) collective-permute-start(bf16[2,32,256]{2,1,0:T(8,128)(2,1)S(1)} %pad_maximum_fusion.3), channel_id=1, source_target_pairs={{0,4},{1,5},{2,6},{3,7},{4,0},{5,1},{6,2},{7,3},{8,12},{9,13},{10,... | collective-permute-start | bytes 98312 | tf_op jit(solution)/shard_map/ppermute | solution.py:29
  64.2 5.8 %collective-permute-start.11 = (bf16[9,32,256]{2,1,0:T(8,128)(2,1)S(1)}, bf16[9,32,256]{2,1,0:T(8,128)(2,1)S(1)}, u32[]{:S(2)}, u32[]{:S(2)}) collective-permute-start(bf16[9,32,256]{2,1,0:T(8,128)(2,1)S(1)} %bitcast_dynamic-update-slice_fusion), channel_id=1, source_target_pairs={{0,128},{16,144},{32,160},{48,176},{64,192},{80,208},{96,224},{112... | collective-permute-start | bytes 442376 | tf_op jit(solution)/shard_map/ppermute | solution.py:33
  72.8 59.8 %all-to-all-start.2 = ((bf16[8,2,9,32,256]{4,3,2,1,0:T(8,128)(2,1)}), bf16[8,2,9,32,256]{4,3,2,1,0:T(8,128)(2,1)}, u32[]{:S(2)}, u32[]{:S(2)}) async-start(bf16[8,2,9,32,256]{4,3,2,1,0:T(8,128)(2,1)} %broadcast_in_dim.17), calls=%async_computation.2 | async-start | bytes 4718592 | tf_op jit(solution)/shard_map/all_to_all | solution.py:242
  82.4 16.7 %collective-permute-start.13 = (bf16[512,768]{1,0:T(8,128)(2,1)S(1)}, bf16[512,768]{1,0:T(8,128)(2,1)S(1)}, u32[]{:S(2)}, u32[]{:S(2)}) collective-permute-start(bf16[512,768]{1,0:T(8,128)(2,1)S(1)} %get-tuple-element.23.refs_8_), channel_id=1, source_target_pairs={{0,8},{1,9},{2,10},{3,11},{4,12},{5,13},{6,14},{7,15},{8,0},{9,1},... | collective-permute-start | bytes 2359304 | tf_op jit(solution)/shard_map/ppermute | solution.py:29
  83.7 17.0 %collective-permute-start.16 = (bf16[512,768]{1,0:T(8,128)(2,1)S(1)}, bf16[512,768]{1,0:T(8,128)(2,1)}, u32[]{:S(2)}, u32[]{:S(2)}) collective-permute-start(bf16[512,768]{1,0:T(8,128)(2,1)S(1)} %get-tuple-element.23.refs_8_), channel_id=1, source_target_pairs={{0,2},{1,3},{2,4},{3,5},{4,6},{5,7},{6,0},{7,1},{8,10},{9,11},{10,... | collective-permute-start | bytes 2359304 | tf_op jit(solution)/shard_map/ppermute | solution.py:29
  83.7 17.1 %collective-permute-start.17 = (bf16[512,768]{1,0:T(8,128)(2,1)S(1)}, bf16[512,768]{1,0:T(8,128)(2,1)}, u32[]{:S(2)}, u32[]{:S(2)}) collective-permute-start(bf16[512,768]{1,0:T(8,128)(2,1)S(1)} %get-tuple-element.23.refs_8_), channel_id=1, source_target_pairs={{0,6},{1,7},{2,0},{3,1},{4,2},{5,3},{6,4},{7,5},{8,14},{9,15},{10,... | collective-permute-start | bytes 2359304 | tf_op jit(solution)/shard_map/ppermute | solution.py:29
  99.1 17.4 %collective-permute-start.15 = (bf16[512,768]{1,0:T(8,128)(2,1)S(1)}, bf16[512,768]{1,0:T(8,128)(2,1)S(1)}, u32[]{:S(2)}, u32[]{:S(2)}) collective-permute-start(bf16[512,768]{1,0:T(8,128)(2,1)S(1)} %collective-permute-done.13.refs_11_), channel_id=1, source_target_pairs={{0,6},{1,7},{2,0},{3,1},{4,2},{5,3},{6,4},{7,5},{8,14},{9,15},{10,... | collective-permute-start | bytes 2359304 | tf_op jit(solution)/shard_map/ppermute | solution.py:29
  99.2 22.0 %collective-permute-start.14 = (bf16[512,768]{1,0:T(8,128)(2,1)S(1)}, bf16[512,768]{1,0:T(8,128)(2,1)}, u32[]{:S(2)}, u32[]{:S(2)}) collective-permute-start(bf16[512,768]{1,0:T(8,128)(2,1)S(1)} %collective-permute-done.13.refs_11_), channel_id=1, source_target_pairs={{0,2},{1,3},{2,4},{3,5},{4,6},{5,7},{6,0},{7,1},{8,10},{9,11},{10,... | collective-permute-start | bytes 2359304 | tf_op jit(solution)/shard_map/ppermute | solution.py:29
  100.6 45.8 %collective-permute-start.18 = (bf16[512,768]{1,0:T(8,128)(2,1)}, bf16[512,768]{1,0:T(8,128)(2,1)S(1)}, u32[]{:S(2)}, u32[]{:S(2)}) collective-permute-start(bf16[512,768]{1,0:T(8,128)(2,1)} %collective-permute-done.16.refs_9_), channel_id=1, source_target_pairs={{0,2},{1,3},{2,4},{3,5},{4,6},{5,7},{6,0},{7,1},{8,10},{9,11},{10,... | collective-permute-start | bytes 2359304 | tf_op jit(solution)/shard_map/ppermute | solution.py:29
  108.8 1.1 copy-start.2
  116.5 0.9 copy-start.5
  117.4 29.1 %collective-permute-start.19 = (bf16[512,768]{1,0:T(8,128)(2,1)}, bf16[512,768]{1,0:T(8,128)(2,1)S(1)}, u32[]{:S(2)}, u32[]{:S(2)}) collective-permute-start(bf16[512,768]{1,0:T(8,128)(2,1)} %after.4.refs_5_), channel_id=1, source_target_pairs={{0,6},{1,7},{2,0},{3,1},{4,2},{5,3},{6,4},{7,5},{8,14},{9,15},{10,... | collective-permute-start | bytes 2359304 | tf_op jit(solution)/shard_map/ppermute | solution.py:29
  121.1 1.1 copy-start.6
  128.1 1.1 copy-start.3
  136.9 1.6 copy-start
  138.5 7.9 %copy-start.4 = (f32[512,768]{1,0:T(8,128)S(1)}, f32[512,768]{1,0:T(8,128)}, u32[]{:S(2)}) copy-start(f32[512,768]{1,0:T(8,128)} %copy-done.3) | copy-start | bytes 4718596
  142.2 7.1 %copy-start.16 = (bf16[512,256]{1,0:T(8,128)(2,1)S(1)}, bf16[512,256]{1,0:T(8,128)(2,1)}, u32[]{:S(2)}) copy-start(bf16[512,256]{1,0:T(8,128)(2,1)} %get-tuple-element.20) | copy-start | bytes 786436
  142.3 8.4 %copy-start.17 = (bf16[512,256]{1,0:T(8,128)(2,1)S(1)}, bf16[512,256]{1,0:T(8,128)(2,1)}, u32[]{:S(2)}) copy-start(bf16[512,256]{1,0:T(8,128)(2,1)} %get-tuple-element.19) | copy-start | bytes 786436
  142.3 14.8 %collective-permute-start.21 = (bf16[512,256]{1,0:T(8,128)(2,1)S(1)}, bf16[512,256]{1,0:T(8,128)(2,1)S(1)}, u32[]{:S(2)}, u32[]{:S(2)}) collective-permute-start(bf16[512,256]{1,0:T(8,128)(2,1)S(1)} %blocks_dot.11), channel_id=1, source_target_pairs={{0,1},{1,0},{2,3},{3,2},{4,5},{5,4},{6,7},{7,6},{8,9},{9,8},{10,11... | collective-permute-start | bytes 786440 | tf_op jit(solution)/shard_map/ppermute | solution.py:29
  149.3 1.4 copy-start.10
  149.3 10.8 %collective-permute-start.20 = (bf16[512,768]{1,0:T(8,128)(2,1)S(1)}, bf16[512,768]{1,0:T(8,128)(2,1)S(1)}, u32[]{:S(2)}, u32[]{:S(2)}) collective-permute-start(bf16[512,768]{1,0:T(8,128)(2,1)S(1)} %blocks_dot.9), channel_id=1, source_target_pairs={{0,1},{1,0},{2,3},{3,2},{4,5},{5,4},{6,7},{7,6},{8,9},{9,8},{10,11... | collective-permute-start | bytes 2359304 | tf_op jit(solution)/shard_map/ppermute | solution.py:29
  149.4 2.4 %copy-start.1 = (bf16[8,512,256]{2,1,0:T(8,128)(2,1)S(1)}, bf16[8,512,256]{2,1,0:T(8,128)(2,1)}, u32[]{:S(2)}) copy-start(bf16[8,512,256]{2,1,0:T(8,128)(2,1)} %get-tuple-element.22.refs_8_) | copy-start | bytes 6291460
  151.8 3.7 %copy-start.7 = (f32[512,768]{1,0:T(8,128)S(1)}, f32[512,768]{1,0:T(8,128)}, u32[]{:S(2)}) copy-start(f32[512,768]{1,0:T(8,128)} %get-tuple-element.25) | copy-start | bytes 4718596

commit v3 on v2

--- a/solution.py
+++ b/solution.py
@@ -97,51 +97,84 @@
     return (0.5 * one.astype(F32) + 0.5 * other.astype(F32)).astype(BF16)
 
 
-def mix_early(inners, late, yl):
+def early_dot(lefts, blocks, inners, late, yl):
     count, (rows, wide) = len(inners), inners[0].shape
-    half = rows // YL
-
-    def kernel(yl_ref, *refs):
-        mixed_ref, outer_ref, average_ref = refs[-3:]
-        lates = refs[count:-3]
-        for h in range(YL):
-            at = slice(h * half, h * half + half)
-            outers = [r[...].reshape(half, wide) for r in lates[h * (count + 1) : (h + 1) * (count + 1)]]
-            for k in range(count):
-                mixed_ref[k, at] = mix(refs[k][at], outers[k])
-            outer_ref[at] = outers[0]
-            average_ref[at] = outers[count]
+    half, tile, sides = rows // YL, 256, len(lefts)
+    steps = rows // tile
+    lates = YL * (count + 1)
+
+    def kernel(place_ref, *refs):
+        tokens, refs = refs[: sides * count], refs[sides * count :]
+        outer_ref, average_ref, mixed_ref = refs[-3:]
+        outs = refs[-3 - sides : -3]
+        step = pl.program_id(0)
+
+        @pl.when(step == 0)
+        def _():
+            for h in range(YL):
+                at = slice(h * half, h * half + half)
+                outers = [r[...].reshape(half, wide) for r in refs[count + h * (count + 1) :][: count + 1]]
+                for k in range(count):
+                    mixed_ref[k, at] = mix(refs[k][at], outers[k])
+                outer_ref[at] = outers[0]
+                average_ref[at] = outers[count]
+
+        for side in range(sides):
+
+            @pl.when(step // steps == side)
+            def _(side=side):
+                total = jnp.zeros((tile, wide), F32)
+                for k in range(count):
+                    total = total + jnp.dot(
+                        tokens[side * count + k][...], mixed_ref[k], preferred_element_type=F32
+                    )
+                outs[side][...] = total.astype(outs[side].dtype)
+
+    def row(side, i):
+        return jnp.clip(i - side * steps, 0, steps - 1)
+
+    def left_spec(side, k):
+        return pl.BlockSpec((tile, rows), lambda i, place: (row(side, i), place[1 + k]))
 
     def late_spec(h, k):
-        return pl.BlockSpec((Z, None, None, rows // REP, wide), lambda i, yl: (0, (yl[0] + h) % YL, k, 0, 0))
+        return pl.BlockSpec((Z, None, None, rows // REP, wide), lambda i, place: (0, (place[0] + h) % YL, k, 0, 0))
 
     def whole(*shape):
-        return pl.BlockSpec(shape, lambda i, yl: (0,) * len(shape))
-
-    lates = [late_spec(h, k) for h in range(YL) for k in range(count + 1)]
+        return pl.BlockSpec(shape, lambda i, place: (0,) * len(shape))
+
+    def row_spec(side):
+        return pl.BlockSpec((tile, wide), lambda i, place: (row(side, i), 0))
+
     return pl.pallas_call(
         kernel,
         grid_spec=pltpu.PrefetchScalarGridSpec(
             num_scalar_prefetch=1,
-            grid=(1,),
-            in_specs=[whole(rows, wide)] * count + lates,
-            out_specs=[whole(count, rows, wide), whole(rows, wide), whole(rows, wide)],
+            grid=(sides * steps,),
+            in_specs=[left_spec(side, k) for side in range(sides) for k in range(count)]
+            + [whole(rows, wide)] * count
+            + [late_spec(h, k) for h in range(YL) for k in range(count + 1)],
+            out_specs=[row_spec(side) for side in range(sides)] + [whole(rows, wide)] * 2,
+            scratch_shapes=[pltpu.VMEM((count, rows, wide), BF16)],
         ),
-        out_shape=[
-            jax.ShapeDtypeStruct((count, rows, wide), BF16),
-            jax.ShapeDtypeStruct((rows, wide), BF16),
-            jax.ShapeDtypeStruct((rows, wide), BF16),
-        ],
+        out_shape=[jax.ShapeDtypeStruct((rows, wide), dtype) for dtype in (BF16, F32)]
+        + [jax.ShapeDtypeStruct((rows, wide), BF16)] * 2,
         compiler_params=pltpu.CompilerParams(vmem_limit_bytes=60 * MIB),
         cost_estimate=pl.CostEstimate(
-            flops=3 * count * rows * wide, bytes_accessed=6 * count * rows * wide, transcendentals=0
+            flops=2 * sides * rows * rows * count * wide,
+            bytes_accessed=2 * rows * count * (sides * rows + 3 * wide),
+            transcendentals=0,
         ),
-        name="mix_early",
-    )(yl[None], *inners, *([late] * len(lates)))
+        name="early_dot",
+    )(
+        jnp.concatenate([yl[None], blocks]),
+        *[left for left in lefts for _ in range(count)],
+        *inners,
+        *([late] * lates),
+    )
 
 
 def blocks_dot(lefts, blocks, pieces, start=None, out=F32):
-    rows, tile = lefts[0].shape[0], 256
+    rows, tile = lefts[0].shape[0], 256 * len(lefts)
     steps = rows // tile
     count, sides = len(pieces), len(lefts)
     arrays = []
@@ -253,10 +286,10 @@
     there_across = fsdp_move(there_right, dx=-1)
     sums = dot(SIDES, [(there_left,), (there_right,)], sums)
 
-    mixed_early, outer_early, average_early = mix_early(inners, after(late, sums[0]), yl)
-    pieces = [(mixed_early, k) for k in range(CHIPS)]
-    theirs_early = fsdp_move(dot(ORDER, pieces, lefts=both[:1], out=BF16)[0], dc=1)
-    ours_early = dot(ORDER, pieces, lefts=both[1:])[0]
+    theirs_early, ours_early, outer_early, average_early = early_dot(
+        both, CORE * chips_of(ORDER) + core, inners, after(late, sums[0]), yl
+    )
+    theirs_early = fsdp_move(theirs_early, dc=1)
     momentum_early = 0.9 * momentum[:, early] + average_early.astype(F32)
     outer_next = jnp.concatenate([outer_main, outer_early], axis=1)
     momentum_next = jnp.concatenate([momentum_main, momentum_early], axis=1)

time: 162 us -> 161 us (level)
    pallas_call x6 -> x4, Pallas kernels: 27 us -> 19 us  [blocks_dot(): pl.pallas_call(kernel, grid_spec=pltpu.PrefetchScalarGridSpec(num_scalar_...]
    pallas_call x1, Pallas kernels: 4.35 us -> 11.2 us  [early_dot(): pl.pallas_call(kernel, grid_spec=pltpu.PrefetchScalarGridSpec(num_scalar_...]
    unnamed x45 -> x47, local copies, waits for them, and re-layouts: 6.9 us -> 7.13 us
  transfers between devices with their start and end apart: 25 -> 25, of which waited for: 11 -> 11; matrix products, arithmetic and copies ran while one was open for 8% -> 9% of each run, Pallas kernels for 21% -> 21%
where the time goes in v3:
time: 161 us; the launch traced here: 160 us
  starting transfers between devices  53.8 us (33%)
  waiting for transfers between devices  49.5 us (31%)
  Pallas kernels  33 us (20%)
  local copies, waits for them, and re-layouts  12.6 us (8%)
  other arithmetic  9.91 us (6%)
    ppermute x21, waiting for transfers between devices, fsdp_move(): return lax.ppermute(array, 'fsdp', perm)  42.1 us
    ppermute x21, starting transfers between devices, fsdp_move(): return lax.ppermute(array, 'fsdp', perm)  31.4 us
    pallas_call x4, Pallas kernels, blocks_dot(): pl.pallas_call(kernel, grid_spec=pltpu.PrefetchScalarGridSpec(num_scalar_...  19 us
    pallas_call x1, Pallas kernels, early_dot(): pl.pallas_call(kernel, grid_spec=pltpu.PrefetchScalarGridSpec(num_scalar_...  11.2 us
    all_to_all x1, starting transfers between devices, shards(): recv = lax.all_to_all(inner.reshape(REP, part, columns), 'rep', 0, 0)  7.57 us
    all_to_all x1, starting transfers between devices, shards(): average = lax.all_to_all(copies, 'rep', 0, 0).reshape(rows, MAIN)  7.31 us
    unnamed x47, local copies, waits for them, and re-layouts  7.13 us
    all_to_all x1, starting transfers between devices, shards(): late = lax.all_to_all(slices, 'rep', 0, 0, axis_index_groups=SAME_YL)  6 us
  transfers between devices with their start and end apart: 25, of which 11 were waited for; matrix products, arithmetic and copies ran while one was open for 9% of the time, Pallas kernels for 21%

profile of v3, /device:TPU:1, one launch (start us, length us, event | category | flops | bytes accessed | tf_op | source)
XLA Modules:
  0.0 159.8 jit_solution(3320332487847220162)
XLA Ops:
  0.6 3.3 %collective-permute-start.7 = (bf16[512,8192]{1,0:T(8,128)(2,1)}, bf16[512,8192]{1,0:T(8,128)(2,1)}, u32[]{:S(2)}, u32[]{:S(2)}) collective-permute-start(bf16[512,8192]{1,0:T(8,128)(2,1)} %bitcast.29), channel_id=1, source_target_pairs={{0,1},{1,0},{2,3},{3,2},{4,5},{5,4},{6,7},{7,6},{8,9},{9,8},{10,11... | collective-permute-start | bytes 25165832 | tf_op jit(solution)/shard_map/ppermute | solution.py:29
  4.0 7.6 %all-to-all-start = ((bf16[16,32,1024]{2,1,0:T(8,128)(2,1)}), bf16[16,32,1024]{2,1,0:T(8,128)(2,1)S(1)}, u32[]{:S(2)}, u32[]{:S(2)}) async-start(bf16[16,32,1024]{2,1,0:T(8,128)(2,1)} %bitcast.46), calls=%async_computation | async-start | bytes 2097152 | tf_op jit(solution)/shard_map/all_to_all | solution.py:255
  11.6 0.7 slice.20.refs_16_
  12.3 2.6 %collective-permute-start = (bf16[512,256]{1,0:T(8,128)(2,1)}, bf16[512,256]{1,0:T(8,128)(2,1)S(1)}, u32[]{:S(2)}, u32[]{:S(2)}) collective-permute-start(bf16[512,256]{1,0:T(8,128)(2,1)} %slice.20.refs_16_), channel_id=1, source_target_pairs={{0,8},{1,9},{2,10},{3,11},{4,12},{5,13},{6,14},{7,15},{8,0},{9,1},... | collective-permute-start | bytes 786440 | tf_op jit(solution)/shard_map/ppermute | solution.py:29
  14.9 1.2 collective-permute-start.1
  16.1 1.5 collective-permute-start.2
  17.6 1.5 collective-permute-start.3
  19.1 6.4 %collective-permute-done.refs_1_.refs_17_ = bf16[512,256]{1,0:T(8,128)(2,1)S(1)} collective-permute-done((bf16[512,256]{1,0:T(8,128)(2,1)}, bf16[512,256]{1,0:T(8,128)(2,1)S(1)}, u32[]{:S(2)}, u32[]{:S(2)}) %collective-permute-start) | collective-permute-done | bytes 262176 | tf_op jit(solution)/shard_map/ppermute | solution.py:29
  25.5 1.2 collective-permute-start.4
  26.7 1.5 collective-permute-start.5
  28.2 1.5 collective-permute-start.6
  29.8 1.4 constant_dynamic-slice_fusion.momentum_ref
  31.1 1.5 constant_dynamic-slice_fusion.1.refs_0_
  32.6 4.6 %collective-permute-done.4.refs_5_.refs_19_ = bf16[512,256]{1,0:T(8,128)(2,1)S(1)} collective-permute-done((bf16[512,256]{1,0:T(8,128)(2,1)S(1)}, bf16[512,256]{1,0:T(8,128)(2,1)S(1)}, u32[]{:S(2)}, u32[]{:S(2)}) %collective-permute-start.4) | collective-permute-done | bytes 262176 | tf_op jit(solution)/shard_map/ppermute | solution.py:29
  37.2 4.4 %collective-permute-done.6.refs_7_.refs_23_ = bf16[512,256]{1,0:T(8,128)(2,1)} collective-permute-done((bf16[512,256]{1,0:T(8,128)(2,1)S(1)}, bf16[512,256]{1,0:T(8,128)(2,1)}, u32[]{:S(2)}, u32[]{:S(2)}) %collective-permute-start.6) | collective-permute-done | bytes 262176 | tf_op jit(solution)/shard_map/ppermute | solution.py:29
  41.7 0.0 copy-start.9
  41.7 1.0 copy-done.9
  42.6 2.8 %average_slice.1 = (bf16[16,32,768]{2,1,0:T(8,128)(2,1)}, bf16[32,256]{1,0:T(8,128)(2,1)}, bf16[32,256]{1,0:T(8,128)(2,1)}) custom-call(bf16[16,32,1024]{2,1,0:T(8,128)(2,1)} %copy-done.9, bf16[32,1024]{1,0:T(8,128)(2,1)} %after.3.outer_ref, f32[32,256]{1,0:T(8,128)} %constant_dynamic-slice_fusion.momentum_ref), custom_call_target="tpu_custom_call" | custom-call | flops 5242880 | bytes 2097152 | tf_op jit(solution)/shard_map/average_slice/pallas_call | solution.py:82
  45.5 7.3 %all-to-all-start.1 = ((bf16[16,32,768]{2,1,0:T(8,128)(2,1)}), bf16[16,32,768]{2,1,0:T(8,128)(2,1)S(1)}, u32[]{:S(2)}, u32[]{:S(2)}) async-start(bf16[16,32,768]{2,1,0:T(8,128)(2,1)} %get-tuple-element.14), calls=%async_computation.1 | async-start | bytes 1572864 | tf_op jit(solution)/shard_map/all_to_all | solution.py:264
  52.8 1.2 collective-permute-start.8
  54.0 3.0 %collective-permute-done.8 = bf16[32,256]{1,0:T(8,128)(2,1)S(1)} collective-permute-done((bf16[32,256]{1,0:T(8,128)(2,1)S(1)}, bf16[32,256]{1,0:T(8,128)(2,1)S(1)}, u32[]{:S(2)}, u32[]{:S(2)}) %collective-permute-start.8) | collective-permute-done | bytes 16416 | tf_op jit(solution)/shard_map/ppermute | solution.py:29
  57.0 0.5 collective-permute-start.9
  57.5 2.1 %collective-permute-start.10 = (bf16[2,32,256]{2,1,0:T(8,128)(2,1)S(1)}, bf16[2,32,256]{2,1,0:T(8,128)(2,1)S(1)}, u32[]{:S(2)}, u32[]{:S(2)}) collective-permute-start(bf16[2,32,256]{2,1,0:T(8,128)(2,1)S(1)} %pad_maximum_fusion.3), channel_id=1, source_target_pairs={{0,6},{1,7},{2,0},{3,1},{4,2},{5,3},{6,4},{7,5},{8,14},{9,15},{10,... | collective-permute-start | bytes 98312 | tf_op jit(solution)/shard_map/ppermute | solution.py:29
  59.7 1.6 collective-permute-done.9
  61.3 3.0 %collective-permute-done.11 = bf16[2,32,256]{2,1,0:T(8,128)(2,1)S(1)} collective-permute-done((bf16[2,32,256]{2,1,0:T(8,128)(2,1)S(1)}, bf16[2,32,256]{2,1,0:T(8,128)(2,1)S(1)}, u32[]{:S(2)}, u32[]{:S(2)}) %collective-permute-start.11) | collective-permute-done | bytes 32800 | tf_op jit(solution)/shard_map/ppermute | solution.py:29
  64.2 1.5 collective-permute-start.12
  65.7 4.2 %collective-permute-done.12 = bf16[9,32,256]{2,1,0:T(8,128)(2,1)S(1)} collective-permute-done((bf16[9,32,256]{2,1,0:T(8,128)(2,1)S(1)}, bf16[9,32,256]{2,1,0:T(8,128)(2,1)S(1)}, u32[]{:S(2)}, u32[]{:S(2)}) %collective-permute-start.12) | collective-permute-done | bytes 147488 | tf_op jit(solution)/shard_map/ppermute | solution.py:33
  70.0 1.0 all-to-all-done.1
  71.0 1.8 %broadcast_in_dim.17 = bf16[8,2,9,32,256]{4,3,2,1,0:T(8,128)(2,1)} broadcast(bf16[2,9,32,256]{3,2,1,0:T(8,128)(2,1)S(1)} %pad_maximum_fusion.2), dimensions={1,2,3,4} | broadcast | bytes 2654208 | tf_op jit(solution)/shard_map/broadcast_in_dim | solution.py:272
  72.8 6.0 %all-to-all-start.2 = ((bf16[8,2,9,32,256]{4,3,2,1,0:T(8,128)(2,1)}), bf16[8,2,9,32,256]{4,3,2,1,0:T(8,128)(2,1)}, u32[]{:S(2)}, u32[]{:S(2)}) async-start(bf16[8,2,9,32,256]{4,3,2,1,0:T(8,128)(2,1)} %broadcast_in_dim.17), calls=%async_computation.2 | async-start | bytes 4718592 | tf_op jit(solution)/shard_map/all_to_all | solution.py:275
  78.8 3.6 %multiply_convert_fusion.1 = (bf16[512,768]{1,0:T(8,128)(2,1)S(1)}, bf16[512,768]{1,0:T(8,128)(2,1)}, f32[512,768]{1,0:T(8,128)}) fusion(bf16[512,1024]{1,0:T(8,128)(2,1)S(1)} %bitcast.48, f32[512,1024]{1,0:T(8,128)} %param.6, bf16[16,32,768]{2,1,0:T(8,128)(2,1)S(1)} %all-to-all-done.1, bf16[512,1024]{1,0:T(8,128)(2,1)} %param.4), kind=kLoop, calls=%fused_computation.7 | loop fusion | flops 5505024 | bytes 7077888 | tf_op jit(solution)/shard_map/convert_element_type | solution.py:97
  82.4 1.2 collective-permute-start.13
  83.6 2.7 %collective-permute-start.17 = (bf16[512,768]{1,0:T(8,128)(2,1)S(1)}, bf16[512,768]{1,0:T(8,128)(2,1)}, u32[]{:S(2)}, u32[]{:S(2)}) collective-permute-start(bf16[512,768]{1,0:T(8,128)(2,1)S(1)} %get-tuple-element.25.refs_8_), channel_id=1, source_target_pairs={{0,6},{1,7},{2,0},{3,1},{4,2},{5,3},{6,4},{7,5},{8,14},{9,15},{10,... | collective-permute-start | bytes 2359304 | tf_op jit(solution)/shard_map/ppermute | solution.py:29
  86.3 12.8 %collective-permute-done.13.refs_11_ = bf16[512,768]{1,0:T(8,128)(2,1)S(1)} collective-permute-done((bf16[512,768]{1,0:T(8,128)(2,1)S(1)}, bf16[512,768]{1,0:T(8,128)(2,1)S(1)}, u32[]{:S(2)}, u32[]{:S(2)}) %collective-permute-start.13) | collective-permute-done | bytes 786464 | tf_op jit(solution)/shard_map/ppermute | solution.py:29
  99.1 0.1 fusion.3.at_ref
  99.2 1.5 collective-permute-start.14
  100.7 0.1 fusion.4.at_ref
  100.8 0.1 stack.73
  100.8 0.1 collective-permute-start.18
  101.0 8.1 %blocks_dot.4 = (f32[512,768]{1,0:T(8,128)S(1)}, f32[512,768]{1,0:T(8,128)}) custom-call(s32[4]{0:T(128)S(1)} %fusion.4.at_ref, bf16[512,8192]{1,0:T(8,128)(2,1)} %collective-permute-done.7.refs_0_.refs_1_.refs_2_.refs_3_.refs_4_.refs_5_.refs_6_.refs_7_, ...), custom_call_target="tpu_custom_call" | custom-call | flops 3221225472 | bytes 10485760 | tf_op jit(solution)/shard_map/blocks_dot/pallas_call | solution.py:216
  109.1 1.1 copy-done
  110.2 6.3 %collective-permute-done.15.refs_0_ = bf16[512,768]{1,0:T(8,128)(2,1)S(1)} collective-permute-done((bf16[512,768]{1,0:T(8,128)(2,1)S(1)}, bf16[512,768]{1,0:T(8,128)(2,1)S(1)}, u32[]{:S(2)}, u32[]{:S(2)}) %collective-permute-start.15) | collective-permute-done | bytes 786464 | tf_op jit(solution)/shard_map/ppermute | solution.py:29
  116.5 0.9 copy-done.3
  117.4 3.5 %collective-permute-start.19 = (bf16[512,768]{1,0:T(8,128)(2,1)}, bf16[512,768]{1,0:T(8,128)(2,1)S(1)}, u32[]{:S(2)}, u32[]{:S(2)}) collective-permute-start(bf16[512,768]{1,0:T(8,128)(2,1)} %after.4.refs_5_), channel_id=1, source_target_pairs={{0,6},{1,7},{2,0},{3,1},{4,2},{5,3},{6,4},{7,5},{8,14},{9,15},{10,... | collective-permute-start | bytes 2359304 | tf_op jit(solution)/shard_map/ppermute | solution.py:29
  120.9 0.1 fusion.5.at_ref
  121.0 0.6 pad_add_fusion.place_ref
  121.7 1.1 copy-done.4
  122.8 5.3 %blocks_dot.5 = (f32[512,768]{1,0:T(8,128)S(1)}, f32[512,768]{1,0:T(8,128)S(1)}) custom-call(s32[2]{0:T(128)S(1)} %fusion.3.at_ref, bf16[512,8192]{1,0:T(8,128)(2,1)} %collective-permute-done.7.refs_0_.refs_1_.refs_2_.refs_3_.refs_4_.refs_5_.refs_6_.refs_7_, ...), custom_call_target="tpu_custom_call" | custom-call | flops 1610612736 | bytes 6815744 | tf_op jit(solution)/shard_map/blocks_dot/pallas_call | solution.py:216
  128.1 1.1 copy-done.1
  129.3 1.1 copy-done.5
  130.4 2.2 %all-to-all-done.2.refs_0_ = bf16[8,2,9,32,256]{4,3,2,1,0:T(8,128)(2,1)} async-done(((bf16[8,2,9,32,256]{4,3,2,1,0:T(8,128)(2,1)}), bf16[8,2,9,32,256]{4,3,2,1,0:T(8,128)(2,1)}, u32[]{:S(2)}, u32[]{:S(2)}) %all-to-all-start.2) | async-done | bytes 2359328 | tf_op jit(solution)/shard_map/all_to_all | solution.py:275
  132.7 11.2 %early_dot.1 = (bf16[512,256]{1,0:T(8,128)(2,1)}, f32[512,256]{1,0:T(8,128)}, bf16[512,256]{1,0:T(8,128)(2,1)}, bf16[512,256]{1,0:T(8,128)(2,1)}) custom-call(s32[9]{0:T(128)} %pad_add_fusion.place_ref, bf16[512,8192]{1,0:T(8,128)(2,1)} %collective-permute-done.7.refs_0_.refs_1_.refs_2_.refs_3_.refs_4_.refs_5_.refs_6_.refs_7_, ...), custom_call_target="tpu_custom_call" | custom-call | flops 2147483648 | bytes 14680064 | tf_op jit(solution)/shard_map/early_dot/pallas_call | solution.py:148
  143.8 4.1 %collective-permute-start.21 = (bf16[512,256]{1,0:T(8,128)(2,1)}, bf16[512,256]{1,0:T(8,128)(2,1)S(1)}, u32[]{:S(2)}, u32[]{:S(2)}) collective-permute-start(bf16[512,256]{1,0:T(8,128)(2,1)} %get-tuple-element.24), channel_id=1, source_target_pairs={{0,1},{1,0},{2,3},{3,2},{4,5},{5,4},{6,7},{7,6},{8,9},{9,8},{10,11... | collective-permute-start | bytes 786440 | tf_op jit(solution)/shard_map/ppermute | solution.py:29
  148.0 2.8 %blocks_dot.7 = bf16[512,768]{1,0:T(8,128)(2,1)S(1)} custom-call(s32[2]{0:T(128)S(1)} %fusion.5.at_ref, bf16[512,8192]{1,0:T(8,128)(2,1)} %collective-permute-done.7.refs_0_.refs_1_.refs_2_.refs_3_.refs_4_.refs_5_.refs_6_.refs_7_, bf16[512,8192]{1,0:T(8,128)(2,1)} %collective-permute-done.7.refs_0_.refs_1_.refs_2_.refs_3_.refs_4_.refs_5_.refs_6_.refs_7_, ...), custom_call_target="tpu_custom_call" | custom-call | flops 805306368 | bytes 4194304 | tf_op jit(solution)/shard_map/blocks_dot/pallas_call | solution.py:216
  150.8 0.0 copy-start.10
  150.8 0.1 collective-permute-start.20
  150.9 1.3 convert_add_fusion.2
  152.2 1.1 pad_maximum_fusion.1
  153.3 1.6 %pad_maximum_fusion = f32[512,1024]{1,0:T(8,128)} fusion(f32[512,256]{1,0:T(8,128)S(1)} %convert_add_fusion.2, f32[512,768]{1,0:T(8,128)S(1)} %copy-done.7), kind=kLoop, calls=%fused_computation | loop fusion | flops 524288 | bytes 4194304 | tf_op jit(solution)/shard_map/concatenate | solution.py:295
  154.9 0.1 multiply_convert_fusion.2
  155.0 0.6 copy-done.6
  155.6 2.8 %blocks_dot.6 = f32[512,768]{1,0:T(8,128)S(1)} custom-call(s32[2]{0:T(128)S(1)} %fusion.5.at_ref, bf16[512,8192]{1,0:T(8,128)(2,1)} %bitcast.44, bf16[512,8192]{1,0:T(8,128)(2,1)} %bitcast.45, bf16[512,768]{1,0:T(8,128)(2,1)S(1)} %collective-permute-done.18.refs_2_, bf16[512,768]{1,0:T(8,128)(2,1)S(1)} %collective-permute-done.19.refs_3_, ...), custom_call_target="tpu_custom_call" | custom-call | flops 805306368 | bytes 4194304 | tf_op jit(solution)/shard_map/blocks_dot/pallas_call | solution.py:216
  158.5 0.2 multiply_convert_fusion
  158.7 1.1 maximum_bitcast_fusion
  (62 shorter events, 0.2 us)
Async XLA Ops:
  0.6 10.9 %copy-start.8 = (bf16[1,512,1024]{2,1,0:T(8,128)(2,1)S(1)}, bf16[1,512,1024]{2,1,0:T(8,128)(2,1)}, u32[]{:S(2)}) copy-start(bf16[1,512,1024]{2,1,0:T(8,128)(2,1)} %param.5) | copy-start | bytes 3145732
  0.6 100.3 %collective-permute-start.7 = (bf16[512,8192]{1,0:T(8,128)(2,1)}, bf16[512,8192]{1,0:T(8,128)(2,1)}, u32[]{:S(2)}, u32[]{:S(2)}) collective-permute-start(bf16[512,8192]{1,0:T(8,128)(2,1)} %bitcast.29), channel_id=1, source_target_pairs={{0,1},{1,0},{2,3},{3,2},{4,5},{5,4},{6,7},{7,6},{8,9},{9,8},{10,11... | collective-permute-start | bytes 25165832 | tf_op jit(solution)/shard_map/ppermute | solution.py:29
  4.0 37.7 %all-to-all-start = ((bf16[16,32,1024]{2,1,0:T(8,128)(2,1)}), bf16[16,32,1024]{2,1,0:T(8,128)(2,1)S(1)}, u32[]{:S(2)}, u32[]{:S(2)}) async-start(bf16[16,32,1024]{2,1,0:T(8,128)(2,1)} %bitcast.46), calls=%async_computation | async-start | bytes 2097152 | tf_op jit(solution)/shard_map/all_to_all | solution.py:255
  12.3 13.2 %collective-permute-start = (bf16[512,256]{1,0:T(8,128)(2,1)}, bf16[512,256]{1,0:T(8,128)(2,1)S(1)}, u32[]{:S(2)}, u32[]{:S(2)}) collective-permute-start(bf16[512,256]{1,0:T(8,128)(2,1)} %slice.20.refs_16_), channel_id=1, source_target_pairs={{0,8},{1,9},{2,10},{3,11},{4,12},{5,13},{6,14},{7,15},{8,0},{9,1},... | collective-permute-start | bytes 786440 | tf_op jit(solution)/shard_map/ppermute | solution.py:29
  14.9 11.8 %collective-permute-start.1 = (bf16[512,256]{1,0:T(8,128)(2,1)}, bf16[512,256]{1,0:T(8,128)(2,1)S(1)}, u32[]{:S(2)}, u32[]{:S(2)}) collective-permute-start(bf16[512,256]{1,0:T(8,128)(2,1)} %slice.20.refs_16_), channel_id=1, source_target_pairs={{0,2},{1,3},{2,4},{3,5},{4,6},{5,7},{6,0},{7,1},{8,10},{9,11},{10,... | collective-permute-start | bytes 786440 | tf_op jit(solution)/shard_map/ppermute | solution.py:29
  16.1 12.1 %collective-permute-start.2 = (bf16[512,256]{1,0:T(8,128)(2,1)}, bf16[512,256]{1,0:T(8,128)(2,1)S(1)}, u32[]{:S(2)}, u32[]{:S(2)}) collective-permute-start(bf16[512,256]{1,0:T(8,128)(2,1)} %slice.20.refs_16_), channel_id=1, source_target_pairs={{0,6},{1,7},{2,0},{3,1},{4,2},{5,3},{6,4},{7,5},{8,14},{9,15},{10,... | collective-permute-start | bytes 786440 | tf_op jit(solution)/shard_map/ppermute | solution.py:29
  17.6 15.0 %collective-permute-start.3 = (bf16[512,256]{1,0:T(8,128)(2,1)}, bf16[512,256]{1,0:T(8,128)(2,1)S(1)}, u32[]{:S(2)}, u32[]{:S(2)}) collective-permute-start(bf16[512,256]{1,0:T(8,128)(2,1)} %slice.20.refs_16_), channel_id=1, source_target_pairs={{0,4},{1,5},{2,6},{3,7},{4,0},{5,1},{6,2},{7,3},{8,12},{9,13},{10,... | collective-permute-start | bytes 786440 | tf_op jit(solution)/shard_map/ppermute | solution.py:29
  25.5 16.1 %copy-start.11 = (bf16[512,256]{1,0:T(8,128)(2,1)}, bf16[512,256]{1,0:T(8,128)(2,1)S(1)}, u32[]{:S(2)}) copy-start(bf16[512,256]{1,0:T(8,128)(2,1)S(1)} %collective-permute-done.refs_1_.refs_17_) | copy-start | bytes 786436
  25.5 11.6 %collective-permute-start.4 = (bf16[512,256]{1,0:T(8,128)(2,1)S(1)}, bf16[512,256]{1,0:T(8,128)(2,1)S(1)}, u32[]{:S(2)}, u32[]{:S(2)}) collective-permute-start(bf16[512,256]{1,0:T(8,128)(2,1)S(1)} %collective-permute-done.refs_1_.refs_17_), channel_id=1, source_target_pairs={{0,2},{1,3},{2,4},{3,5},{4,6},{5,7},{6,0},{7,1},{8,10},{9,11},{10,... | collective-permute-start | bytes 786440 | tf_op jit(solution)/shard_map/ppermute | solution.py:29
  26.7 14.9 %copy-start.12 = (bf16[512,256]{1,0:T(8,128)(2,1)}, bf16[512,256]{1,0:T(8,128)(2,1)S(1)}, u32[]{:S(2)}) copy-start(bf16[512,256]{1,0:T(8,128)(2,1)S(1)} %collective-permute-done.1.refs_2_.refs_18_) | copy-start | bytes 786436
  26.7 10.4 %collective-permute-start.5 = (bf16[512,256]{1,0:T(8,128)(2,1)S(1)}, bf16[512,256]{1,0:T(8,128)(2,1)}, u32[]{:S(2)}, u32[]{:S(2)}) collective-permute-start(bf16[512,256]{1,0:T(8,128)(2,1)S(1)} %collective-permute-done.refs_1_.refs_17_), channel_id=1, source_target_pairs={{0,6},{1,7},{2,0},{3,1},{4,2},{5,3},{6,4},{7,5},{8,14},{9,15},{10,... | collective-permute-start | bytes 786440 | tf_op jit(solution)/shard_map/ppermute | solution.py:29
  28.2 13.4 %copy-start.13 = (bf16[512,256]{1,0:T(8,128)(2,1)}, bf16[512,256]{1,0:T(8,128)(2,1)S(1)}, u32[]{:S(2)}) copy-start(bf16[512,256]{1,0:T(8,128)(2,1)S(1)} %collective-permute-done.2.refs_3_.refs_20_) | copy-start | bytes 786436
  28.2 13.4 %collective-permute-start.6 = (bf16[512,256]{1,0:T(8,128)(2,1)S(1)}, bf16[512,256]{1,0:T(8,128)(2,1)}, u32[]{:S(2)}, u32[]{:S(2)}) collective-permute-start(bf16[512,256]{1,0:T(8,128)(2,1)S(1)} %collective-permute-done.refs_1_.refs_17_), channel_id=1, source_target_pairs={{0,4},{1,5},{2,6},{3,7},{4,0},{5,1},{6,2},{7,3},{8,12},{9,13},{10,... | collective-permute-start | bytes 786440 | tf_op jit(solution)/shard_map/ppermute | solution.py:29
  32.6 9.0 %copy-start.14 = (bf16[512,256]{1,0:T(8,128)(2,1)}, bf16[512,256]{1,0:T(8,128)(2,1)S(1)}, u32[]{:S(2)}) copy-start(bf16[512,256]{1,0:T(8,128)(2,1)S(1)} %collective-permute-done.3.refs_4_.refs_22_) | copy-start | bytes 786436
  37.2 4.5 %copy-start.15 = (bf16[512,256]{1,0:T(8,128)(2,1)}, bf16[512,256]{1,0:T(8,128)(2,1)S(1)}, u32[]{:S(2)}) copy-start(bf16[512,256]{1,0:T(8,128)(2,1)S(1)} %collective-permute-done.4.refs_5_.refs_19_) | copy-start | bytes 786436
  41.7 1.0 copy-start.9
  45.5 7.3 %copy-start.19 = (bf16[32,256]{1,0:T(8,128)(2,1)S(1)}, bf16[32,256]{1,0:T(8,128)(2,1)}, u32[]{:S(2)}) copy-start(bf16[32,256]{1,0:T(8,128)(2,1)} %get-tuple-element.15) | copy-start | bytes 49156
  45.5 18.8 %copy-start.20 = (bf16[32,256]{1,0:T(8,128)(2,1)S(1)}, bf16[32,256]{1,0:T(8,128)(2,1)}, u32[]{:S(2)}) copy-start(bf16[32,256]{1,0:T(8,128)(2,1)} %get-tuple-element.16) | copy-start | bytes 49156
  45.5 25.5 %all-to-all-start.1 = ((bf16[16,32,768]{2,1,0:T(8,128)(2,1)}), bf16[16,32,768]{2,1,0:T(8,128)(2,1)S(1)}, u32[]{:S(2)}, u32[]{:S(2)}) async-start(bf16[16,32,768]{2,1,0:T(8,128)(2,1)} %get-tuple-element.14), calls=%async_computation.1 | async-start | bytes 1572864 | tf_op jit(solution)/shard_map/all_to_all | solution.py:264
  52.8 4.2 %collective-permute-start.8 = (bf16[32,256]{1,0:T(8,128)(2,1)S(1)}, bf16[32,256]{1,0:T(8,128)(2,1)S(1)}, u32[]{:S(2)}, u32[]{:S(2)}) collective-permute-start(bf16[32,256]{1,0:T(8,128)(2,1)S(1)} %copy-done.19), channel_id=1, source_target_pairs={{0,8},{1,9},{2,10},{3,11},{4,12},{5,13},{6,14},{7,15},{8,0},{9,1},... | collective-permute-start | bytes 49160 | tf_op jit(solution)/shard_map/ppermute | solution.py:29
  57.0 4.3 %collective-permute-start.9 = (bf16[2,32,256]{2,1,0:T(8,128)(2,1)S(1)}, bf16[2,32,256]{2,1,0:T(8,128)(2,1)S(1)}, u32[]{:S(2)}, u32[]{:S(2)}) collective-permute-start(bf16[2,32,256]{2,1,0:T(8,128)(2,1)S(1)} %pad_maximum_fusion.3), channel_id=1, source_target_pairs={{0,2},{1,3},{2,4},{3,5},{4,6},{5,7},{6,0},{7,1},{8,10},{9,11},{10,... | collective-permute-start | bytes 98312 | tf_op jit(solution)/shard_map/ppermute | solution.py:29
  57.5 3.7 %collective-permute-start.10 = (bf16[2,32,256]{2,1,0:T(8,128)(2,1)S(1)}, bf16[2,32,256]{2,1,0:T(8,128)(2,1)S(1)}, u32[]{:S(2)}, u32[]{:S(2)}) collective-permute-start(bf16[2,32,256]{2,1,0:T(8,128)(2,1)S(1)} %pad_maximum_fusion.3), channel_id=1, source_target_pairs={{0,6},{1,7},{2,0},{3,1},{4,2},{5,3},{6,4},{7,5},{8,14},{9,15},{10,... | collective-permute-start | bytes 98312 | tf_op jit(solution)/shard_map/ppermute | solution.py:29
  59.7 4.6 %collective-permute-start.11 = (bf16[2,32,256]{2,1,0:T(8,128)(2,1)S(1)}, bf16[2,32,256]{2,1,0:T(8,128)(2,1)S(1)}, u32[]{:S(2)}, u32[]{:S(2)}) collective-permute-start(bf16[2,32,256]{2,1,0:T(8,128)(2,1)S(1)} %pad_maximum_fusion.3), channel_id=1, source_target_pairs={{0,4},{1,5},{2,6},{3,7},{4,0},{5,1},{6,2},{7,3},{8,12},{9,13},{10,... | collective-permute-start | bytes 98312 | tf_op jit(solution)/shard_map/ppermute | solution.py:29
  64.2 5.7 %collective-permute-start.12 = (bf16[9,32,256]{2,1,0:T(8,128)(2,1)S(1)}, bf16[9,32,256]{2,1,0:T(8,128)(2,1)S(1)}, u32[]{:S(2)}, u32[]{:S(2)}) collective-permute-start(bf16[9,32,256]{2,1,0:T(8,128)(2,1)S(1)} %bitcast_dynamic-update-slice_fusion), channel_id=1, source_target_pairs={{0,128},{16,144},{32,160},{48,176},{64,192},{80,208},{96,224},{112... | collective-permute-start | bytes 442376 | tf_op jit(solution)/shard_map/ppermute | solution.py:33
  72.8 59.8 %all-to-all-start.2 = ((bf16[8,2,9,32,256]{4,3,2,1,0:T(8,128)(2,1)}), bf16[8,2,9,32,256]{4,3,2,1,0:T(8,128)(2,1)}, u32[]{:S(2)}, u32[]{:S(2)}) async-start(bf16[8,2,9,32,256]{4,3,2,1,0:T(8,128)(2,1)} %broadcast_in_dim.17), calls=%async_computation.2 | async-start | bytes 4718592 | tf_op jit(solution)/shard_map/all_to_all | solution.py:275
  82.4 16.7 %collective-permute-start.13 = (bf16[512,768]{1,0:T(8,128)(2,1)S(1)}, bf16[512,768]{1,0:T(8,128)(2,1)S(1)}, u32[]{:S(2)}, u32[]{:S(2)}) collective-permute-start(bf16[512,768]{1,0:T(8,128)(2,1)S(1)} %get-tuple-element.25.refs_8_), channel_id=1, source_target_pairs={{0,8},{1,9},{2,10},{3,11},{4,12},{5,13},{6,14},{7,15},{8,0},{9,1},... | collective-permute-start | bytes 2359304 | tf_op jit(solution)/shard_map/ppermute | solution.py:29
  83.6 17.2 %collective-permute-start.16 = (bf16[512,768]{1,0:T(8,128)(2,1)S(1)}, bf16[512,768]{1,0:T(8,128)(2,1)}, u32[]{:S(2)}, u32[]{:S(2)}) collective-permute-start(bf16[512,768]{1,0:T(8,128)(2,1)S(1)} %get-tuple-element.25.refs_8_), channel_id=1, source_target_pairs={{0,2},{1,3},{2,4},{3,5},{4,6},{5,7},{6,0},{7,1},{8,10},{9,11},{10,... | collective-permute-start | bytes 2359304 | tf_op jit(solution)/shard_map/ppermute | solution.py:29
  83.6 17.3 %collective-permute-start.17 = (bf16[512,768]{1,0:T(8,128)(2,1)S(1)}, bf16[512,768]{1,0:T(8,128)(2,1)}, u32[]{:S(2)}, u32[]{:S(2)}) collective-permute-start(bf16[512,768]{1,0:T(8,128)(2,1)S(1)} %get-tuple-element.25.refs_8_), channel_id=1, source_target_pairs={{0,6},{1,7},{2,0},{3,1},{4,2},{5,3},{6,4},{7,5},{8,14},{9,15},{10,... | collective-permute-start | bytes 2359304 | tf_op jit(solution)/shard_map/ppermute | solution.py:29
  99.1 17.4 %collective-permute-start.15 = (bf16[512,768]{1,0:T(8,128)(2,1)S(1)}, bf16[512,768]{1,0:T(8,128)(2,1)S(1)}, u32[]{:S(2)}, u32[]{:S(2)}) collective-permute-start(bf16[512,768]{1,0:T(8,128)(2,1)S(1)} %collective-permute-done.13.refs_11_), channel_id=1, source_target_pairs={{0,6},{1,7},{2,0},{3,1},{4,2},{5,3},{6,4},{7,5},{8,14},{9,15},{10,... | collective-permute-start | bytes 2359304 | tf_op jit(solution)/shard_map/ppermute | solution.py:29
  99.2 22.5 %collective-permute-start.14 = (bf16[512,768]{1,0:T(8,128)(2,1)S(1)}, bf16[512,768]{1,0:T(8,128)(2,1)}, u32[]{:S(2)}, u32[]{:S(2)}) collective-permute-start(bf16[512,768]{1,0:T(8,128)(2,1)S(1)} %collective-permute-done.13.refs_11_), channel_id=1, source_target_pairs={{0,2},{1,3},{2,4},{3,5},{4,6},{5,7},{6,0},{7,1},{8,10},{9,11},{10,... | collective-permute-start | bytes 2359304 | tf_op jit(solution)/shard_map/ppermute | solution.py:29
  100.8 47.1 %collective-permute-start.18 = (bf16[512,768]{1,0:T(8,128)(2,1)}, bf16[512,768]{1,0:T(8,128)(2,1)S(1)}, u32[]{:S(2)}, u32[]{:S(2)}) collective-permute-start(bf16[512,768]{1,0:T(8,128)(2,1)} %collective-permute-done.16.refs_9_), channel_id=1, source_target_pairs={{0,2},{1,3},{2,4},{3,5},{4,6},{5,7},{6,0},{7,1},{8,10},{9,11},{10,... | collective-permute-start | bytes 2359304 | tf_op jit(solution)/shard_map/ppermute | solution.py:29
  109.1 1.2 copy-start
  116.5 0.9 copy-start.3
  117.4 30.5 %collective-permute-start.19 = (bf16[512,768]{1,0:T(8,128)(2,1)}, bf16[512,768]{1,0:T(8,128)(2,1)S(1)}, u32[]{:S(2)}, u32[]{:S(2)}) collective-permute-start(bf16[512,768]{1,0:T(8,128)(2,1)} %after.4.refs_5_), channel_id=1, source_target_pairs={{0,6},{1,7},{2,0},{3,1},{4,2},{5,3},{6,4},{7,5},{8,14},{9,15},{10,... | collective-permute-start | bytes 2359304 | tf_op jit(solution)/shard_map/ppermute | solution.py:29
  121.7 1.1 copy-start.4
  128.1 1.2 copy-start.1
  129.3 1.2 copy-start.5
  132.7 15.3 %copy-start.2 = (f32[512,768]{1,0:T(8,128)S(1)}, f32[512,768]{1,0:T(8,128)}, u32[]{:S(2)}) copy-start(f32[512,768]{1,0:T(8,128)} %copy-done.1) | copy-start | bytes 4718596
  143.8 7.1 %copy-start.17 = (bf16[512,256]{1,0:T(8,128)(2,1)S(1)}, bf16[512,256]{1,0:T(8,128)(2,1)}, u32[]{:S(2)}) copy-start(bf16[512,256]{1,0:T(8,128)(2,1)} %get-tuple-element.21) | copy-start | bytes 786436
  143.8 8.3 %copy-start.18 = (bf16[512,256]{1,0:T(8,128)(2,1)S(1)}, bf16[512,256]{1,0:T(8,128)(2,1)}, u32[]{:S(2)}) copy-start(bf16[512,256]{1,0:T(8,128)(2,1)} %get-tuple-element.20) | copy-start | bytes 786436
  143.8 11.1 %collective-permute-start.21 = (bf16[512,256]{1,0:T(8,128)(2,1)}, bf16[512,256]{1,0:T(8,128)(2,1)S(1)}, u32[]{:S(2)}, u32[]{:S(2)}) collective-permute-start(bf16[512,256]{1,0:T(8,128)(2,1)} %get-tuple-element.24), channel_id=1, source_target_pairs={{0,1},{1,0},{2,3},{3,2},{4,5},{5,4},{6,7},{7,6},{8,9},{9,8},{10,11... | collective-permute-start | bytes 786440 | tf_op jit(solution)/shard_map/ppermute | solution.py:29
  150.8 1.4 copy-start.10
  150.8 7.7 %collective-permute-start.20 = (bf16[512,768]{1,0:T(8,128)(2,1)S(1)}, bf16[512,768]{1,0:T(8,128)(2,1)S(1)}, u32[]{:S(2)}, u32[]{:S(2)}) collective-permute-start(bf16[512,768]{1,0:T(8,128)(2,1)S(1)} %blocks_dot.7), channel_id=1, source_target_pairs={{0,1},{1,0},{2,3},{3,2},{4,5},{5,4},{6,7},{7,6},{8,9},{9,8},{10,11... | collective-permute-start | bytes 2359304 | tf_op jit(solution)/shard_map/ppermute | solution.py:29
  150.9 2.4 %copy-start.7 = (f32[512,768]{1,0:T(8,128)S(1)}, f32[512,768]{1,0:T(8,128)}, u32[]{:S(2)}) copy-start(f32[512,768]{1,0:T(8,128)} %get-tuple-element.27) | copy-start | bytes 4718596
  153.3 1.6 %copy-start.16 = (f32[512,256]{1,0:T(8,128)S(1)}, f32[512,256]{1,0:T(8,128)}, u32[]{:S(2)}) copy-start(f32[512,256]{1,0:T(8,128)} %get-tuple-element.23) | copy-start | bytes 1572868
  153.3 2.3 %copy-start.6 = (f32[512,768]{1,0:T(8,128)S(1)}, f32[512,768]{1,0:T(8,128)}, u32[]{:S(2)}) copy-start(f32[512,768]{1,0:T(8,128)} %copy-done.5) | copy-start | bytes 4718596

commit v4 on v3

--- a/solution.py
+++ b/solution.py
@@ -97,7 +97,7 @@
     return (0.5 * one.astype(F32) + 0.5 * other.astype(F32)).astype(BF16)
 
 
-def early_dot(lefts, blocks, inners, late, yl):
+def early_dot(lefts, blocks, inners, late, yl, momentum):
     count, (rows, wide) = len(inners), inners[0].shape
     half, tile, sides = rows // YL, 256, len(lefts)
     steps = rows // tile
@@ -105,7 +105,8 @@
 
     def kernel(place_ref, *refs):
         tokens, refs = refs[: sides * count], refs[sides * count :]
-        outer_ref, average_ref, mixed_ref = refs[-3:]
+        outer_ref, momentum_next_ref, mixed_ref = refs[-3:]
+        momentum_ref = refs[count + lates]
         outs = refs[-3 - sides : -3]
         step = pl.program_id(0)
 
@@ -117,7 +118,7 @@
                 for k in range(count):
                     mixed_ref[k, at] = mix(refs[k][at], outers[k])
                 outer_ref[at] = outers[0]
-                average_ref[at] = outers[count]
+                momentum_next_ref[at] = 0.9 * momentum_ref[at] + outers[count].astype(F32)
 
         for side in range(sides):
 
@@ -152,12 +153,13 @@
             grid=(sides * steps,),
             in_specs=[left_spec(side, k) for side in range(sides) for k in range(count)]
             + [whole(rows, wide)] * count
-            + [late_spec(h, k) for h in range(YL) for k in range(count + 1)],
+            + [late_spec(h, k) for h in range(YL) for k in range(count + 1)]
+            + [pl.BlockSpec((rows, wide), lambda i, place: (0, MAIN // wide))],
             out_specs=[row_spec(side) for side in range(sides)] + [whole(rows, wide)] * 2,
             scratch_shapes=[pltpu.VMEM((count, rows, wide), BF16)],
         ),
         out_shape=[jax.ShapeDtypeStruct((rows, wide), dtype) for dtype in (BF16, F32)]
-        + [jax.ShapeDtypeStruct((rows, wide), BF16)] * 2,
+        + [jax.ShapeDtypeStruct((rows, wide), dtype) for dtype in (BF16, F32)],
         compiler_params=pltpu.CompilerParams(vmem_limit_bytes=60 * MIB),
         cost_estimate=pl.CostEstimate(
             flops=2 * sides * rows * rows * count * wide,
@@ -170,6 +172,7 @@
         *[left for left in lefts for _ in range(count)],
         *inners,
         *([late] * lates),
+        momentum,
     )
 
 
@@ -286,11 +289,10 @@
     there_across = fsdp_move(there_right, dx=-1)
     sums = dot(SIDES, [(there_left,), (there_right,)], sums)
 
-    theirs_early, ours_early, outer_early, average_early = early_dot(
-        both, CORE * chips_of(ORDER) + core, inners, after(late, sums[0]), yl
+    theirs_early, ours_early, outer_early, momentum_early = early_dot(
+        both, CORE * chips_of(ORDER) + core, inners, after(late, sums[0]), yl, momentum
     )
     theirs_early = fsdp_move(theirs_early, dc=1)
-    momentum_early = 0.9 * momentum[:, early] + average_early.astype(F32)
     outer_next = jnp.concatenate([outer_main, outer_early], axis=1)
     momentum_next = jnp.concatenate([momentum_main, momentum_early], axis=1)
 

time: 161 us -> 165 us (1.025)
  starting transfers between devices: 53.8 us -> 55.9 us
    ppermute x21, waiting for transfers between devices: 42.1 us -> 44.5 us  [fsdp_move(): return lax.ppermute(array, 'fsdp', perm)]
    ppermute x21, starting transfers between devices: 31.4 us -> 33.6 us  [fsdp_move(): return lax.ppermute(array, 'fsdp', perm)]
    unnamed x47 -> x43, local copies, waits for them, and re-layouts: 7.13 us -> 6.08 us
  transfers between devices with their start and end apart: 25 -> 25, of which waited for: 11 -> 12; matrix products, arithmetic and copies ran while one was open for 9% -> 9% of each run, Pallas kernels for 21% -> 19%
where the time goes in v4:
time: 165 us; the launch traced here: 164 us
  starting transfers between devices  55.9 us (34%)
  waiting for transfers between devices  50.6 us (31%)
  Pallas kernels  33.9 us (21%)
  local copies, waits for them, and re-layouts  11.8 us (7%)
  other arithmetic  11.1 us (7%)
    ppermute x21, waiting for transfers between devices, fsdp_move(): return lax.ppermute(array, 'fsdp', perm)  44.5 us
    ppermute x21, starting transfers between devices, fsdp_move(): return lax.ppermute(array, 'fsdp', perm)  33.6 us
    pallas_call x4, Pallas kernels, blocks_dot(): pl.pallas_call(kernel, grid_spec=pltpu.PrefetchScalarGridSpec(num_scalar_...  19.8 us
    pallas_call x1, Pallas kernels, early_dot(): pl.pallas_call(kernel, grid_spec=pltpu.PrefetchScalarGridSpec(num_scalar_...  11.3 us
    all_to_all x1, starting transfers between devices, shards(): recv = lax.all_to_all(inner.reshape(REP, part, columns), 'rep', 0, 0)  7.62 us
    all_to_all x1, starting transfers between devices, shards(): average = lax.all_to_all(copies, 'rep', 0, 0).reshape(rows, MAIN)  7.02 us
    unnamed x43, local copies, waits for them, and re-layouts  6.08 us
    all_to_all x1, starting transfers between devices, shards(): late = lax.all_to_all(slices, 'rep', 0, 0, axis_index_groups=SAME_YL)  5.19 us
  transfers between devices with their start and end apart: 25, of which 12 were waited for; matrix products, arithmetic and copies ran while one was open for 9% of the time, Pallas kernels for 19%

profile of v4, /device:TPU:1, one launch (start us, length us, event | category | flops | bytes accessed | tf_op | source)
XLA Modules:
  0.0 164.3 jit_solution(108339436866731425)
XLA Ops:
  0.6 0.0 copy-start.7
  0.6 3.3 %collective-permute-start.7 = (bf16[512,8192]{1,0:T(8,128)(2,1)}, bf16[512,8192]{1,0:T(8,128)(2,1)}, u32[]{:S(2)}, u32[]{:S(2)}) collective-permute-start(bf16[512,8192]{1,0:T(8,128)(2,1)} %bitcast.29), channel_id=1, source_target_pairs={{0,1},{1,0},{2,3},{3,2},{4,5},{5,4},{6,7},{7,6},{8,9},{9,8},{10,11... | collective-permute-start | bytes 25165832 | tf_op jit(solution)/shard_map/ppermute | solution.py:29
  4.0 7.6 %all-to-all-start = ((bf16[16,32,1024]{2,1,0:T(8,128)(2,1)}), bf16[16,32,1024]{2,1,0:T(8,128)(2,1)}, u32[]{:S(2)}, u32[]{:S(2)}) async-start(bf16[16,32,1024]{2,1,0:T(8,128)(2,1)} %bitcast.46), calls=%async_computation | async-start | bytes 2097152 | tf_op jit(solution)/shard_map/all_to_all | solution.py:258
  11.6 1.7 %slice.16.refs_16_ = bf16[512,256]{1,0:T(8,128)(2,1)} slice(bf16[512,1024]{1,0:T(8,128)(2,1)} %bitcast.47), slice={[0:512], [768:1024]} | slice | bytes 524288 | tf_op jit(solution)/shard_map/slice | solution.py:260
  13.3 2.6 %collective-permute-start = (bf16[512,256]{1,0:T(8,128)(2,1)}, bf16[512,256]{1,0:T(8,128)(2,1)S(1)}, u32[]{:S(2)}, u32[]{:S(2)}) collective-permute-start(bf16[512,256]{1,0:T(8,128)(2,1)} %slice.16.refs_16_), channel_id=1, source_target_pairs={{0,8},{1,9},{2,10},{3,11},{4,12},{5,13},{6,14},{7,15},{8,0},{9,1},... | collective-permute-start | bytes 786440 | tf_op jit(solution)/shard_map/ppermute | solution.py:29
  15.9 1.2 collective-permute-start.1
  17.1 1.5 collective-permute-start.2
  18.6 1.5 collective-permute-start.3
  20.1 7.2 %collective-permute-done.refs_1_.refs_17_ = bf16[512,256]{1,0:T(8,128)(2,1)S(1)} collective-permute-done((bf16[512,256]{1,0:T(8,128)(2,1)}, bf16[512,256]{1,0:T(8,128)(2,1)S(1)}, u32[]{:S(2)}, u32[]{:S(2)}) %collective-permute-start) | collective-permute-done | bytes 262176 | tf_op jit(solution)/shard_map/ppermute | solution.py:29
  27.4 1.2 collective-permute-start.4
  28.6 1.5 collective-permute-start.5
  30.0 1.5 collective-permute-start.6
  31.6 0.6 constant_dynamic-slice_fusion.momentum_ref
  32.2 1.5 constant_dynamic-slice_fusion.1.refs_0_
  33.7 5.2 %collective-permute-done.4.refs_5_.refs_19_ = bf16[512,256]{1,0:T(8,128)(2,1)S(1)} collective-permute-done((bf16[512,256]{1,0:T(8,128)(2,1)S(1)}, bf16[512,256]{1,0:T(8,128)(2,1)S(1)}, u32[]{:S(2)}, u32[]{:S(2)}) %collective-permute-start.4) | collective-permute-done | bytes 262176 | tf_op jit(solution)/shard_map/ppermute | solution.py:29
  38.8 3.7 %collective-permute-done.6.refs_7_.refs_23_ = bf16[512,256]{1,0:T(8,128)(2,1)} collective-permute-done((bf16[512,256]{1,0:T(8,128)(2,1)S(1)}, bf16[512,256]{1,0:T(8,128)(2,1)}, u32[]{:S(2)}, u32[]{:S(2)}) %collective-permute-start.6) | collective-permute-done | bytes 262176 | tf_op jit(solution)/shard_map/ppermute | solution.py:29
  42.6 2.8 %average_slice.1 = (bf16[16,32,768]{2,1,0:T(8,128)(2,1)}, bf16[32,256]{1,0:T(8,128)(2,1)}, bf16[32,256]{1,0:T(8,128)(2,1)}) custom-call(bf16[16,32,1024]{2,1,0:T(8,128)(2,1)} %all-to-all-done.recv_ref, bf16[32,1024]{1,0:T(8,128)(2,1)} %after.3.outer_ref, f32[32,256]{1,0:T(8,128)} %constant_dynamic-slice_fusion.momentum_ref), custom_call_target="tpu_custom_call" | custom-call | flops 5242880 | bytes 2097152 | tf_op jit(solution)/shard_map/average_slice/pallas_call | solution.py:82
  45.5 7.0 %all-to-all-start.1 = ((bf16[16,32,768]{2,1,0:T(8,128)(2,1)}), bf16[16,32,768]{2,1,0:T(8,128)(2,1)S(1)}, u32[]{:S(2)}, u32[]{:S(2)}) async-start(bf16[16,32,768]{2,1,0:T(8,128)(2,1)} %get-tuple-element.14), calls=%async_computation.1 | async-start | bytes 1572864 | tf_op jit(solution)/shard_map/all_to_all | solution.py:267
  52.5 1.5 collective-permute-start.8
  54.0 2.6 %collective-permute-done.8 = bf16[32,256]{1,0:T(8,128)(2,1)S(1)} collective-permute-done((bf16[32,256]{1,0:T(8,128)(2,1)S(1)}, bf16[32,256]{1,0:T(8,128)(2,1)S(1)}, u32[]{:S(2)}, u32[]{:S(2)}) %collective-permute-start.8) | collective-permute-done | bytes 16416 | tf_op jit(solution)/shard_map/ppermute | solution.py:29
  56.7 0.9 collective-permute-start.9
  57.6 1.8 %collective-permute-start.10 = (bf16[2,32,256]{2,1,0:T(8,128)(2,1)S(1)}, bf16[2,32,256]{2,1,0:T(8,128)(2,1)S(1)}, u32[]{:S(2)}, u32[]{:S(2)}) collective-permute-start(bf16[2,32,256]{2,1,0:T(8,128)(2,1)S(1)} %pad_maximum_fusion.3), channel_id=1, source_target_pairs={{0,6},{1,7},{2,0},{3,1},{4,2},{5,3},{6,4},{7,5},{8,14},{9,15},{10,... | collective-permute-start | bytes 98312 | tf_op jit(solution)/shard_map/ppermute | solution.py:29
  59.4 0.1 collective-permute-start.11
  59.4 1.5 collective-permute-done.9
  61.0 3.0 %collective-permute-done.11 = bf16[2,32,256]{2,1,0:T(8,128)(2,1)S(1)} collective-permute-done((bf16[2,32,256]{2,1,0:T(8,128)(2,1)S(1)}, bf16[2,32,256]{2,1,0:T(8,128)(2,1)S(1)}, u32[]{:S(2)}, u32[]{:S(2)}) %collective-permute-start.11) | collective-permute-done | bytes 32800 | tf_op jit(solution)/shard_map/ppermute | solution.py:29
  63.9 2.5 %collective-permute-start.12 = (bf16[9,32,256]{2,1,0:T(8,128)(2,1)S(1)}, bf16[9,32,256]{2,1,0:T(8,128)(2,1)S(1)}, u32[]{:S(2)}, u32[]{:S(2)}) collective-permute-start(bf16[9,32,256]{2,1,0:T(8,128)(2,1)S(1)} %bitcast_dynamic-update-slice_fusion), channel_id=1, source_target_pairs={{0,128},{16,144},{32,160},{48,176},{64,192},{80,208},{96,224},{112... | collective-permute-start | bytes 442376 | tf_op jit(solution)/shard_map/ppermute | solution.py:33
  66.4 4.9 %collective-permute-done.12 = bf16[9,32,256]{2,1,0:T(8,128)(2,1)S(1)} collective-permute-done((bf16[9,32,256]{2,1,0:T(8,128)(2,1)S(1)}, bf16[9,32,256]{2,1,0:T(8,128)(2,1)S(1)}, u32[]{:S(2)}, u32[]{:S(2)}) %collective-permute-start.12) | collective-permute-done | bytes 147488 | tf_op jit(solution)/shard_map/ppermute | solution.py:33
  71.4 1.8 %broadcast_in_dim.17 = bf16[8,2,9,32,256]{4,3,2,1,0:T(8,128)(2,1)} broadcast(bf16[2,9,32,256]{3,2,1,0:T(8,128)(2,1)S(1)} %pad_maximum_fusion.2), dimensions={1,2,3,4} | broadcast | bytes 2654208 | tf_op jit(solution)/shard_map/broadcast_in_dim | solution.py:275
  73.2 5.2 %all-to-all-start.2 = ((bf16[8,2,9,32,256]{4,3,2,1,0:T(8,128)(2,1)}), bf16[8,2,9,32,256]{4,3,2,1,0:T(8,128)(2,1)}, u32[]{:S(2)}, u32[]{:S(2)}) async-start(bf16[8,2,9,32,256]{4,3,2,1,0:T(8,128)(2,1)} %broadcast_in_dim.17), calls=%async_computation.2 | async-start | bytes 4718592 | tf_op jit(solution)/shard_map/all_to_all | solution.py:278
  78.4 3.6 %multiply_convert_fusion.1 = (bf16[512,768]{1,0:T(8,128)(2,1)S(1)}, bf16[512,768]{1,0:T(8,128)(2,1)}, f32[512,768]{1,0:T(8,128)}) fusion(bf16[512,1024]{1,0:T(8,128)(2,1)} %bitcast.48, f32[512,1024]{1,0:T(8,128)S(1)} %copy-done.7, bf16[16,32,768]{2,1,0:T(8,128)(2,1)} %copy-done.9, bf16[512,1024]{1,0:T(8,128)(2,1)} %param.4), kind=kLoop, calls=%fused_computation.7 | loop fusion | flops 5505024 | bytes 7077888 | tf_op jit(solution)/shard_map/convert_element_type | solution.py:97
  82.0 1.6 collective-permute-start.13
  83.6 2.7 %collective-permute-start.17 = (bf16[512,768]{1,0:T(8,128)(2,1)S(1)}, bf16[512,768]{1,0:T(8,128)(2,1)}, u32[]{:S(2)}, u32[]{:S(2)}) collective-permute-start(bf16[512,768]{1,0:T(8,128)(2,1)S(1)} %get-tuple-element.25.refs_8_), channel_id=1, source_target_pairs={{0,6},{1,7},{2,0},{3,1},{4,2},{5,3},{6,4},{7,5},{8,14},{9,15},{10,... | collective-permute-start | bytes 2359304 | tf_op jit(solution)/shard_map/ppermute | solution.py:29
  86.3 12.4 %collective-permute-done.13.refs_11_ = bf16[512,768]{1,0:T(8,128)(2,1)S(1)} collective-permute-done((bf16[512,768]{1,0:T(8,128)(2,1)S(1)}, bf16[512,768]{1,0:T(8,128)(2,1)S(1)}, u32[]{:S(2)}, u32[]{:S(2)}) %collective-permute-start.13) | collective-permute-done | bytes 786464 | tf_op jit(solution)/shard_map/ppermute | solution.py:29
  98.7 0.7 collective-permute-start.15
  99.3 0.1 fusion.4.at_ref
  99.4 0.8 collective-permute-start.14
  100.2 0.7 collective-permute-start.18
  100.9 8.1 %blocks_dot.4 = (f32[512,768]{1,0:T(8,128)S(1)}, f32[512,768]{1,0:T(8,128)}) custom-call(s32[4]{0:T(128)S(1)} %fusion.4.at_ref, bf16[512,8192]{1,0:T(8,128)(2,1)} %collective-permute-done.7.refs_0_.refs_1_.refs_2_.refs_3_.refs_4_.refs_5_.refs_6_.refs_7_, ...), custom_call_target="tpu_custom_call" | custom-call | flops 3221225472 | bytes 10485760 | tf_op jit(solution)/shard_map/blocks_dot/pallas_call | solution.py:219
  109.0 1.1 copy-done
  110.1 6.6 %collective-permute-done.15.refs_0_ = bf16[512,768]{1,0:T(8,128)(2,1)S(1)} collective-permute-done((bf16[512,768]{1,0:T(8,128)(2,1)S(1)}, bf16[512,768]{1,0:T(8,128)(2,1)S(1)}, u32[]{:S(2)}, u32[]{:S(2)}) %collective-permute-start.15) | collective-permute-done | bytes 786464 | tf_op jit(solution)/shard_map/ppermute | solution.py:29
  116.8 0.9 copy-done.3
  117.6 3.5 %collective-permute-start.19 = (bf16[512,768]{1,0:T(8,128)(2,1)}, bf16[512,768]{1,0:T(8,128)(2,1)S(1)}, u32[]{:S(2)}, u32[]{:S(2)}) collective-permute-start(bf16[512,768]{1,0:T(8,128)(2,1)} %after.4.refs_5_), channel_id=1, source_target_pairs={{0,6},{1,7},{2,0},{3,1},{4,2},{5,3},{6,4},{7,5},{8,14},{9,15},{10,... | collective-permute-start | bytes 2359304 | tf_op jit(solution)/shard_map/ppermute | solution.py:29
  121.2 0.1 stack.73
  121.2 0.1 fusion.3.at_ref
  121.3 0.1 fusion.5.at_ref
  121.4 0.7 pad_add_fusion.place_ref
  122.1 1.1 copy-done.4
  123.2 5.3 %blocks_dot.5 = (f32[512,768]{1,0:T(8,128)S(1)}, f32[512,768]{1,0:T(8,128)S(1)}) custom-call(s32[2]{0:T(128)S(1)} %fusion.3.at_ref, bf16[512,8192]{1,0:T(8,128)(2,1)} %collective-permute-done.7.refs_0_.refs_1_.refs_2_.refs_3_.refs_4_.refs_5_.refs_6_.refs_7_, ...), custom_call_target="tpu_custom_call" | custom-call | flops 1610612736 | bytes 6815744 | tf_op jit(solution)/shard_map/blocks_dot/pallas_call | solution.py:219
  128.5 1.1 copy-done.1
  129.7 1.1 copy-done.5
  130.8 1.2 all-to-all-done.2.refs_0_
  132.0 1.6 collective-permute-done.18.refs_2_
  133.6 0.6 collective-permute-done.19.refs_3_
  134.3 3.5 %blocks_dot.7 = bf16[512,768]{1,0:T(8,128)(2,1)} custom-call(s32[2]{0:T(128)S(1)} %fusion.5.at_ref, bf16[512,8192]{1,0:T(8,128)(2,1)} %collective-permute-done.7.refs_0_.refs_1_.refs_2_.refs_3_.refs_4_.refs_5_.refs_6_.refs_7_, bf16[512,8192]{1,0:T(8,128)(2,1)} %collective-permute-done.7.refs_0_.refs_1_.refs_2_.refs_3_.refs_4_.refs_5_.refs_6_.refs_7_, ...), custom_call_target="tpu_custom_call" | custom-call | flops 805306368 | bytes 4194304 | tf_op jit(solution)/shard_map/blocks_dot/pallas_call | solution.py:219
  137.8 5.0 %collective-permute-start.20 = (bf16[512,768]{1,0:T(8,128)(2,1)}, bf16[512,768]{1,0:T(8,128)(2,1)}, u32[]{:S(2)}, u32[]{:S(2)}) collective-permute-start(bf16[512,768]{1,0:T(8,128)(2,1)} %blocks_dot.7), channel_id=1, source_target_pairs={{0,1},{1,0},{2,3},{3,2},{4,5},{5,4},{6,7},{7,6},{8,9},{9,8},{10,11... | collective-permute-start | bytes 2359304 | tf_op jit(solution)/shard_map/ppermute | solution.py:29
  142.8 11.3 %early_dot.1 = (bf16[512,256]{1,0:T(8,128)(2,1)}, f32[512,256]{1,0:T(8,128)}, bf16[512,256]{1,0:T(8,128)(2,1)}, f32[512,256]{1,0:T(8,128)}) custom-call(s32[9]{0:T(128)} %pad_add_fusion.place_ref, bf16[512,8192]{1,0:T(8,128)(2,1)} %collective-permute-done.7.refs_0_.refs_1_.refs_2_.refs_3_.refs_4_.refs_5_.refs_6_.refs_7_, ...), custom_call_target="tpu_custom_call" | custom-call | flops 2147483648 | bytes 14680064 | tf_op jit(solution)/shard_map/early_dot/pallas_call | solution.py:149
  154.1 0.1 collective-permute-start.21
  154.2 2.4 %pad_maximum_fusion.1 = bf16[512,1024]{1,0:T(8,128)(2,1)} fusion(bf16[512,256]{1,0:T(8,128)(2,1)} %get-tuple-element.20, bf16[512,768]{1,0:T(8,128)(2,1)} %get-tuple-element.26), kind=kLoop, calls=%fused_computation.8 | loop fusion | flops 2097152 | bytes 2097152 | tf_op jit(solution)/shard_map/concatenate | solution.py:296
  156.7 1.6 pad_maximum_fusion
  158.3 0.1 multiply_convert_fusion.2
  158.4 0.6 copy-done.6
  159.0 2.8 %blocks_dot.6 = f32[512,768]{1,0:T(8,128)S(1)} custom-call(s32[2]{0:T(128)S(1)} %fusion.5.at_ref, bf16[512,8192]{1,0:T(8,128)(2,1)} %bitcast.44, bf16[512,8192]{1,0:T(8,128)(2,1)} %bitcast.45, bf16[512,768]{1,0:T(8,128)(2,1)S(1)} %collective-permute-done.18.refs_2_, bf16[512,768]{1,0:T(8,128)(2,1)S(1)} %collective-permute-done.19.refs_3_, ...), custom_call_target="tpu_custom_call" | custom-call | flops 805306368 | bytes 4194304 | tf_op jit(solution)/shard_map/blocks_dot/pallas_call | solution.py:219
  161.8 1.3 multiply_convert_fusion
  163.2 1.1 maximum_bitcast_fusion
  (57 shorter events, 0.2 us)
Async XLA Ops:
  0.6 30.9 %copy-start.7 = (f32[512,1024]{1,0:T(8,128)S(1)}, f32[512,1024]{1,0:T(8,128)}, u32[]{:S(2)}) copy-start(f32[512,1024]{1,0:T(8,128)} %refs_42_.1) | copy-start | bytes 6291460
  0.6 100.2 %collective-permute-start.7 = (bf16[512,8192]{1,0:T(8,128)(2,1)}, bf16[512,8192]{1,0:T(8,128)(2,1)}, u32[]{:S(2)}, u32[]{:S(2)}) collective-permute-start(bf16[512,8192]{1,0:T(8,128)(2,1)} %bitcast.29), channel_id=1, source_target_pairs={{0,1},{1,0},{2,3},{3,2},{4,5},{5,4},{6,7},{7,6},{8,9},{9,8},{10,11... | collective-permute-start | bytes 25165832 | tf_op jit(solution)/shard_map/ppermute | solution.py:29
  4.0 38.6 %all-to-all-start = ((bf16[16,32,1024]{2,1,0:T(8,128)(2,1)}), bf16[16,32,1024]{2,1,0:T(8,128)(2,1)}, u32[]{:S(2)}, u32[]{:S(2)}) async-start(bf16[16,32,1024]{2,1,0:T(8,128)(2,1)} %bitcast.46), calls=%async_computation | async-start | bytes 2097152 | tf_op jit(solution)/shard_map/all_to_all | solution.py:258
  13.3 14.0 %collective-permute-start = (bf16[512,256]{1,0:T(8,128)(2,1)}, bf16[512,256]{1,0:T(8,128)(2,1)S(1)}, u32[]{:S(2)}, u32[]{:S(2)}) collective-permute-start(bf16[512,256]{1,0:T(8,128)(2,1)} %slice.16.refs_16_), channel_id=1, source_target_pairs={{0,8},{1,9},{2,10},{3,11},{4,12},{5,13},{6,14},{7,15},{8,0},{9,1},... | collective-permute-start | bytes 786440 | tf_op jit(solution)/shard_map/ppermute | solution.py:29
  15.9 12.6 %collective-permute-start.1 = (bf16[512,256]{1,0:T(8,128)(2,1)}, bf16[512,256]{1,0:T(8,128)(2,1)S(1)}, u32[]{:S(2)}, u32[]{:S(2)}) collective-permute-start(bf16[512,256]{1,0:T(8,128)(2,1)} %slice.16.refs_16_), channel_id=1, source_target_pairs={{0,2},{1,3},{2,4},{3,5},{4,6},{5,7},{6,0},{7,1},{8,10},{9,11},{10,... | collective-permute-start | bytes 786440 | tf_op jit(solution)/shard_map/ppermute | solution.py:29
  17.1 12.9 %collective-permute-start.2 = (bf16[512,256]{1,0:T(8,128)(2,1)}, bf16[512,256]{1,0:T(8,128)(2,1)S(1)}, u32[]{:S(2)}, u32[]{:S(2)}) collective-permute-start(bf16[512,256]{1,0:T(8,128)(2,1)} %slice.16.refs_16_), channel_id=1, source_target_pairs={{0,6},{1,7},{2,0},{3,1},{4,2},{5,3},{6,4},{7,5},{8,14},{9,15},{10,... | collective-permute-start | bytes 786440 | tf_op jit(solution)/shard_map/ppermute | solution.py:29
  18.6 15.1 %collective-permute-start.3 = (bf16[512,256]{1,0:T(8,128)(2,1)}, bf16[512,256]{1,0:T(8,128)(2,1)S(1)}, u32[]{:S(2)}, u32[]{:S(2)}) collective-permute-start(bf16[512,256]{1,0:T(8,128)(2,1)} %slice.16.refs_16_), channel_id=1, source_target_pairs={{0,4},{1,5},{2,6},{3,7},{4,0},{5,1},{6,2},{7,3},{8,12},{9,13},{10,... | collective-permute-start | bytes 786440 | tf_op jit(solution)/shard_map/ppermute | solution.py:29
  27.4 15.2 %copy-start.10 = (bf16[512,256]{1,0:T(8,128)(2,1)}, bf16[512,256]{1,0:T(8,128)(2,1)S(1)}, u32[]{:S(2)}) copy-start(bf16[512,256]{1,0:T(8,128)(2,1)S(1)} %collective-permute-done.refs_1_.refs_17_) | copy-start | bytes 786436
  27.4 11.5 %collective-permute-start.4 = (bf16[512,256]{1,0:T(8,128)(2,1)S(1)}, bf16[512,256]{1,0:T(8,128)(2,1)S(1)}, u32[]{:S(2)}, u32[]{:S(2)}) collective-permute-start(bf16[512,256]{1,0:T(8,128)(2,1)S(1)} %collective-permute-done.refs_1_.refs_17_), channel_id=1, source_target_pairs={{0,2},{1,3},{2,4},{3,5},{4,6},{5,7},{6,0},{7,1},{8,10},{9,11},{10,... | collective-permute-start | bytes 786440 | tf_op jit(solution)/shard_map/ppermute | solution.py:29
  28.6 14.0 %copy-start.11 = (bf16[512,256]{1,0:T(8,128)(2,1)}, bf16[512,256]{1,0:T(8,128)(2,1)S(1)}, u32[]{:S(2)}) copy-start(bf16[512,256]{1,0:T(8,128)(2,1)S(1)} %collective-permute-done.1.refs_2_.refs_18_) | copy-start | bytes 786436
  28.6 10.3 %collective-permute-start.5 = (bf16[512,256]{1,0:T(8,128)(2,1)S(1)}, bf16[512,256]{1,0:T(8,128)(2,1)}, u32[]{:S(2)}, u32[]{:S(2)}) collective-permute-start(bf16[512,256]{1,0:T(8,128)(2,1)S(1)} %collective-permute-done.refs_1_.refs_17_), channel_id=1, source_target_pairs={{0,6},{1,7},{2,0},{3,1},{4,2},{5,3},{6,4},{7,5},{8,14},{9,15},{10,... | collective-permute-start | bytes 786440 | tf_op jit(solution)/shard_map/ppermute | solution.py:29
  30.0 12.5 %copy-start.12 = (bf16[512,256]{1,0:T(8,128)(2,1)}, bf16[512,256]{1,0:T(8,128)(2,1)S(1)}, u32[]{:S(2)}) copy-start(bf16[512,256]{1,0:T(8,128)(2,1)S(1)} %collective-permute-done.2.refs_3_.refs_20_) | copy-start | bytes 786436
  30.0 12.5 %collective-permute-start.6 = (bf16[512,256]{1,0:T(8,128)(2,1)S(1)}, bf16[512,256]{1,0:T(8,128)(2,1)}, u32[]{:S(2)}, u32[]{:S(2)}) collective-permute-start(bf16[512,256]{1,0:T(8,128)(2,1)S(1)} %collective-permute-done.refs_1_.refs_17_), channel_id=1, source_target_pairs={{0,4},{1,5},{2,6},{3,7},{4,0},{5,1},{6,2},{7,3},{8,12},{9,13},{10,... | collective-permute-start | bytes 786440 | tf_op jit(solution)/shard_map/ppermute | solution.py:29
  33.7 8.9 %copy-start.13 = (bf16[512,256]{1,0:T(8,128)(2,1)}, bf16[512,256]{1,0:T(8,128)(2,1)S(1)}, u32[]{:S(2)}) copy-start(bf16[512,256]{1,0:T(8,128)(2,1)S(1)} %collective-permute-done.3.refs_4_.refs_22_) | copy-start | bytes 786436
  38.8 3.7 %copy-start.14 = (bf16[512,256]{1,0:T(8,128)(2,1)}, bf16[512,256]{1,0:T(8,128)(2,1)S(1)}, u32[]{:S(2)}) copy-start(bf16[512,256]{1,0:T(8,128)(2,1)S(1)} %collective-permute-done.4.refs_5_.refs_19_) | copy-start | bytes 786436
  45.5 7.0 %copy-start.17 = (bf16[32,256]{1,0:T(8,128)(2,1)S(1)}, bf16[32,256]{1,0:T(8,128)(2,1)}, u32[]{:S(2)}) copy-start(bf16[32,256]{1,0:T(8,128)(2,1)} %get-tuple-element.15) | copy-start | bytes 49156
  45.5 18.5 %copy-start.18 = (bf16[32,256]{1,0:T(8,128)(2,1)S(1)}, bf16[32,256]{1,0:T(8,128)(2,1)}, u32[]{:S(2)}) copy-start(bf16[32,256]{1,0:T(8,128)(2,1)} %get-tuple-element.16) | copy-start | bytes 49156
  45.5 25.9 %all-to-all-start.1 = ((bf16[16,32,768]{2,1,0:T(8,128)(2,1)}), bf16[16,32,768]{2,1,0:T(8,128)(2,1)S(1)}, u32[]{:S(2)}, u32[]{:S(2)}) async-start(bf16[16,32,768]{2,1,0:T(8,128)(2,1)} %get-tuple-element.14), calls=%async_computation.1 | async-start | bytes 1572864 | tf_op jit(solution)/shard_map/all_to_all | solution.py:267
  52.5 4.2 %collective-permute-start.8 = (bf16[32,256]{1,0:T(8,128)(2,1)S(1)}, bf16[32,256]{1,0:T(8,128)(2,1)S(1)}, u32[]{:S(2)}, u32[]{:S(2)}) collective-permute-start(bf16[32,256]{1,0:T(8,128)(2,1)S(1)} %copy-done.17), channel_id=1, source_target_pairs={{0,8},{1,9},{2,10},{3,11},{4,12},{5,13},{6,14},{7,15},{8,0},{9,1},... | collective-permute-start | bytes 49160 | tf_op jit(solution)/shard_map/ppermute | solution.py:29
  56.7 4.3 %collective-permute-start.9 = (bf16[2,32,256]{2,1,0:T(8,128)(2,1)S(1)}, bf16[2,32,256]{2,1,0:T(8,128)(2,1)S(1)}, u32[]{:S(2)}, u32[]{:S(2)}) collective-permute-start(bf16[2,32,256]{2,1,0:T(8,128)(2,1)S(1)} %pad_maximum_fusion.3), channel_id=1, source_target_pairs={{0,2},{1,3},{2,4},{3,5},{4,6},{5,7},{6,0},{7,1},{8,10},{9,11},{10,... | collective-permute-start | bytes 98312 | tf_op jit(solution)/shard_map/ppermute | solution.py:29
  57.6 3.4 %collective-permute-start.10 = (bf16[2,32,256]{2,1,0:T(8,128)(2,1)S(1)}, bf16[2,32,256]{2,1,0:T(8,128)(2,1)S(1)}, u32[]{:S(2)}, u32[]{:S(2)}) collective-permute-start(bf16[2,32,256]{2,1,0:T(8,128)(2,1)S(1)} %pad_maximum_fusion.3), channel_id=1, source_target_pairs={{0,6},{1,7},{2,0},{3,1},{4,2},{5,3},{6,4},{7,5},{8,14},{9,15},{10,... | collective-permute-start | bytes 98312 | tf_op jit(solution)/shard_map/ppermute | solution.py:29
  59.4 4.6 %collective-permute-start.11 = (bf16[2,32,256]{2,1,0:T(8,128)(2,1)S(1)}, bf16[2,32,256]{2,1,0:T(8,128)(2,1)S(1)}, u32[]{:S(2)}, u32[]{:S(2)}) collective-permute-start(bf16[2,32,256]{2,1,0:T(8,128)(2,1)S(1)} %pad_maximum_fusion.3), channel_id=1, source_target_pairs={{0,4},{1,5},{2,6},{3,7},{4,0},{5,1},{6,2},{7,3},{8,12},{9,13},{10,... | collective-permute-start | bytes 98312 | tf_op jit(solution)/shard_map/ppermute | solution.py:29
  63.9 7.4 %collective-permute-start.12 = (bf16[9,32,256]{2,1,0:T(8,128)(2,1)S(1)}, bf16[9,32,256]{2,1,0:T(8,128)(2,1)S(1)}, u32[]{:S(2)}, u32[]{:S(2)}) collective-permute-start(bf16[9,32,256]{2,1,0:T(8,128)(2,1)S(1)} %bitcast_dynamic-update-slice_fusion), channel_id=1, source_target_pairs={{0,128},{16,144},{32,160},{48,176},{64,192},{80,208},{96,224},{112... | collective-permute-start | bytes 442376 | tf_op jit(solution)/shard_map/ppermute | solution.py:33
  71.4 1.8 %copy-start.9 = (bf16[16,32,768]{2,1,0:T(8,128)(2,1)}, bf16[16,32,768]{2,1,0:T(8,128)(2,1)S(1)}, u32[]{:S(2)}) copy-start(bf16[16,32,768]{2,1,0:T(8,128)(2,1)S(1)} %all-to-all-done.1) | copy-start | bytes 2359300
  73.2 58.8 %all-to-all-start.2 = ((bf16[8,2,9,32,256]{4,3,2,1,0:T(8,128)(2,1)}), bf16[8,2,9,32,256]{4,3,2,1,0:T(8,128)(2,1)}, u32[]{:S(2)}, u32[]{:S(2)}) async-start(bf16[8,2,9,32,256]{4,3,2,1,0:T(8,128)(2,1)} %broadcast_in_dim.17), calls=%async_computation.2 | async-start | bytes 4718592 | tf_op jit(solution)/shard_map/all_to_all | solution.py:278
  82.0 16.6 %collective-permute-start.13 = (bf16[512,768]{1,0:T(8,128)(2,1)S(1)}, bf16[512,768]{1,0:T(8,128)(2,1)S(1)}, u32[]{:S(2)}, u32[]{:S(2)}) collective-permute-start(bf16[512,768]{1,0:T(8,128)(2,1)S(1)} %get-tuple-element.25.refs_8_), channel_id=1, source_target_pairs={{0,8},{1,9},{2,10},{3,11},{4,12},{5,13},{6,14},{7,15},{8,0},{9,1},... | collective-permute-start | bytes 2359304 | tf_op jit(solution)/shard_map/ppermute | solution.py:29
  83.6 16.6 %collective-permute-start.16 = (bf16[512,768]{1,0:T(8,128)(2,1)S(1)}, bf16[512,768]{1,0:T(8,128)(2,1)}, u32[]{:S(2)}, u32[]{:S(2)}) collective-permute-start(bf16[512,768]{1,0:T(8,128)(2,1)S(1)} %get-tuple-element.25.refs_8_), channel_id=1, source_target_pairs={{0,2},{1,3},{2,4},{3,5},{4,6},{5,7},{6,0},{7,1},{8,10},{9,11},{10,... | collective-permute-start | bytes 2359304 | tf_op jit(solution)/shard_map/ppermute | solution.py:29
  83.6 17.3 %collective-permute-start.17 = (bf16[512,768]{1,0:T(8,128)(2,1)S(1)}, bf16[512,768]{1,0:T(8,128)(2,1)}, u32[]{:S(2)}, u32[]{:S(2)}) collective-permute-start(bf16[512,768]{1,0:T(8,128)(2,1)S(1)} %get-tuple-element.25.refs_8_), channel_id=1, source_target_pairs={{0,6},{1,7},{2,0},{3,1},{4,2},{5,3},{6,4},{7,5},{8,14},{9,15},{10,... | collective-permute-start | bytes 2359304 | tf_op jit(solution)/shard_map/ppermute | solution.py:29
  98.7 18.1 %collective-permute-start.15 = (bf16[512,768]{1,0:T(8,128)(2,1)S(1)}, bf16[512,768]{1,0:T(8,128)(2,1)S(1)}, u32[]{:S(2)}, u32[]{:S(2)}) collective-permute-start(bf16[512,768]{1,0:T(8,128)(2,1)S(1)} %collective-permute-done.13.refs_11_), channel_id=1, source_target_pairs={{0,6},{1,7},{2,0},{3,1},{4,2},{5,3},{6,4},{7,5},{8,14},{9,15},{10,... | collective-permute-start | bytes 2359304 | tf_op jit(solution)/shard_map/ppermute | solution.py:29
  99.4 22.6 %collective-permute-start.14 = (bf16[512,768]{1,0:T(8,128)(2,1)S(1)}, bf16[512,768]{1,0:T(8,128)(2,1)}, u32[]{:S(2)}, u32[]{:S(2)}) collective-permute-start(bf16[512,768]{1,0:T(8,128)(2,1)S(1)} %collective-permute-done.13.refs_11_), channel_id=1, source_target_pairs={{0,2},{1,3},{2,4},{3,5},{4,6},{5,7},{6,0},{7,1},{8,10},{9,11},{10,... | collective-permute-start | bytes 2359304 | tf_op jit(solution)/shard_map/ppermute | solution.py:29
  100.2 33.4 %collective-permute-start.18 = (bf16[512,768]{1,0:T(8,128)(2,1)}, bf16[512,768]{1,0:T(8,128)(2,1)S(1)}, u32[]{:S(2)}, u32[]{:S(2)}) collective-permute-start(bf16[512,768]{1,0:T(8,128)(2,1)} %collective-permute-done.16.refs_9_), channel_id=1, source_target_pairs={{0,2},{1,3},{2,4},{3,5},{4,6},{5,7},{6,0},{7,1},{8,10},{9,11},{10,... | collective-permute-start | bytes 2359304 | tf_op jit(solution)/shard_map/ppermute | solution.py:29
  109.0 1.1 copy-start
  116.8 0.9 copy-start.3
  117.6 16.6 %collective-permute-start.19 = (bf16[512,768]{1,0:T(8,128)(2,1)}, bf16[512,768]{1,0:T(8,128)(2,1)S(1)}, u32[]{:S(2)}, u32[]{:S(2)}) collective-permute-start(bf16[512,768]{1,0:T(8,128)(2,1)} %after.4.refs_5_), channel_id=1, source_target_pairs={{0,6},{1,7},{2,0},{3,1},{4,2},{5,3},{6,4},{7,5},{8,14},{9,15},{10,... | collective-permute-start | bytes 2359304 | tf_op jit(solution)/shard_map/ppermute | solution.py:29
  122.1 1.1 copy-start.4
  128.5 1.1 copy-start.1
  129.7 1.1 copy-start.5
  132.0 2.2 %copy-start.2 = (f32[512,768]{1,0:T(8,128)S(1)}, f32[512,768]{1,0:T(8,128)}, u32[]{:S(2)}) copy-start(f32[512,768]{1,0:T(8,128)} %copy-done.1) | copy-start | bytes 4718596
  137.8 24.0 %collective-permute-start.20 = (bf16[512,768]{1,0:T(8,128)(2,1)}, bf16[512,768]{1,0:T(8,128)(2,1)}, u32[]{:S(2)}, u32[]{:S(2)}) collective-permute-start(bf16[512,768]{1,0:T(8,128)(2,1)} %blocks_dot.7), channel_id=1, source_target_pairs={{0,1},{1,0},{2,3},{3,2},{4,5},{5,4},{6,7},{7,6},{8,9},{9,8},{10,11... | collective-permute-start | bytes 2359304 | tf_op jit(solution)/shard_map/ppermute | solution.py:29
  154.1 2.6 %copy-start.8 = (f32[512,768]{1,0:T(8,128)S(1)}, f32[512,768]{1,0:T(8,128)}, u32[]{:S(2)}) copy-start(f32[512,768]{1,0:T(8,128)} %get-tuple-element.27) | copy-start | bytes 4718596
  154.1 2.6 %copy-start.16 = (f32[512,256]{1,0:T(8,128)S(1)}, f32[512,256]{1,0:T(8,128)}, u32[]{:S(2)}) copy-start(f32[512,256]{1,0:T(8,128)} %get-tuple-element.21) | copy-start | bytes 1572868
  154.1 4.2 %collective-permute-start.21 = (bf16[512,256]{1,0:T(8,128)(2,1)}, bf16[512,256]{1,0:T(8,128)(2,1)S(1)}, u32[]{:S(2)}, u32[]{:S(2)}) collective-permute-start(bf16[512,256]{1,0:T(8,128)(2,1)} %get-tuple-element.24), channel_id=1, source_target_pairs={{0,1},{1,0},{2,3},{3,2},{4,5},{5,4},{6,7},{7,6},{8,9},{9,8},{10,11... | collective-permute-start | bytes 786440 | tf_op jit(solution)/shard_map/ppermute | solution.py:29
  156.7 1.6 %copy-start.15 = (f32[512,256]{1,0:T(8,128)S(1)}, f32[512,256]{1,0:T(8,128)}, u32[]{:S(2)}) copy-start(f32[512,256]{1,0:T(8,128)} %get-tuple-element.23) | copy-start | bytes 1572868
  156.7 2.3 %copy-start.6 = (f32[512,768]{1,0:T(8,128)S(1)}, f32[512,768]{1,0:T(8,128)}, u32[]{:S(2)}) copy-start(f32[512,768]{1,0:T(8,128)} %copy-done.5) | copy-start | bytes 4718596
